TPU v7x, 32 devices: a whole 2x2x4 slice. The times are simulated.
32 devices in a mesh: dp: 16 (over z, x, core), rep: 2 (over y).
Axes of the slice: x: 2, y: 2, z: 4, core: 2. Of those that a mesh axis runs over, the one named last changes fastest.
Arguments:
- block_input: float32 [65536, 384], P(('dp', 'rep')), may hold values from -6 to 6
- expert_out: float32 [65536, 207], P(('dp', 'rep')), may hold values from -6 to 6
- upstream: float32 [65536, 69], P(('dp', 'rep')), may hold values from -6 to 6
- lead_index: int32 [32], P(('dp', 'rep')), may hold values from 0 to 39
- lead_frames: int32 [40], replicated, may hold values from 1000 to 7999
- lead_embed: float32 [40, 384], replicated, may hold values from -3 to 3
- first_gain: float32 [384], replicated, may hold values from 0.5 to 1.5
- first_shift: float32 [384], replicated, may hold values from -0.625 to 0.625
- attend_weight: bfloat16 [384, 1152], replicated, may hold values from -0.3125 to 0.3125
- query_bias: float32 [384], replicated, may hold values from -0.625 to 0.625
- value_bias: float32 [384], replicated, may hold values from -0.125 to 0.125
- merge_weight: bfloat16 [384, 384], replicated, may hold values from -6 to 6
- merge_bias: float32 [384], replicated, may hold values from -0.625 to 0.625
- second_gain: float32 [384], replicated, may hold values from 0.5 to 1.5
- second_shift: float32 [384], replicated, may hold values from -0.625 to 0.625
- expand_weight: bfloat16 [384, 1536], replicated, may hold values from -0.3125 to 0.3125
- expand_bias: float32 [1536], replicated, may hold values from -0.625 to 0.625
- shrink_weight: bfloat16 [1536, 384], replicated, may hold values from -0.15625 to 0.15625
- shrink_bias: float32 [384], replicated, may hold values from -0.625 to 0.625
- router_weight: bfloat16 [384, 207], replicated, may hold values from -0.15625 to 0.15625
- router_bias: float32 [207], replicated, may hold values from -0.4375 to 0.4375
- correction: float32 [69], replicated, may hold values from -1.75 to 1.75
Outputs:
- blended: float32 [65536, 69], P(('dp', 'rep'))
- grad_input: float32 [65536, 384], P(('dp', 'rep'))
- grad_lead_embed: float32 [40, 384], replicated
- grad_first_gain: float32 [384], replicated
- grad_first_shift: float32 [384], replicated
- grad_attend_weight: float32 [384, 1152], replicated
- grad_query_bias: float32 [384], replicated
- grad_value_bias: float32 [384], replicated
- grad_merge_weight: float32 [384, 384], replicated
- grad_merge_bias: float32 [384], replicated
- grad_second_gain: float32 [384], replicated
- grad_second_shift: float32 [384], replicated
- grad_expand_weight: float32 [384, 1536], replicated
- grad_expand_bias: float32 [1536], replicated
- grad_shrink_weight: float32 [1536, 384], replicated
- grad_shrink_bias: float32 [384], replicated
- grad_router_weight: float32 [384, 207], replicated
- grad_router_bias: float32 [207], replicated
- grad_correction: float32 [69], replicated
All inputs are finite; a program needn't handle non-finite values.
Results may differ from a plain program's by a relative error of at most 0.0068.
Values sent between devices are 32-bit elements; how exact they have to be, the bound alone decides.
No kernel may reach another device: no remote copies, remote signals or barrier semaphores. Data moves between devices by JAX's collectives and lax.ppermute only.
A program may use at most 256 MiB of HBM per device.

v0:
```python
import jax
import jax.numpy as jnp
from jax import lax
from jax.sharding import PartitionSpec as P

HEADS = 6
QBLOCK = 512


EPSILON = 1e-05
PENALTY = 1.0
GELU_COEF = 0.7978845608028654


def norm_rows(values, scaling, offset):
    centre = jnp.mean(values, axis=-1, keepdims=True)
    centred = values - centre
    spread = jnp.mean(centred * centred, axis=-1, keepdims=True)
    return centred * lax.rsqrt(spread + EPSILON) * scaling + offset


def gelu_tanh(values):
    return (
        0.5 * values * (1.0 + jnp.tanh(GELU_COEF * (values + 0.044715 * values * values * values)))
    )


def expert_head(logits, correction, expert_frame):
    row_count = logits.shape[0]
    channels = correction.shape[0]
    grouped = logits.reshape(row_count, -1, channels)
    largest = jnp.max(grouped, axis=1, keepdims=True)
    shifted = grouped - largest
    log_gates = shifted - jnp.log(jnp.sum(jnp.exp(shifted), axis=1, keepdims=True))
    gate_probs = jnp.exp(log_gates)
    blended = (
        jnp.sum(gate_probs * expert_frame.reshape(row_count, -1, channels), axis=1) + correction
    )
    entropy = -jnp.sum(gate_probs * log_gates)
    return (blended, entropy)


def split_heads(projected):
    features = projected.shape[1] // 3
    row_count = projected.shape[0]
    head_size = features // HEADS
    queries = projected[:, :features].reshape(row_count, HEADS, head_size)
    key_rows = projected[:, features : 2 * features].reshape(row_count, HEADS, head_size)
    values = projected[:, 2 * features :].reshape(row_count, HEADS, head_size)
    return (queries, key_rows, values, head_size ** (-0.5))


def attend_forward(projected):
    queries, key_rows, values, scaling = split_heads(projected)
    row_count = projected.shape[0]
    offsets = jnp.arange(row_count // QBLOCK, dtype=jnp.int32) * QBLOCK

    def one_block(unused, offset):
        query_block = lax.dynamic_slice_in_dim(queries, offset, QBLOCK, 0)
        scores = (
            jnp.einsum("qhd,khd->hqk", query_block, key_rows, preferred_element_type=jnp.float32)
            * scaling
        )
        largest = jnp.max(scores, axis=-1, keepdims=True)
        raised = jnp.exp(scores - largest)
        row_total = jnp.sum(raised, axis=-1, keepdims=True)
        softmax_out = (raised / row_total).astype(jnp.bfloat16)
        mixed_rows = jnp.einsum(
            "hqk,khd->qhd", softmax_out, values, preferred_element_type=jnp.float32
        )
        return (unused, (mixed_rows.reshape(QBLOCK, -1), (largest + jnp.log(row_total))[..., 0]))

    unused, (mixed_rows, log_total) = lax.scan(one_block, jnp.zeros((), jnp.float32), offsets)
    return (mixed_rows.reshape(row_count, -1), log_total)


def attend_backward(projected, log_total, d_mixed):
    queries, key_rows, values, scaling = split_heads(projected)
    row_count = projected.shape[0]
    d_heads = d_mixed.reshape(queries.shape)
    offsets = jnp.arange(row_count // QBLOCK, dtype=jnp.int32) * QBLOCK

    def one_block(running, slices):
        d_keys, d_values = running
        offset, block_total = slices
        query_block = lax.dynamic_slice_in_dim(queries, offset, QBLOCK, 0)
        d_block = lax.dynamic_slice_in_dim(d_heads, offset, QBLOCK, 0)
        scores = (
            jnp.einsum("qhd,khd->hqk", query_block, key_rows, preferred_element_type=jnp.float32)
            * scaling
        )
        soft_probs = jnp.exp(scores - block_total[..., None])
        d_prob = jnp.einsum("qhd,khd->hqk", d_block, values, preferred_element_type=jnp.float32)
        centre = jnp.sum(d_prob * soft_probs, axis=-1, keepdims=True)
        d_scores = (soft_probs * (d_prob - centre)).astype(jnp.bfloat16)
        d_query = (
            jnp.einsum("hqk,khd->qhd", d_scores, key_rows, preferred_element_type=jnp.float32)
            * scaling
        )
        d_keys = (
            d_keys
            + jnp.einsum("hqk,qhd->khd", d_scores, query_block, preferred_element_type=jnp.float32)
            * scaling
        )
        d_values = d_values + jnp.einsum(
            "hqk,qhd->khd",
            soft_probs.astype(jnp.bfloat16),
            d_block,
            preferred_element_type=jnp.float32,
        )
        return ((d_keys, d_values), d_query.reshape(QBLOCK, -1))

    zeros_init = jnp.zeros(queries.shape, jnp.float32)
    (d_keys, d_values), d_query = lax.scan(
        one_block, (zeros_init, zeros_init), (offsets, log_total)
    )
    return jnp.concatenate(
        [
            d_query.reshape(row_count, -1),
            d_keys.reshape(row_count, -1),
            d_values.reshape(row_count, -1),
        ],
        axis=1,
    )


def body(
    block_input,
    expert_out,
    upstream,
    lead_index,
    lead_frames,
    lead_embed,
    first_gain,
    first_shift,
    attend_weight,
    query_bias,
    value_bias,
    merge_weight,
    merge_bias,
    second_gain,
    second_shift,
    expand_weight,
    expand_bias,
    shrink_weight,
    shrink_bias,
    router_weight,
    router_bias,
    correction,
):
    frame_count = lead_index.shape[0]
    features = block_input.shape[1]
    channels = correction.shape[0]
    lead_total = lead_embed.shape[0]
    frame_len = block_input.shape[0] // frame_count
    lead_hot = (lead_index[:, None] == jnp.arange(lead_total, dtype=jnp.int32)[None, :]).astype(
        jnp.float32
    )
    local_counts = jnp.sum(lead_hot, axis=0).astype(jnp.int32)
    counts = lax.psum(local_counts, ("dp", "rep")).astype(jnp.float32)
    all_frames = frame_count * lax.axis_size("dp") * lax.axis_size("rep")
    table = lead_frames.astype(jnp.float32)
    chosen = jnp.sum(lead_hot * table[None, :], axis=1)
    present = jnp.sum(lead_hot * counts[None, :], axis=1)
    frame_weight = chosen * all_frames / (present * jnp.sum(table))
    bias_rows = jnp.concatenate([query_bias, jnp.zeros_like(query_bias), value_bias])
    params = (
        lead_embed,
        first_gain,
        first_shift,
        attend_weight,
        query_bias,
        value_bias,
        merge_weight,
        merge_bias,
        second_gain,
        second_shift,
        expand_weight,
        expand_bias,
        shrink_weight,
        shrink_bias,
        router_weight,
        router_bias,
        correction,
    )

    def frame_step(running, slices):
        frame_in, expert_frame, upstream_frame, lead_row_hot, weight = slices
        lead_row = jnp.dot(lead_row_hot, lead_embed, precision=lax.Precision.HIGHEST)
        stream = frame_in + lead_row[None, :]
        first_norm, first_pull = jax.vjp(norm_rows, stream, first_gain, first_shift)
        first_low = first_norm.astype(jnp.bfloat16)
        projected = (
            jnp.dot(first_low, attend_weight, preferred_element_type=jnp.float32) + bias_rows
        ).astype(jnp.bfloat16)
        mixed_heads, log_total = attend_forward(projected)
        mixed_low = mixed_heads.astype(jnp.bfloat16)
        stream_mid = (
            stream
            + jnp.dot(mixed_low, merge_weight, preferred_element_type=jnp.float32)
            + merge_bias
        )
        second_norm, second_pull = jax.vjp(norm_rows, stream_mid, second_gain, second_shift)
        second_low = second_norm.astype(jnp.bfloat16)
        pre_act = (
            jnp.dot(second_low, expand_weight, preferred_element_type=jnp.float32) + expand_bias
        )
        activated, gelu_pull = jax.vjp(gelu_tanh, pre_act)
        hidden = activated.astype(jnp.bfloat16)
        output = (
            stream_mid
            + jnp.dot(hidden, shrink_weight, preferred_element_type=jnp.float32)
            + shrink_bias
        )
        output_low = output.astype(jnp.bfloat16)
        logits = (
            jnp.dot(output_low, router_weight, preferred_element_type=jnp.float32) + router_bias
        )

        def head_terms(logit_rows, offset_rows):
            return expert_head(logit_rows, offset_rows, expert_frame)

        (blended, entropy), head_pull = jax.vjp(head_terms, logits, correction)
        d_logits, grad_correction = head_pull((weight * upstream_frame, weight * PENALTY))
        d_logits_low = d_logits.astype(jnp.bfloat16)
        grad_router = jnp.einsum(
            "nd,ne->de", output_low, d_logits_low, preferred_element_type=jnp.float32
        )
        grad_router_bias = jnp.sum(d_logits, axis=0)
        d_output = jnp.einsum(
            "ne,de->nd", d_logits_low, router_weight, preferred_element_type=jnp.float32
        )
        grad_shrink_bias = jnp.sum(d_output, axis=0)
        d_output_low = d_output.astype(jnp.bfloat16)
        grad_shrink = jnp.einsum(
            "nf,nd->fd", hidden, d_output_low, preferred_element_type=jnp.float32
        )
        d_hidden = jnp.einsum(
            "nd,fd->nf", d_output_low, shrink_weight, preferred_element_type=jnp.float32
        )
        (d_pre,) = gelu_pull(d_hidden)
        grad_expand_bias = jnp.sum(d_pre, axis=0)
        d_pre_low = d_pre.astype(jnp.bfloat16)
        grad_expand = jnp.einsum(
            "nd,nf->df", second_low, d_pre_low, preferred_element_type=jnp.float32
        )
        d_second = jnp.einsum(
            "nf,df->nd", d_pre_low, expand_weight, preferred_element_type=jnp.float32
        )
        d_mid_part, grad_second_gain, grad_second_shift = second_pull(d_second)
        d_mid = d_output + d_mid_part
        grad_merge_bias = jnp.sum(d_mid, axis=0)
        d_mid_low = d_mid.astype(jnp.bfloat16)
        grad_merge = jnp.einsum(
            "nd,ne->de", mixed_low, d_mid_low, preferred_element_type=jnp.float32
        )
        d_mixed = jnp.einsum(
            "ne,de->nd", d_mid_low, merge_weight, preferred_element_type=jnp.float32
        ).astype(jnp.bfloat16)
        d_projected = attend_backward(projected, log_total, d_mixed).astype(jnp.bfloat16)
        grad_query_bias = jnp.sum(d_projected[:, :features], axis=0, dtype=jnp.float32)
        grad_value_bias = jnp.sum(d_projected[:, 2 * features :], axis=0, dtype=jnp.float32)
        grad_attend = jnp.einsum(
            "nd,ne->de", first_low, d_projected, preferred_element_type=jnp.float32
        )
        d_first = jnp.einsum(
            "ne,de->nd", d_projected, attend_weight, preferred_element_type=jnp.float32
        )
        d_stream_part, grad_first_gain, grad_first_shift = first_pull(d_first)
        d_stream = d_mid + d_stream_part
        grad_embed = lead_row_hot[:, None] * jnp.sum(d_stream, axis=0)[None, :]
        new_grads = (
            grad_embed,
            grad_first_gain,
            grad_first_shift,
            grad_attend,
            grad_query_bias,
            grad_value_bias,
            grad_merge,
            grad_merge_bias,
            grad_second_gain,
            grad_second_shift,
            grad_expand,
            grad_expand_bias,
            grad_shrink,
            grad_shrink_bias,
            grad_router,
            grad_router_bias,
            grad_correction,
        )
        return (jax.tree.map(jnp.add, running, new_grads), (blended, d_stream))

    initial = tuple((jnp.zeros(member.shape, jnp.float32) for member in params))
    local_grads, (blended, d_input) = lax.scan(
        frame_step,
        initial,
        (
            block_input.reshape(frame_count, frame_len, features),
            expert_out.reshape(frame_count, frame_len, -1),
            upstream.reshape(frame_count, frame_len, channels),
            lead_hot,
            frame_weight,
        ),
    )
    flat_grads = jnp.concatenate([member.reshape(-1) for member in local_grads])
    devices = lax.axis_size("dp") * lax.axis_size("rep")
    padded = jnp.pad(flat_grads, (0, -flat_grads.shape[0] % devices))
    grad_shard = lax.psum_scatter(padded, ("dp", "rep"), scatter_dimension=0, tiled=True)
    summed = lax.all_gather(grad_shard, ("dp", "rep"), axis=0, tiled=True)
    pieces = []
    position = 0
    for member in params:
        length = member.size
        pieces.append(summed[position : position + length].reshape(member.shape))
        position += length
    return (blended.reshape(-1, channels), d_input.reshape(-1, features)) + tuple(pieces)


def solution(mesh):
    return jax.shard_map(
        body,
        mesh=mesh,
        in_specs=(
            P(("dp", "rep"), None),
            P(("dp", "rep"), None),
            P(("dp", "rep"), None),
            P(("dp", "rep")),
            P(),
            P(),
            P(),
            P(),
            P(),
            P(),
            P(),
            P(),
            P(),
            P(),
            P(),
            P(),
            P(),
            P(),
            P(),
            P(),
            P(),
            P(),
        ),
        out_specs=(
            P(("dp", "rep"), None),
            P(("dp", "rep"), None),
            P(),
            P(),
            P(),
            P(),
            P(),
            P(),
            P(),
            P(),
            P(),
            P(),
            P(),
            P(),
            P(),
            P(),
            P(),
            P(),
            P(),
        ),
        check_vma=False,
    )
```

profile of v0, /device:TPU:0, one launch (start us, length us, event | category | flops | bytes accessed | tf_op | source)
XLA Modules:
  0.0 1195.3 jit_solution(4784536689284613081)
XLA Ops:
  8.4 42.0 %psum.7 = s32[40]{0:T(128)S(1)} all-reduce(s32[40]{0:T(128)S(1)} %fusion.55), channel_id=1, replica_groups=mesh['dp'=16,'rep'=2] {'dp','rep'}, use_global_device_ids=true, to_apply=%region_12.13 | all-reduce | flops 40 | bytes 320 | tf_op jit(solution)/shard_map/psum | solution.py:160
  60.8 3.5 copy.77
  74.6 154.4 %while.36 = (s32[]{:T(128)}, bf16[4,512,384]{2,1,0:T(8,128)(2,1)}, f32[4,6,512]{2,1,0:T(8,128)}, s32[4]{0:T(128)}, bf16[2048,6,64]{0,2,1:T(8,128)(2,1)}, /*index...) while((s32[]{:T(128)}, bf16[4,512,384]{2,1,0:T(8,128)(2,1)}, ...), condition=%wide.region_5.6_spmd, body=%wide.region_2.5_spmd.sunk | while | flops 1667232768 | bytes 87449816 | solution.py:73
  77.8 11.2 multiply_reduce_fusion.11
  89.0 10.9 fusion.116
  99.9 10.9 fusion.117
  116.4 11.2 multiply_reduce_fusion.11
  127.5 10.9 fusion.116
  138.4 10.9 fusion.117
  154.9 11.2 multiply_reduce_fusion.11
  166.1 10.9 fusion.116
  177.0 10.9 fusion.117
  193.5 11.2 multiply_reduce_fusion.11
  204.6 10.9 fusion.116
  215.5 10.9 fusion.117
  229.1 3.6 fusion.67
  233.5 9.6 multiply_convert_fusion.1
  276.2 6.2 fusion.60
  285.1 18.5 %fusion.41 = f32[1536,384]{1,0:T(8,128)} fusion(bf16[2048,1536]{1,0:T(8,128)(2,1)} %copy-done.72, f32[2048,384]{1,0:T(8,128)S(1)} %get-tuple-element.429), kind=kOutput, calls=%fused_computation.85 | convolution fusion | flops 2416705536 | bytes 11796480 | tf_op jit(solution)/shard_map/while/body/eval_jaxpr/nf,nd->fd/dot_general | solution.py:235
  303.6 15.9 %fusion.70 = (f32[1536]{0:T(1024)}, bf16[2048,1536]{1,0:T(8,128)(2,1)S(1)}) fusion(bf16[1536,384]{1,0:T(8,128)(2,1)S(1)} %copy-done.64, f32[2048,384]{1,0:T(8,128)S(1)} %get-tuple-element.429, f32[2048,1536]{1,0:T(8,128)} %get-tuple-element.421, f32[1536]{0:T(1024)S(1)} %copy-done.67), kind=kOutput, calls=%fused_computation.133 | convolution fusion | flops 2498492928 | bytes 23212032 | tf_op jit(solution)/shard_map/while/body/eval_jaxpr/nd,fd->nf/dot_general | solution.py:238
  319.5 4.1 fusion.30
  323.6 5.8 fusion.69
  329.4 3.5 copy.81
  333.0 3.6 copy.80
  336.5 3.5 multiply_reduce_fusion.5
  350.4 351.3 %while.37 = (s32[]{:T(128)}, f32[2048,6,64]{0,2,1:T(8,128)}, f32[2048,6,64]{0,2,1:T(8,128)}, bf16[4,512,384]{2,1,0:T(8,128)(2,1)}, s32[4]{0:T(128)}, /*index=5*/...) while((s32[]{:T(128)}, f32[2048,6,64]{0,2,1:T(8,128)}, ...), condition=%wide.region_22.23_spmd.clone, body=%wide.region_20.22_spmd.clone.sunk | while | flops 4106351616 | bytes 209670352 | solution.py:114
  354.7 11.2 fusion.127
  365.8 14.6 %bitcast_add_fusion.5 = f32[2048,6,64]{0,2,1:T(8,128)} fusion(f32[2048,6,64]{0,2,1:T(8,128)} %get-tuple-element.591, f32[6,512,2048]{2,1,0:T(8,128)} %fusion.127, f32[6,512]{1,0:T(8,128)S(1)} %dynamic-slice_bitcast_fusion.2, pred[]{:T(512)S(6)} %compare.4, bf16[2048,6,64]{0,2,1:T(8,128)(2,1)} %get-tuple-element.610, s32[]{:T(128)S(6)} %select_n.11), kind=kOutput, calls=%fused_computation.18.clone.1 | convolution fusion | flops 825753600 | bytes 31862788 | tf_op jit(solution)/shard_map/while/body/eval_jaxpr/while/body/eval_jaxpr/hqk,qhd->khd/dot_general | solution.py:105
  380.4 16.9 %multiply_reduce_fusion.12 = (f32[6,512]{1,0:T(8,128)S(1)}, f32[6,512,2048]{2,1,0:T(8,128)}) fusion(f32[6,512,2048]{2,1,0:T(8,128)} %fusion.127, f32[6,512]{1,0:T(8,128)S(1)} %dynamic-slice_bitcast_fusion.2, bf16[2048,6,64]{0,2,1:T(8,128)(2,1)} %get-tuple-element.611, bf16[2048,6,64]{0,2,1:T(8,128)(2,1)} %get-tuple-element.610, s32[]{:T(128)S(6)} %select_n.11), kind=kOutput, calls=%fused_computation.12.clone.1 | convolution fusion | flops 830469120 | bytes 52322308 | tf_op jit(solution)/shard_map/while/body/eval_jaxpr/while/body/eval_jaxpr/qhd,khd->hqk/dot_general | solution.py:93
  397.4 21.5 %multiply_convert_fusion.3 = bf16[6,512,2048]{2,1,0:T(8,128)(2,1)} fusion(f32[6,512,2048]{2,1,0:T(8,128)} %get-tuple-element.544, f32[6,512,2048]{2,1,0:T(8,128)} %fusion.127, f32[6,512]{1,0:T(8,128)S(1)} %get-tuple-element.545, f32[6,512]{1,0:T(8,128)S(1)} %dynamic-slice_bitcast_fusion.2), kind=kLoop, calls=%fused_computation.11.clone.1 | loop fusion | flops 31457280 | bytes 62939136 | tf_op jit(solution)/shard_map/while/body/eval_jaxpr/while/body/eval_jaxpr/convert_element_type | solution.py:95
  418.9 8.5 convolution_multiply_fusion.2
  427.4 8.8 bitcast_add_fusion.4
  441.1 11.2 fusion.127
  452.2 15.5 %bitcast_add_fusion.5 = f32[2048,6,64]{0,2,1:T(8,128)} fusion(f32[2048,6,64]{0,2,1:T(8,128)} %get-tuple-element.591, f32[6,512,2048]{2,1,0:T(8,128)} %fusion.127, f32[6,512]{1,0:T(8,128)S(1)} %dynamic-slice_bitcast_fusion.2, pred[]{:T(512)S(6)} %compare.4, bf16[2048,6,64]{0,2,1:T(8,128)(2,1)} %get-tuple-element.610, s32[]{:T(128)S(6)} %select_n.11), kind=kOutput, calls=%fused_computation.18.clone.1 | convolution fusion | flops 825753600 | bytes 31862788 | tf_op jit(solution)/shard_map/while/body/eval_jaxpr/while/body/eval_jaxpr/hqk,qhd->khd/dot_general | solution.py:105
  467.7 16.9 %multiply_reduce_fusion.12 = (f32[6,512]{1,0:T(8,128)S(1)}, f32[6,512,2048]{2,1,0:T(8,128)}) fusion(f32[6,512,2048]{2,1,0:T(8,128)} %fusion.127, f32[6,512]{1,0:T(8,128)S(1)} %dynamic-slice_bitcast_fusion.2, bf16[2048,6,64]{0,2,1:T(8,128)(2,1)} %get-tuple-element.611, bf16[2048,6,64]{0,2,1:T(8,128)(2,1)} %get-tuple-element.610, s32[]{:T(128)S(6)} %select_n.11), kind=kOutput, calls=%fused_computation.12.clone.1 | convolution fusion | flops 830469120 | bytes 52322308 | tf_op jit(solution)/shard_map/while/body/eval_jaxpr/while/body/eval_jaxpr/qhd,khd->hqk/dot_general | solution.py:93
  484.6 21.5 %multiply_convert_fusion.3 = bf16[6,512,2048]{2,1,0:T(8,128)(2,1)} fusion(f32[6,512,2048]{2,1,0:T(8,128)} %get-tuple-element.544, f32[6,512,2048]{2,1,0:T(8,128)} %fusion.127, f32[6,512]{1,0:T(8,128)S(1)} %get-tuple-element.545, f32[6,512]{1,0:T(8,128)S(1)} %dynamic-slice_bitcast_fusion.2), kind=kLoop, calls=%fused_computation.11.clone.1 | loop fusion | flops 31457280 | bytes 62939136 | tf_op jit(solution)/shard_map/while/body/eval_jaxpr/while/body/eval_jaxpr/convert_element_type | solution.py:95
  506.1 8.5 convolution_multiply_fusion.2
  514.6 9.7 bitcast_add_fusion.4
  529.2 11.2 fusion.127
  540.4 15.5 %bitcast_add_fusion.5 = f32[2048,6,64]{0,2,1:T(8,128)} fusion(f32[2048,6,64]{0,2,1:T(8,128)} %get-tuple-element.591, f32[6,512,2048]{2,1,0:T(8,128)} %fusion.127, f32[6,512]{1,0:T(8,128)S(1)} %dynamic-slice_bitcast_fusion.2, pred[]{:T(512)S(6)} %compare.4, bf16[2048,6,64]{0,2,1:T(8,128)(2,1)} %get-tuple-element.610, s32[]{:T(128)S(6)} %select_n.11), kind=kOutput, calls=%fused_computation.18.clone.1 | convolution fusion | flops 825753600 | bytes 31862788 | tf_op jit(solution)/shard_map/while/body/eval_jaxpr/while/body/eval_jaxpr/hqk,qhd->khd/dot_general | solution.py:105
  555.9 16.9 %multiply_reduce_fusion.12 = (f32[6,512]{1,0:T(8,128)S(1)}, f32[6,512,2048]{2,1,0:T(8,128)}) fusion(f32[6,512,2048]{2,1,0:T(8,128)} %fusion.127, f32[6,512]{1,0:T(8,128)S(1)} %dynamic-slice_bitcast_fusion.2, bf16[2048,6,64]{0,2,1:T(8,128)(2,1)} %get-tuple-element.611, bf16[2048,6,64]{0,2,1:T(8,128)(2,1)} %get-tuple-element.610, s32[]{:T(128)S(6)} %select_n.11), kind=kOutput, calls=%fused_computation.12.clone.1 | convolution fusion | flops 830469120 | bytes 52322308 | tf_op jit(solution)/shard_map/while/body/eval_jaxpr/while/body/eval_jaxpr/qhd,khd->hqk/dot_general | solution.py:93
  572.8 21.5 %multiply_convert_fusion.3 = bf16[6,512,2048]{2,1,0:T(8,128)(2,1)} fusion(f32[6,512,2048]{2,1,0:T(8,128)} %get-tuple-element.544, f32[6,512,2048]{2,1,0:T(8,128)} %fusion.127, f32[6,512]{1,0:T(8,128)S(1)} %get-tuple-element.545, f32[6,512]{1,0:T(8,128)S(1)} %dynamic-slice_bitcast_fusion.2), kind=kLoop, calls=%fused_computation.11.clone.1 | loop fusion | flops 31457280 | bytes 62939136 | tf_op jit(solution)/shard_map/while/body/eval_jaxpr/while/body/eval_jaxpr/convert_element_type | solution.py:95
  594.3 8.5 convolution_multiply_fusion.2
  602.8 9.7 bitcast_add_fusion.4
  617.4 11.1 fusion.127
  628.5 15.5 %bitcast_add_fusion.5 = f32[2048,6,64]{0,2,1:T(8,128)} fusion(f32[2048,6,64]{0,2,1:T(8,128)} %get-tuple-element.591, f32[6,512,2048]{2,1,0:T(8,128)} %fusion.127, f32[6,512]{1,0:T(8,128)S(1)} %dynamic-slice_bitcast_fusion.2, pred[]{:T(512)S(6)} %compare.4, bf16[2048,6,64]{0,2,1:T(8,128)(2,1)} %get-tuple-element.610, s32[]{:T(128)S(6)} %select_n.11), kind=kOutput, calls=%fused_computation.18.clone.1 | convolution fusion | flops 825753600 | bytes 31862788 | tf_op jit(solution)/shard_map/while/body/eval_jaxpr/while/body/eval_jaxpr/hqk,qhd->khd/dot_general | solution.py:105
  644.0 16.9 %multiply_reduce_fusion.12 = (f32[6,512]{1,0:T(8,128)S(1)}, f32[6,512,2048]{2,1,0:T(8,128)}) fusion(f32[6,512,2048]{2,1,0:T(8,128)} %fusion.127, f32[6,512]{1,0:T(8,128)S(1)} %dynamic-slice_bitcast_fusion.2, bf16[2048,6,64]{0,2,1:T(8,128)(2,1)} %get-tuple-element.611, bf16[2048,6,64]{0,2,1:T(8,128)(2,1)} %get-tuple-element.610, s32[]{:T(128)S(6)} %select_n.11), kind=kOutput, calls=%fused_computation.12.clone.1 | convolution fusion | flops 830469120 | bytes 52322308 | tf_op jit(solution)/shard_map/while/body/eval_jaxpr/while/body/eval_jaxpr/qhd,khd->hqk/dot_general | solution.py:93
  660.9 21.5 %multiply_convert_fusion.3 = bf16[6,512,2048]{2,1,0:T(8,128)(2,1)} fusion(f32[6,512,2048]{2,1,0:T(8,128)} %get-tuple-element.544, f32[6,512,2048]{2,1,0:T(8,128)} %fusion.127, f32[6,512]{1,0:T(8,128)S(1)} %get-tuple-element.545, f32[6,512]{1,0:T(8,128)S(1)} %dynamic-slice_bitcast_fusion.2), kind=kLoop, calls=%fused_computation.11.clone.1 | loop fusion | flops 31457280 | bytes 62939136 | tf_op jit(solution)/shard_map/while/body/eval_jaxpr/while/body/eval_jaxpr/convert_element_type | solution.py:95
  682.4 8.5 convolution_multiply_fusion.2
  690.9 9.6 bitcast_add_fusion.4
  701.7 3.4 convert.13
  708.8 3.8 convert_reduce_fusion
  715.3 6.6 fusion.34
  721.9 4.7 fusion.68
  736.4 3.6 copy.85
  740.0 3.6 multiply_reduce_fusion.4
  749.9 61.1 %concatenate.13 = f32[1869204]{0:T(1024)} concatenate(f32[15360]{0:T(1024)S(1)} %mul.388, f32[384]{0:T(512)S(1)} %get-tuple-element.348, f32[384]{0:T(512)S(1)} %copy-done.56, f32[442368]{0:T(1024)} %reshape.311, f32[384]{0:T(512)S(1)} %copy-done.52, f32[384]{0:T(512)S(1)} %copy-done.53, f32[147456]{0:T(1024)S(1)} %reshape.312, f32[384]{0:T(512)S(1)} %copy-done.51, ...), dimensions={0} | concatenate | bytes 14953632 | tf_op jit(solution)/shard_map/concatenate | solution.py:305
  811.0 5.6 pad.4
  816.7 169.6 %all-reduce.8.cloned.1.call-done = f32[1869216]{0:T(1024)} async-done(((f32[1869216]{0:T(1024)}), f32[1869216]{0:T(1024)}) %all-reduce.8.cloned.1.call-update) | async-done | bytes 7476880
  986.3 3.5 broadcast.191
  991.8 3.6 copy.89
  996.3 166.1 %all-reduce.6.cloned.1.call-done = f32[1869216]{0:T(1024)} async-done(((f32[1869216]{0:T(1024)}), f32[1869216]{0:T(1024)}) %all-reduce.6.cloned.1.call-update) | async-done | bytes 7476880
  1168.4 4.1 fusion.65
  1172.5 3.4 reshape.320
  (276 shorter events, 135.5 us)
Async XLA Ops:
  7.2 225.9 %copy-start = (bf16[384,1536]{1,0:T(8,128)(2,1)S(1)}, bf16[384,1536]{1,0:T(8,128)(2,1)}, u32[]{:S(2)}) copy-start(bf16[384,1536]{1,0:T(8,128)(2,1)} %param.41) | copy-start | bytes 3538948
  7.2 979.1 %all-reduce.8.cloned.1.call-start = ((), (), s32[]{:S(2)}) async-start(), calls=%async_computation.1 | async-start | bytes 14958592
  56.1 4.7 copy-start.17
  60.8 3.6 copy-start.44
  64.5 3.8 copy-start.37
  64.5 3.8 copy-start.58
  64.6 3.7 copy-start.59
  64.6 3.8 copy-start.45
  64.6 3.8 copy-start.65
  64.6 3.8 copy-start.70
  67.2 4.1 copy-start.35
  67.7 3.6 copy-start.39
  89.0 10.9 copy-start.7
  99.9 10.9 copy-start.26
  127.5 10.9 copy-start.7
  138.4 10.9 copy-start.26
  166.1 10.9 copy-start.7
  177.0 10.9 copy-start.26
  204.6 10.9 copy-start.7
  215.5 10.9 copy-start.26
  232.7 10.4 copy-start.4
  233.5 9.6 copy-start.63
  233.5 9.6 copy-start.68
  243.1 3.9 copy-start.33
  243.1 3.9 copy-start.60
  268.9 3.0 copy-start.23
  276.2 6.2 copy-start.28
  285.1 18.5 %copy-start.15 = (f32[2048,384]{1,0:T(8,128)}, f32[2048,384]{1,0:T(8,128)S(1)}, u32[]{:S(2)}) copy-start(f32[2048,384]{1,0:T(8,128)S(1)} %get-tuple-element.429) | copy-start | bytes 9437188
  285.1 18.5 %copy-start.64 = (bf16[1536,384]{1,0:T(8,128)(2,1)S(1)}, bf16[1536,384]{1,0:T(8,128)(2,1)}, u32[]{:S(2)}) copy-start(bf16[1536,384]{1,0:T(8,128)(2,1)} %param.43) | copy-start | bytes 3538948
  303.6 15.9 %copy-start.5 = (f32[2048,384]{0,1:T(8,128)S(1)}, f32[2048,384]{0,1:T(8,128)}, u32[]{:S(2)}) copy-start(f32[2048,384]{0,1:T(8,128)} %copy-done.4) | copy-start | bytes 9437188
  336.5 3.7 copy-start.6
  336.5 4.7 copy-start.11
  345.0 4.1 copy-start.8
  701.7 6.0 copy-start.21
  708.7 6.4 copy-start.36
  708.8 6.4 copy-start.38
  708.8 6.4 copy-start.40
  708.8 6.4 copy-start.46
  708.8 6.5 copy-start.71
  715.2 6.7 copy-start.29
  715.2 6.6 copy-start.30
  715.2 6.6 copy-start.66
  721.9 5.2 copy-start.34
  730.6 3.2 copy-start.24
  740.0 3.6 copy-start.43
  740.0 3.8 copy-start.3
  740.0 4.7 copy-start.10
  740.0 4.7 copy-start.41
  746.6 3.1 copy-start.62
  746.6 3.2 copy-start.31
  746.6 3.2 copy-start.48
  746.6 3.2 copy-start.49
  746.6 3.2 copy-start.50
  746.7 3.2 copy-start.51
  746.7 3.2 copy-start.52
  746.7 3.2 copy-start.53
  746.7 3.2 copy-start.54
  746.7 3.2 copy-start.55
  746.7 3.2 copy-start.56
  746.7 3.2 copy-start.57
  816.6 345.9 %all-reduce.6.cloned.1.call-start = ((), (), s32[]{:S(2)}) async-start(), calls=%async_computation | async-start | bytes 14958592
  991.8 3.6 copy-start.25
  991.8 3.6 copy-start.61
  1178.7 9.5 copy-start.1
  (17 other events, 30.2 us)
Sparse Core Ops, SparseCore 0:
  816.7 169.4 all-reduce.7
  993.1 169.3 all-reduce.5
where the time goes:
time: 1210 us; the launch traced here: 1200 us
  matrix products  417 us (34%)
  waiting for transfers between devices  336 us (28%)
  local copies, waits for them, and re-layouts  186 us (15%)
  other arithmetic  180 us (15%)
  blocking collectives  42 us (3%)
  between operations  17.7 us (1%)
  loops' own time  16.6 us (1%)
    unnamed x4, waiting for transfers between devices  336 us
    dot_general x8, matrix products, one_block(): jnp.einsum('qhd,khd->hqk', query_block, key_rows, preferred_element_type=...  89.3 us
    convert_element_type x4, other arithmetic, one_block(): d_scores = (soft_probs * (d_prob - centre)).astype(jnp.bfloat16)  86 us
    dot_general x4, matrix products, one_block(): jnp.einsum('qhd,khd->hqk', d_block, values, preferred_element_type=jnp.fl...  67.6 us
    dot_general x4, matrix products, one_block(): jnp.einsum('hqk,qhd->khd', soft_probs.astype(jnp.bfloat16), d_block, pref...  61.1 us
    concatenate x1, local copies, waits for them, and re-layouts, body(): flat_grads = jnp.concatenate([member.reshape(-1) for member in local_grads])  61.1 us
    dot_general x4, matrix products, one_block(): jnp.einsum('hqk,khd->qhd', softmax_out, values, preferred_element_type=jn...  43.7 us
    reduce_sum x4, other arithmetic, one_block(): row_total = jnp.sum(raised, axis=-1, keepdims=True)  43.5 us
  transfers between devices with their start and end apart: 2, of which 2 were waited for; matrix products, arithmetic and copies ran while one was open for 0% of the time, Pallas kernels for 0%

commit v1 on v0

v1 whole, which is shorter than its diff:
```python
import functools

import jax
import jax.numpy as jnp
from jax import lax
from jax.experimental import pallas as pl
from jax.experimental.pallas import tpu as pltpu
from jax.sharding import PartitionSpec as P

HEADS = 6
EPSILON = 1e-05
PENALTY = 1.0
GELU_COEF = 0.7978845608028654
GELU_CUBE = 0.044715
LOG2E = 1.4426950408889634
LANES = 128
STEP = 512
LIMIT = 56 * 2**20

low = jnp.bfloat16
full = jnp.float32


def mul(left, right, dims=((1,), (0,))):
    return lax.dot_general(left, right, (dims, ((), ())), preferred_element_type=full)


NT = ((1,), (1,))
TN = ((0,), (0,))


def params(count):
    return pltpu.CompilerParams(
        dimension_semantics=("arbitrary",) * count, vmem_limit_bytes=LIMIT
    )


def whole(shape):
    return pl.BlockSpec(shape, lambda *step: (0,) * len(shape))


SCALAR = pl.BlockSpec(memory_space=pltpu.SMEM)


def normalize(values):
    centre = jnp.mean(values, axis=-1, keepdims=True)
    centred = values - centre
    spread = jnp.mean(centred * centred, axis=-1, keepdims=True)
    scale = lax.rsqrt(spread + EPSILON)
    return centred * scale, scale


def norm_back(grad, unit, scale, gain):
    e = grad * gain
    first = jnp.mean(e, axis=-1, keepdims=True)
    second = jnp.mean(e * unit, axis=-1, keepdims=True)
    return scale * (e - first - unit * second)


def column_sum(values):
    return jnp.sum(values, axis=0, keepdims=True)


def project_kernel(lead, x, embed, gain, shift, weight, bias, first, projected):
    stream = x[...] + embed[pl.ds(lead[0], 1), :]
    unit, _ = normalize(stream)
    rounded = (unit * gain[...] + shift[...]).astype(low)
    first[...] = rounded
    projected[...] = (mul(rounded, weight[...]) + bias[...]).astype(low)


def project(lead, x, embed, gain, shift, weight, bias):
    rows, features = x.shape
    wide = weight.shape[1]
    return pl.pallas_call(
        project_kernel,
        grid=(rows // STEP,),
        in_specs=[
            SCALAR,
            pl.BlockSpec((STEP, features), lambda i: (i, 0)),
            whole(embed.shape),
            whole(gain.shape),
            whole(shift.shape),
            whole(weight.shape),
            whole(bias.shape),
        ],
        out_specs=[
            pl.BlockSpec((STEP, features), lambda i: (i, 0)),
            pl.BlockSpec((STEP, wide), lambda i: (i, 0)),
        ],
        out_shape=[
            jax.ShapeDtypeStruct((rows, features), low),
            jax.ShapeDtypeStruct((rows, wide), low),
        ],
        compiler_params=params(1),
        name="project",
    )(lead, x, embed, gain, shift, weight, bias)


def attend_kernel(size, q, k, v, probs, mixed, inverse, turned):
    keys = k.shape[0]
    count = q.shape[0]
    scaling = size ** (-0.5) * LOG2E

    @pl.when(pl.program_id(1) == 0)
    def _():
        across = v[...].T
        tail = lax.broadcasted_iota(jnp.int32, (16, keys), 0)
        ones = jnp.where(tail == 0, 1.0, 0.0).astype(low)
        for head in range(2):
            turned[head, 0:size, :] = across[head * size : (head + 1) * size, :]
            turned[head, size : size + 16, :] = ones

    lane = lax.broadcasted_iota(jnp.int32, (1, LANES), 1)

    def scores(head, start):
        mask = jnp.where(lane // size == head, 1.0, 0.0).astype(low)
        return mul(k[start : start + STEP, :], q[...] * mask, NT) * scaling

    def finish(head, total):
        spread = total[size : size + 1, :]
        inv = 1.0 / spread
        inverse[0, head : head + 1, :] = inv
        mixed[head * size : (head + 1) * size, :] = (total[0:size, :] * inv).astype(low)
        return spread

    extremes = []
    for head in range(2):
        total = jnp.zeros((size + 16, count), full)
        for start in range(0, keys, STEP):
            p = jnp.exp2(scores(head, start)).astype(low)
            probs[0, head, start : start + STEP, :] = p
            total = total + mul(turned[head, :, start : start + STEP], p)
        spread = finish(head, total)
        extremes.append(spread)

    both = jnp.concatenate(extremes, axis=0)
    inside = jnp.where((both > 1e-18) & (both < 1e18), 1.0, 0.0)

    @pl.when(jnp.min(inside) < 0.5)
    def _():
        for head in range(2):
            top = jnp.full((1, count), -jnp.inf, full)
            for start in range(0, keys, STEP):
                top = jnp.maximum(
                    top, jnp.max(scores(head, start), axis=0, keepdims=True)
                )
            total = jnp.zeros((size + 16, count), full)
            for start in range(0, keys, STEP):
                p = jnp.exp2(scores(head, start) - top).astype(low)
                probs[0, head, start : start + STEP, :] = p
                total = total + mul(turned[head, :, start : start + STEP], p)
            finish(head, total)


def attend(projected):
    rows, wide = projected.shape
    features = wide // 3
    pairs = features // LANES
    size = features // HEADS
    return pl.pallas_call(
        functools.partial(attend_kernel, size),
        grid=(pairs, rows // STEP),
        in_specs=[
            pl.BlockSpec((STEP, LANES), lambda p, i: (i, p)),
            pl.BlockSpec((rows, LANES), lambda p, i: (0, pairs + p)),
            pl.BlockSpec((rows, LANES), lambda p, i: (0, 2 * pairs + p)),
        ],
        out_specs=[
            pl.BlockSpec((1, 2, rows, STEP), lambda p, i: (p, 0, 0, i)),
            pl.BlockSpec((LANES, STEP), lambda p, i: (p, i)),
            pl.BlockSpec((1, 8, STEP), lambda p, i: (p, 0, i)),
        ],
        out_shape=[
            jax.ShapeDtypeStruct((pairs, 2, rows, rows), low),
            jax.ShapeDtypeStruct((features, rows), low),
            jax.ShapeDtypeStruct((pairs, 8, rows), full),
        ],
        scratch_shapes=[pltpu.VMEM((2, size + 16, rows), low)],
        compiler_params=params(2),
        name="attend",
    )(projected, projected, projected)


def middle_kernel(
    spans,
    lead,
    weight,
    x,
    mixed,
    experts,
    upstream,
    embed,
    merge_w,
    merge_b,
    gain,
    shift,
    expand_w,
    expand_b,
    shrink_w,
    shrink_b,
    router_w,
    router_b,
    correction,
    blended,
    d_mid,
    d_mixed,
    grads,
):
    features = x.shape[1]
    hidden_size = expand_w.shape[1]
    channels = correction.shape[1]
    chunk = features

    @pl.when(pl.program_id(0) == 0)
    def _():
        grads[...] = jnp.zeros_like(grads)

    def add(name, values, part=0):
        base = spans[name][0]
        height = values.shape[0]
        for block in range(values.shape[1] // LANES):
            start = base + (part + block) * height
            grads[start : start + height, :] += values[
                :, block * LANES : (block + 1) * LANES
            ]

    stream = x[...] + embed[pl.ds(lead[0], 1), :]
    mid = stream + mul(mixed[...], merge_w[...], TN) + merge_b[...]
    unit, scale = normalize(mid)
    second = (unit * gain[...] + shift[...]).astype(low)
    output = mid + shrink_b[...]
    hidden, slope = [], []
    for start in range(0, hidden_size, chunk):
        part = slice(start, start + chunk)
        u = mul(second, expand_w[:, part]) + expand_b[:, part]
        square = u * u
        t = jnp.tanh(GELU_COEF * u * (1.0 + GELU_CUBE * square))
        half = 0.5 + 0.5 * t
        act = (u * half).astype(low)
        hidden.append(act)
        slope.append(
            half
            + 0.5
            * GELU_COEF
            * u
            * (1.0 - t * t)
            * (1.0 + 3.0 * GELU_CUBE * square)
        )
        output = output + mul(act, shrink_w[part, :])
    output_low = output.astype(low)
    logits = mul(output_low, router_w[...]) + router_b[...]
    lane = lax.broadcasted_iota(jnp.int32, (1, LANES), 1)
    valid = lane < channels
    parts = [logits[:, e * LANES : (e + 1) * LANES] for e in range(3)]
    largest = jnp.maximum(jnp.maximum(parts[0], parts[1]), parts[2])
    parts = [part - largest for part in parts]
    raised = [jnp.exp(part) for part in parts]
    total = raised[0] + raised[1] + raised[2]
    shared = jnp.log(total)
    logs = [part - shared for part in parts]
    inverse = 1.0 / total
    gates = [value * inverse for value in raised]

    def widen(values):
        return jnp.concatenate(
            [values, jnp.zeros((values.shape[0], LANES - channels), full)], axis=1
        )

    frames = [
        widen(experts[:, e * channels : (e + 1) * channels]) for e in range(3)
    ]
    up = widen(upstream[...])
    mix = gates[0] * frames[0] + gates[1] * frames[1] + gates[2] * frames[2]
    entropy = -(gates[0] * logs[0] + gates[1] * logs[1] + gates[2] * logs[2])
    blended[...] = mix[:, :channels] + correction[...]
    frame_weight = weight[0]
    d_parts = [
        jnp.where(
            valid,
            frame_weight
            * gates[e]
            * (up * (frames[e] - mix) - PENALTY * (logs[e] + entropy)),
            0.0,
        )
        for e in range(3)
    ]
    add("correction", frame_weight * column_sum(up))
    d_logits = jnp.concatenate(d_parts, axis=1)
    add("router_bias", column_sum(d_logits))
    d_logits_low = d_logits.astype(low)
    add("router", mul(output_low, d_logits_low, TN))
    d_output = mul(d_logits_low, router_w[...], NT)
    add("shrink_bias", column_sum(d_output))
    d_output_low = d_output.astype(low)
    d_second = jnp.zeros_like(d_output)
    for index, start in enumerate(range(0, hidden_size, chunk)):
        part = slice(start, start + chunk)
        d_pre = mul(d_output_low, shrink_w[part, :], NT) * slope[index]
        add("expand_bias", column_sum(d_pre), start // LANES)
        d_pre_low = d_pre.astype(low)
        d_second = d_second + mul(d_pre_low, expand_w[:, part], NT)
        add("expand", mul(second, d_pre_low, TN), start // LANES)
        base = spans["shrink"][0]
        product = mul(hidden[index], d_output_low, TN)
        for block in range(features // LANES):
            at = base + block * hidden_size + start
            grads[at : at + chunk, :] += product[:, block * LANES : (block + 1) * LANES]
    add("second_gain", column_sum(d_second * unit))
    add("second_shift", column_sum(d_second))
    grad_mid = d_output + norm_back(d_second, unit, scale, gain[...])
    d_mid[...] = grad_mid
    add("merge_bias", column_sum(grad_mid))
    d_mid_low = grad_mid.astype(low)
    add("merge", mul(mixed[...], d_mid_low))
    d_mixed[...] = mul(merge_w[...], d_mid_low, NT).astype(low)


def middle(spans, height, lead, weight, x, mixed, experts, upstream, tables):
    rows, features = x.shape
    channels = upstream.shape[1]
    step = 256
    return pl.pallas_call(
        functools.partial(middle_kernel, spans),
        grid=(rows // step,),
        in_specs=[
            SCALAR,
            SCALAR,
            pl.BlockSpec((step, features), lambda i: (i, 0)),
            pl.BlockSpec((features, step), lambda i: (0, i)),
            pl.BlockSpec((step, experts.shape[1]), lambda i: (i, 0)),
            pl.BlockSpec((step, channels), lambda i: (i, 0)),
        ]
        + [whole(table.shape) for table in tables],
        out_specs=[
            pl.BlockSpec((step, channels), lambda i: (i, 0)),
            pl.BlockSpec((step, features), lambda i: (i, 0)),
            pl.BlockSpec((features, step), lambda i: (0, i)),
            whole((height, LANES)),
        ],
        out_shape=[
            jax.ShapeDtypeStruct((rows, channels), full),
            jax.ShapeDtypeStruct((rows, features), full),
            jax.ShapeDtypeStruct((features, rows), low),
            jax.ShapeDtypeStruct((height, LANES), full),
        ],
        compiler_params=params(1),
        name="middle",
    )(lead, weight, x, mixed, experts, upstream, *tables)


def attend_back_kernel(
    size,
    q,
    k,
    v,
    d_mixed,
    mixed,
    inverse,
    first,
    probs,
    d_part,
    grads,
    d_across,
    d_down,
    d_query,
):
    step = pl.program_id(0)
    last = pl.num_programs(0) - 1
    rows = q.shape[0]
    block = k.shape[0]
    scaling = size ** (-0.5)
    lane = lax.broadcasted_iota(jnp.int32, (1, LANES), 1)

    @pl.when(step == 0)
    def _():
        stack = []
        for head in range(2):
            span = slice(head * size, (head + 1) * size)
            inv = inverse[0, head : head + 1, :]
            scaled = (d_mixed[span, :].astype(full) * inv).astype(low)
            stack.append(scaled)
            centre = -column_sum(scaled.astype(full) * mixed[span, :].astype(full))
            high = centre.astype(low)
            rest = centre - high.astype(full)
            mid = rest.astype(low)
            last_bits = (rest - mid.astype(full)).astype(low)
            row = lax.broadcasted_iota(jnp.int32, (size, rows), 0)
            extra = jnp.where(
                row == 0,
                high.astype(full),
                jnp.where(
                    row == 1,
                    mid.astype(full),
                    jnp.where(row == 2, last_bits.astype(full), 0.0),
                ),
            ).astype(low)
            d_across[head, span, :] = scaled
            d_across[head, (1 - head) * size : (2 - head) * size, :] = extra
        d_down[...] = jnp.concatenate(stack, axis=0).T
        d_query[...] = jnp.zeros_like(d_query)

    k_across = k[...].T
    d_keys, d_values = [], []
    for head in range(2):
        base = (1 - head) * size
        data = jnp.where(lane // size == head, 1.0, 0.0).astype(low)
        ones = jnp.where((lane >= base) & (lane < base + 3), 1.0, 0.0).astype(low)
        values = v[...] * data + ones
        d_k = jnp.zeros((block, LANES), full)
        d_v = jnp.zeros((block, LANES), full)
        for start in range(0, rows, STEP):
            span = slice(start, start + STEP)
            p = probs[0, head, :, span]
            d_p = mul(values, d_across[head, :, span])
            d_s = (p.astype(full) * d_p).astype(low)
            d_query[head * size : (head + 1) * size, span] += mul(
                k_across[head * size : (head + 1) * size, :], d_s
            )
            d_v = d_v + mul(p, d_down[span, :])
            d_k = d_k + mul(d_s, q[span, :])
        d_keys.append(d_k)
        d_values.append(d_v)
    at = pl.ds(pl.multiple_of(step * block, block), block)
    d_part[1, at, :] = (jnp.where(lane < size, *d_keys) * scaling).astype(low)
    d_part[2, at, :] = jnp.where(lane < size, *d_values).astype(low)

    @pl.when(step == last)
    def _():
        d_part[0] = (d_query[...].T * scaling).astype(low)
        features = first.shape[1]
        for kind in range(3):
            grads[kind * features : (kind + 1) * features, :] = mul(
                first[...], d_part[kind], TN
            )


def attend_back(pair, projected, d_mixed, mixed, inverse, first, probs):
    rows, wide = projected.shape
    features = wide // 3
    pairs = features // LANES
    size = features // HEADS
    return pl.pallas_call(
        functools.partial(attend_back_kernel, size),
        grid=(rows // STEP,),
        in_specs=[
            pl.BlockSpec((rows, LANES), lambda i: (0, pair)),
            pl.BlockSpec((STEP, LANES), lambda i: (i, pairs + pair)),
            pl.BlockSpec((STEP, LANES), lambda i: (i, 2 * pairs + pair)),
            pl.BlockSpec((LANES, rows), lambda i: (pair, 0)),
            pl.BlockSpec((LANES, rows), lambda i: (pair, 0)),
            pl.BlockSpec((1, 8, rows), lambda i: (pair, 0, 0)),
            whole(first.shape),
            pl.BlockSpec((1, 2, STEP, rows), lambda i: (pair, 0, i, 0)),
        ],
        out_specs=[
            whole((3, rows, LANES)),
            whole((3 * features, LANES)),
        ],
        out_shape=[
            jax.ShapeDtypeStruct((3, rows, LANES), low),
            jax.ShapeDtypeStruct((3 * features, LANES), full),
        ],
        scratch_shapes=[
            pltpu.VMEM((2, LANES, rows), low),
            pltpu.VMEM((rows, LANES), low),
            pltpu.VMEM((LANES, rows), full),
        ],
        compiler_params=params(1),
        name="attend_back",
    )(projected, projected, projected, d_mixed, mixed, inverse, first, probs)


def finish_kernel(pairs, lead, x, embed, gain, weight, d_mid, *rest):
    d_parts = rest[:pairs]
    grad_input, sums = rest[pairs:]

    @pl.when(pl.program_id(0) == 0)
    def _():
        sums[...] = jnp.zeros_like(sums)

    stream = x[...] + embed[pl.ds(lead[0], 1), :]
    unit, scale = normalize(stream)
    d_first = jnp.zeros_like(stream)
    for pair in range(pairs):
        for kind in range(3):
            at = (kind * pairs + pair) * LANES
            d_first = d_first + mul(
                d_parts[pair][kind], weight[:, at : at + LANES], NT
            )
    d_stream = d_mid[...] + norm_back(d_first, unit, scale, gain[...])
    grad_input[...] = d_stream
    lanes = [column_sum(d_parts[pair][0].astype(full)) for pair in range(pairs)]
    values = [column_sum(d_parts[pair][2].astype(full)) for pair in range(pairs)]
    sums[0:1, :] += column_sum(d_first * unit)
    sums[1:2, :] += column_sum(d_first)
    sums[2:3, :] += jnp.concatenate(lanes, axis=1)
    sums[3:4, :] += jnp.concatenate(values, axis=1)
    sums[4:5, :] += column_sum(d_stream)


def finish(lead, x, embed, gain, weight, d_mid, d_parts):
    rows, features = x.shape
    pairs = len(d_parts)
    return pl.pallas_call(
        functools.partial(finish_kernel, pairs),
        grid=(rows // STEP,),
        in_specs=[
            SCALAR,
            pl.BlockSpec((STEP, features), lambda i: (i, 0)),
            whole(embed.shape),
            whole(gain.shape),
            whole(weight.shape),
            pl.BlockSpec((STEP, features), lambda i: (i, 0)),
        ]
        + [pl.BlockSpec((3, STEP, LANES), lambda i: (0, i, 0))] * pairs,
        out_specs=[
            pl.BlockSpec((STEP, features), lambda i: (i, 0)),
            whole((8, features)),
        ],
        out_shape=[
            jax.ShapeDtypeStruct((rows, features), full),
            jax.ShapeDtypeStruct((8, features), full),
        ],
        compiler_params=params(1),
        name="finish",
    )(lead, x, embed, gain, weight, d_mid, *d_parts)


def bits_of(sizes):
    order = []
    for axis in ("dp", "rep"):
        bit = 1
        while bit < sizes[axis]:
            order.append((axis, bit))
            bit *= 2
    return order


def swap(values, sizes, axis, bit):
    return lax.ppermute(values, axis, [(i, i ^ bit) for i in range(sizes[axis])])


def sum_small(values, sizes):
    for axis, bit in bits_of(sizes):
        values = values + swap(values, sizes, axis, bit)
    return values


def sum_all(values, sizes):
    taken = []
    for axis, bit in bits_of(sizes):
        half = values.shape[0] // 2
        side = (lax.axis_index(axis) // bit) % 2
        keep = lax.dynamic_slice_in_dim(values, side * half, half, 0)
        send = lax.dynamic_slice_in_dim(values, (1 - side) * half, half, 0)
        values = keep + swap(send, sizes, axis, bit)
        taken.append((axis, bit, side))
    for axis, bit, side in reversed(taken):
        other = swap(values, sizes, axis, bit)
        values = jnp.where(
            side == 0,
            jnp.concatenate([values, other]),
            jnp.concatenate([other, values]),
        )
    return values


def up_to(value, step):
    return -(-value // step) * step


def body(sizes, *args):
    (
        block_input,
        expert_out,
        upstream,
        lead_index,
        lead_frames,
        lead_embed,
        first_gain,
        first_shift,
        attend_weight,
        query_bias,
        value_bias,
        merge_weight,
        merge_bias,
        second_gain,
        second_shift,
        expand_weight,
        expand_bias,
        shrink_weight,
        shrink_bias,
        router_weight,
        router_bias,
        correction,
    ) = args
    rows, features = block_input.shape
    channels = correction.shape[0]
    leads = lead_embed.shape[0]
    hidden = expand_bias.shape[0]
    devices = sizes["dp"] * sizes["rep"]
    pairs = features // LANES
    grain = 8 * devices

    lead_hot = (lead_index[0] == jnp.arange(leads, dtype=jnp.int32)).astype(full)
    counts = sum_small(lead_hot, sizes)
    table = lead_frames.astype(full)
    weight = (
        jnp.sum(lead_hot * table)
        * devices
        / (jnp.sum(lead_hot * counts) * jnp.sum(table))
    ).reshape(1)

    def row(vector):
        return vector.reshape(1, -1)

    bias = row(jnp.concatenate([query_bias, jnp.zeros_like(query_bias), value_bias]))
    first, projected = project(
        lead_index,
        block_input,
        lead_embed,
        row(first_gain),
        row(first_shift),
        attend_weight,
        bias,
    )
    probs, mixed, inverse = attend(projected)

    widths = (
        ("expand", features * hidden),
        ("shrink", features * hidden),
        ("merge", features * features),
        ("router", features * 3 * LANES),
        ("expand_bias", hidden),
        ("shrink_bias", features),
        ("merge_bias", features),
        ("second_gain", features),
        ("second_shift", features),
        ("router_bias", 3 * LANES),
        ("correction", LANES),
    )
    spans, height = {}, 0
    for name, width in widths:
        spans[name] = (height, height + width // LANES)
        height += width // LANES
    height = up_to(height, grain)
    wide_router = jnp.pad(
        router_weight.reshape(features, 3, channels),
        ((0, 0), (0, 0), (0, LANES - channels)),
    ).reshape(features, 3 * LANES)
    wide_bias = jnp.pad(
        router_bias.reshape(3, channels), ((0, 0), (0, LANES - channels))
    ).reshape(1, 3 * LANES)
    tables = (
        lead_embed,
        merge_weight,
        row(merge_bias),
        row(second_gain),
        row(second_shift),
        expand_weight,
        row(expand_bias),
        shrink_weight,
        row(shrink_bias),
        wide_router,
        wide_bias,
        row(correction),
    )
    blended, d_mid, d_mixed, grads = middle(
        spans,
        height,
        lead_index,
        weight,
        block_input,
        mixed,
        expert_out,
        upstream,
        tables,
    )
    d_parts, d_weights = [], []
    for pair in range(pairs):
        d_part, d_weight = attend_back(
            pair, projected, d_mixed, mixed, inverse, first, probs
        )
        d_parts.append(d_part)
        d_weights.append(d_weight)
    grad_input, sums = finish(
        lead_index,
        block_input,
        lead_embed,
        row(first_gain),
        attend_weight,
        d_mid,
        d_parts,
    )
    grads = sum_all(grads, sizes)
    embed_rows = lead_hot[:, None] * sums[4][None, :]
    tail = jnp.concatenate(
        d_weights + [sums[:4].reshape(-1, LANES), embed_rows.reshape(-1, LANES)]
    )
    tail_rows = tail.shape[0]
    tail = jnp.pad(tail, ((0, up_to(tail_rows, grain) - tail_rows), (0, 0)))
    tail = sum_all(tail, sizes)

    def matrix(values, height):
        return values.reshape(-1, height, LANES).transpose(1, 0, 2).reshape(height, -1)

    def take(name):
        start, stop = spans[name]
        return grads[start:stop]

    def clip(values):
        return values.reshape(-1, 3, LANES)[:, :, :channels].reshape(-1, 3 * channels)

    size = pairs * 3 * features
    attend_grad = (
        tail[:size]
        .reshape(pairs, 3, features, LANES)
        .transpose(2, 1, 0, 3)
        .reshape(features, 3 * features)
    )
    vectors = tail[size : size + 4 * pairs].reshape(4, features)
    embed_grad = tail[size + 4 * pairs : tail_rows].reshape(leads, features)
    return (
        blended,
        grad_input,
        embed_grad,
        vectors[0],
        vectors[1],
        attend_grad,
        vectors[2],
        vectors[3],
        matrix(take("merge"), features),
        take("merge_bias").reshape(-1),
        take("second_gain").reshape(-1),
        take("second_shift").reshape(-1),
        matrix(take("expand"), features),
        take("expand_bias").reshape(-1),
        matrix(take("shrink"), hidden),
        take("shrink_bias").reshape(-1),
        clip(matrix(take("router"), features)),
        clip(take("router_bias").reshape(1, -1)).reshape(-1),
        take("correction").reshape(-1)[:channels],
    )


def solution(mesh):
    split = P(("dp", "rep"), None)
    sizes = dict(mesh.shape)
    return jax.shard_map(
        functools.partial(body, sizes),
        mesh=mesh,
        in_specs=(split, split, split, P(("dp", "rep"))) + (P(),) * 18,
        out_specs=(split, split) + (P(),) * 17,
        check_vma=False,
    )
```

time: 1210 us -> 440 us (0.36)
  matrix products: 417 us -> 0 us
  waiting for transfers between devices: 336 us -> 139 us
  Pallas kernels: 0 us -> 184 us
  other arithmetic: 180 us -> 22.3 us
  local copies, waits for them, and re-layouts: 186 us -> 52.1 us
  blocking collectives: 42 us -> 0 us
  starting transfers between devices: 0.08 us -> 31.3 us
  loops' own time: 16.6 us -> 0 us
  between operations: 17.7 us -> 4.3 us
    dot_general x44 -> x0, matrix products: 417 us -> none  [the longest x8 89.3 us: one_block(): jnp.einsum('qhd,khd->hqk', query_block, key_rows, preferred_element_type=...]
    unnamed x4 -> x0, waiting for transfers between devices: 336 us -> none
    pallas_call x0 -> x7, Pallas kernels: none -> 184 us  [the longest x3 79.7 us: attend_back(): pl.pallas_call(functools.partial(attend_back_kernel, size), grid=(rows //...]
    ppermute x0 -> x25, waiting for transfers between devices: none -> 139 us  [swap(): lax.ppermute(values, axis, [(i, i ^ bit) for i in range(sizes[axis])])]
    convert_element_type x6 -> x1, other arithmetic: 86.5 us -> 0.01 us  [body(): (lead_index[0] == jnp.arange(leads, dtype=jnp.int32)).astype(full)]
    reduce_sum x22 -> x2, other arithmetic: 81.4 us -> 1.21 us  [the longest x1 0.61 us: body(): jnp.sum(table)]
    concatenate x1, local copies, waits for them, and re-layouts: 61.1 us -> 6.23 us  [body(): jnp.concatenate(d_weights + [sums[:4].reshape(-1, LANES), embed_rows.resh...]
    psum x1 -> x0, blocking collectives: 42 us -> none  [body(): counts = lax.psum(local_counts, ('dp', 'rep')).astype(jnp.float32)]
  transfers between devices with their start and end apart: 2 -> 25, of which waited for: 2 -> 19; matrix products, arithmetic and copies ran while one was open for 0% -> 10% of each run, Pallas kernels for 0% -> 31%
where the time goes in v1:
time: 440 us; the launch traced here: 433 us
  Pallas kernels  184 us (42%)
  waiting for transfers between devices  139 us (32%)
  local copies, waits for them, and re-layouts  52.1 us (12%)
  starting transfers between devices  31.3 us (7%)
  other arithmetic  22.3 us (5%)
    ppermute x25, waiting for transfers between devices, swap(): lax.ppermute(values, axis, [(i, i ^ bit) for i in range(sizes[axis])])  139 us
    pallas_call x3, Pallas kernels, attend_back(): pl.pallas_call(functools.partial(attend_back_kernel, size), grid=(rows //...  79.7 us
    pallas_call x1, Pallas kernels, middle(): pl.pallas_call(functools.partial(middle_kernel, spans), grid=(rows // ste...  50.3 us
    pallas_call x1, Pallas kernels, attend(): pl.pallas_call(functools.partial(attend_kernel, size), grid=(pairs, rows...  37 us
    ppermute x25, starting transfers between devices, swap(): lax.ppermute(values, axis, [(i, i ^ bit) for i in range(sizes[axis])])  31.3 us
    unnamed x39, local copies, waits for them, and re-layouts  16.3 us
    select_n x10, other arithmetic, sum_all(): jnp.where(side == 0, jnp.concatenate([values, other]), jnp.concatenate([o...  14 us
    pallas_call x1, Pallas kernels, finish(): pl.pallas_call(functools.partial(finish_kernel, pairs), grid=(rows // STE...  9.34 us
  transfers between devices with their start and end apart: 25, of which 19 were waited for; matrix products, arithmetic and copies ran while one was open for 10% of the time, Pallas kernels for 31%

profile of v1, /device:TPU:0, one launch (start us, length us, event | category | flops | bytes accessed | tf_op | source)
XLA Modules:
  0.0 433.0 jit_solution(16921010633361343378)
XLA Ops:
  1.8 1.2 reshape.154.gain
  3.1 1.2 reshape.155.shift
  5.6 7.2 %project.1 = (bf16[2048,384]{1,0:T(8,128)(2,1)}, bf16[2048,1152]{1,0:T(8,128)(2,1)}) custom-call(s32[1]{0:T(128)} %copy.66.lead, f32[2048,384]{1,0:T(8,128)} %x.11, f32[40,384]{1,0:T(8,128)} %embed.5, f32[1,384]{1,0:T(1,128)} %reshape.154.gain, f32[1,384]{1,0:T(1,128)} %reshape.155.shift, bf16[384,1152]{1,0:T(8,128)(2,1)} %weight.3, f32[1,1152]{1,0:T(1,128)} %reshape.156.bias), custom_call_target="tpu_custom_call" | custom-call | tf_op jit(solution)/shard_map/project/pallas_call | solution.py:75
  12.9 37.0 %attend.1 = (bf16[3,2,2048,2048]{3,2,1,0:T(8,128)(2,1)}, bf16[384,2048]{1,0:T(8,128)(2,1)}, f32[3,8,2048]{2,1,0:T(8,128)}) custom-call(bf16[2048,1152]{1,0:T(8,128)(2,1)} %get-tuple-element.36.q.k.v, bf16[2048,1152]{1,0:T(8,128)(2,1)} %get-tuple-element.36.q.k.v, bf16[2048,1152]{1,0:T(8,128)(2,1)} %get-tuple-element.36.q.k.v), custom_call_target="tpu_custom_call" | custom-call | tf_op jit(solution)/shard_map/attend/pallas_call | solution.py:161
  50.0 1.8 copy.50.experts
  51.8 1.3 copy.51.upstream
  58.3 2.5 collective-permute-start.1
  60.8 1.5 collective-permute-done.1
  62.3 2.1 collective-permute-start.2
  64.4 1.5 collective-permute-done.2
  65.9 3.0 collective-permute-start.3
  69.0 1.5 collective-permute-done.3
  70.5 1.8 collective-permute-start.4
  76.0 50.3 %middle.1 = (f32[2048,69]{1,0:T(8,128)}, f32[2048,384]{1,0:T(8,128)}, bf16[384,2048]{1,0:T(8,128)(2,1)}, f32[11776,128]{1,0:T(8,128)}) custom-call(s32[1]{0:T(128)} %copy.66.lead, f32[1]{0:T(128)} %bitcast.1.weight, f32[2048,384]{1,0:T(8,128)} %x.11, bf16[384,2048]{1,0:T(8,128)(2,1)} %get-tuple-element.37.mixed, f32[2048,207]{1,0:T(8,128)} %copy.50.experts, ...), custom_call_target="tpu_custom_call" | custom-call | tf_op jit(solution)/shard_map/middle/pallas_call | solution.py:323
  126.3 2.1 constant_dynamic-slice_fusion.4
  128.5 5.5 %collective-permute-done.15 = f32[5888,128]{1,0:T(8,128)} collective-permute-done((f32[5888,128]{1,0:T(8,128)S(1)}, f32[5888,128]{1,0:T(8,128)}, u32[]{:S(2)}, u32[]{:S(2)}) %collective-permute-start.15) | collective-permute-done | bytes 3014688 | tf_op jit(solution)/shard_map/ppermute | solution.py:541
  134.0 3.1 dynamic-slice_add_fusion
  137.1 1.2 constant_dynamic-slice_fusion.3
  138.3 1.8 collective-permute-start.16
  140.1 33.6 %collective-permute-done.16 = f32[2944,128]{1,0:T(8,128)} collective-permute-done((f32[2944,128]{1,0:T(8,128)}, f32[2944,128]{1,0:T(8,128)}, u32[]{:S(2)}, u32[]{:S(2)}) %collective-permute-start.16) | collective-permute-done | bytes 1507360 | tf_op jit(solution)/shard_map/ppermute | solution.py:541
  173.7 1.5 dynamic-slice_add_fusion.1
  175.3 1.1 copy-done.1
  176.4 1.9 collective-permute-start.17
  178.6 26.5 %attend_back.3 = (bf16[3,2048,128]{2,1,0:T(8,128)(2,1)}, f32[1152,128]{1,0:T(8,128)}) custom-call(bf16[2048,1152]{1,0:T(8,128)(2,1)} %get-tuple-element.36.q.k.v, bf16[2048,1152]{1,0:T(8,128)(2,1)} %get-tuple-element.36.q.k.v, bf16[2048,1152]{1,0:T(8,128)(2,1)} %get-tuple-element.36.q.k.v, bf16[384,2048]{1,0:T(8,128)(2,1)} %get-tuple-element.40.d_mixed, ...), custom_call_target="tpu_custom_call" | custom-call | tf_op jit(solution)/shard_map/attend_back/pallas_call | solution.py:443
  205.1 26.7 %attend_back.4 = (bf16[3,2048,128]{2,1,0:T(8,128)(2,1)}, f32[1152,128]{1,0:T(8,128)}) custom-call(bf16[2048,1152]{1,0:T(8,128)(2,1)} %get-tuple-element.36.q.k.v, bf16[2048,1152]{1,0:T(8,128)(2,1)} %get-tuple-element.36.q.k.v, bf16[2048,1152]{1,0:T(8,128)(2,1)} %get-tuple-element.36.q.k.v, bf16[384,2048]{1,0:T(8,128)(2,1)} %get-tuple-element.40.d_mixed, ...), custom_call_target="tpu_custom_call" | custom-call | tf_op jit(solution)/shard_map/attend_back/pallas_call | solution.py:443
  231.8 26.5 %attend_back.5 = (bf16[3,2048,128]{2,1,0:T(8,128)(2,1)}, f32[1152,128]{1,0:T(8,128)}) custom-call(bf16[2048,1152]{1,0:T(8,128)(2,1)} %get-tuple-element.36.q.k.v, bf16[2048,1152]{1,0:T(8,128)(2,1)} %get-tuple-element.36.q.k.v, bf16[2048,1152]{1,0:T(8,128)(2,1)} %get-tuple-element.36.q.k.v, bf16[384,2048]{1,0:T(8,128)(2,1)} %get-tuple-element.40.d_mixed, ...), custom_call_target="tpu_custom_call" | custom-call | tf_op jit(solution)/shard_map/attend_back/pallas_call | solution.py:443
  258.2 9.3 %finish.1 = (f32[2048,384]{1,0:T(8,128)}, f32[8,384]{1,0:T(8,128)}) custom-call(s32[1]{0:T(128)} %copy.66.lead, f32[2048,384]{1,0:T(8,128)} %x.11, f32[40,384]{1,0:T(8,128)} %embed.5, f32[1,384]{1,0:T(1,128)} %reshape.154.gain, bf16[384,1152]{1,0:T(8,128)(2,1)} %weight.3, f32[2048,384]{1,0:T(8,128)} %get-tuple-element.39.d_mid, ...), custom_call_target="tpu_custom_call" | custom-call | tf_op jit(solution)/shard_map/finish/pallas_call | solution.py:505
  269.2 2.6 collective-permute-start.18
  272.0 6.2 %concatenate.67 = f32[3588,128]{1,0:T(8,128)S(1)} concatenate(f32[1152,128]{1,0:T(8,128)} %get-tuple-element.48, f32[1152,128]{1,0:T(8,128)} %get-tuple-element.49, f32[1152,128]{1,0:T(8,128)} %get-tuple-element.50, f32[12,128]{1,0:T(8,128)S(1)} %reshape.167, f32[120,128]{1,0:T(8,128)S(1)} %broadcast_multiply_fusion), dimensions={0} | concatenate | bytes 3674112 | tf_op jit(solution)/shard_map/concatenate | solution.py:698
  279.3 8.5 %collective-permute-done.18 = f32[736,128]{1,0:T(8,128)S(1)} collective-permute-done((f32[736,128]{1,0:T(8,128)S(1)}, f32[736,128]{1,0:T(8,128)S(1)}, u32[]{:S(2)}, u32[]{:S(2)}) %collective-permute-start.18) | collective-permute-done | bytes 376864 | tf_op jit(solution)/shard_map/ppermute | solution.py:541
  287.9 1.6 collective-permute-start.19
  289.5 5.1 %collective-permute-done.19 = f32[368,128]{1,0:T(8,128)S(1)} collective-permute-done((f32[368,128]{1,0:T(8,128)S(1)}, f32[368,128]{1,0:T(8,128)S(1)}, u32[]{:S(2)}, u32[]{:S(2)}) %collective-permute-start.19) | collective-permute-done | bytes 188448 | tf_op jit(solution)/shard_map/ppermute | solution.py:541
  294.6 1.6 collective-permute-start.20
  296.3 4.2 collective-permute-done.20
  300.6 1.4 fusion
  302.1 1.6 collective-permute-start.6
  303.7 11.9 %collective-permute-done.21 = f32[736,128]{1,0:T(8,128)S(1)} collective-permute-done((f32[736,128]{1,0:T(8,128)S(1)}, f32[736,128]{1,0:T(8,128)S(1)}, u32[]{:S(2)}, u32[]{:S(2)}) %collective-permute-start.21) | collective-permute-done | bytes 376864 | tf_op jit(solution)/shard_map/ppermute | solution.py:541
  315.9 2.0 collective-permute-start.7
  317.9 17.6 %collective-permute-done.22 = f32[1472,128]{1,0:T(8,128)} collective-permute-done((f32[1472,128]{1,0:T(8,128)S(1)}, f32[1472,128]{1,0:T(8,128)}, u32[]{:S(2)}, u32[]{:S(2)}) %collective-permute-start.22) | collective-permute-done | bytes 753696 | tf_op jit(solution)/shard_map/ppermute | solution.py:541
  335.5 2.0 maximum_select_fusion.3
  337.5 1.6 collective-permute-start.23
  340.5 7.3 %collective-permute-done.8 = f32[240,128]{1,0:T(8,128)S(1)} collective-permute-done((f32[240,128]{1,0:T(8,128)S(1)}, f32[240,128]{1,0:T(8,128)S(1)}, u32[]{:S(2)}, u32[]{:S(2)}) %collective-permute-start.8) | collective-permute-done | bytes 122912 | tf_op jit(solution)/shard_map/ppermute | solution.py:541
  347.8 1.6 collective-permute-start.9
  349.4 2.7 collective-permute-done.9
  352.1 1.6 collective-permute-start.10
  353.7 2.7 collective-permute-done.10
  356.5 14.3 %collective-permute-done.23 = f32[2944,128]{1,0:T(8,128)} collective-permute-done((f32[2944,128]{1,0:T(8,128)S(1)}, f32[2944,128]{1,0:T(8,128)}, u32[]{:S(2)}, u32[]{:S(2)}) %collective-permute-start.23) | collective-permute-done | bytes 1507360 | tf_op jit(solution)/shard_map/ppermute | solution.py:541
  370.8 3.1 maximum_select_fusion.1
  374.7 7.7 %collective-permute-done.12 = f32[480,128]{1,0:T(8,128)S(1)} collective-permute-done((f32[480,128]{1,0:T(8,128)S(1)}, f32[480,128]{1,0:T(8,128)S(1)}, u32[]{:S(2)}, u32[]{:S(2)}) %collective-permute-start.12) | collective-permute-done | bytes 245792 | tf_op jit(solution)/shard_map/ppermute | solution.py:541
  382.5 1.6 collective-permute-start.13
  384.1 11.3 %collective-permute-done.13 = f32[960,128]{1,0:T(8,128)S(1)} collective-permute-done((f32[960,128]{1,0:T(8,128)S(1)}, f32[960,128]{1,0:T(8,128)S(1)}, u32[]{:S(2)}, u32[]{:S(2)}) %collective-permute-start.13) | collective-permute-done | bytes 491552 | tf_op jit(solution)/shard_map/ppermute | solution.py:541
  396.4 2.4 copy.58
  399.3 2.3 maximum_select_fusion.2
  401.7 1.2 copy-done
  403.0 1.3 slice.102
  404.9 2.8 copy.53
  407.8 2.8 copy.59
  410.5 1.4 slice_bitcast_fusion.6
  411.9 5.4 %maximum_select_fusion = f32[11776,128]{1,0:T(8,128)S(1)} fusion(f32[5888,128]{1,0:T(8,128)} %collective-permute-done.24, f32[5888,128]{1,0:T(8,128)S(1)} %maximum_select_fusion.1, pred[]{:T(512)S(6)} %eq.43), kind=kLoop, calls=%fused_computation | loop fusion | flops 4521984 | bytes 12058625 | tf_op jit(solution)/shard_map/jit(_where)/select_n | solution.py:561
  418.0 2.5 fusion.4
  422.9 2.0 copy.55
  424.9 2.0 copy.61
  426.9 2.0 copy.56
  428.9 2.0 copy.62
  (108 shorter events, 21.4 us)
Async XLA Ops:
  1.3 56.9 %collective-permute-start = (f32[40]{0:T(128)S(1)}, f32[40]{0:T(128)S(1)}, u32[]{:S(2)}, u32[]{:S(2)}) collective-permute-start(f32[40]{0:T(128)S(1)} %fusion.1), channel_id=1, source_target_pairs={{0,2},{2,0},{4,6},{6,4},{8,10},{10,8},{12,14},{14,12},{16,18},{18,... | collective-permute-start | bytes 488 | tf_op jit(solution)/shard_map/ppermute | solution.py:541
  12.9 37.0 %copy-start.5 = (f32[2048,207]{0,1:T(8,128)S(1)}, f32[2048,207]{0,1:T(8,128)}, u32[]{:S(2)}) copy-start(f32[2048,207]{0,1:T(8,128)} %param.23) | copy-start | bytes 5087236
  49.9 1.9 copy-start.6
  49.9 3.2 copy-start.9
  49.9 3.8 copy-start.10
  49.9 4.3 %copy-start.11 = (f32[384]{0:T(512)S(1)}, f32[384]{0:T(512)}, u32[]{:S(2)}) copy-start(f32[384]{0:T(512)} %param.36) | copy-start | bytes 4612
  49.9 4.9 %copy-start.8 = (f32[1536]{0:T(1024)S(1)}, f32[1536]{0:T(1024)}, u32[]{:S(2)}) copy-start(f32[1536]{0:T(1024)} %param.38) | copy-start | bytes 18436
  50.0 5.5 %copy-start.12 = (f32[384]{0:T(512)S(1)}, f32[384]{0:T(512)}, u32[]{:S(2)}) copy-start(f32[384]{0:T(512)} %param.40) | copy-start | bytes 4612
  50.0 6.0 %copy-start.7 = (bf16[384,207]{0,1:T(8,128)(2,1)S(1)}, bf16[384,207]{0,1:T(8,128)(2,1)}, u32[]{:S(2)}) copy-start(bf16[384,207]{0,1:T(8,128)(2,1)} %param.41) | copy-start | bytes 476932
  50.0 6.1 %copy-start.13 = (f32[207]{0:T(256)S(1)}, f32[207]{0:T(256)}, u32[]{:S(2)}) copy-start(f32[207]{0:T(256)} %param.42) | copy-start | bytes 2488
  50.0 6.2 %copy-start.14 = (s32[40]{0:T(128)S(1)}, s32[40]{0:T(128)}, u32[]{:S(2)}) copy-start(s32[40]{0:T(128)} %param.26) | copy-start | bytes 484
  58.3 4.0 collective-permute-start.1
  62.3 3.6 collective-permute-start.2
  65.9 4.6 %collective-permute-start.3 = (f32[40]{0:T(128)S(1)}, f32[40]{0:T(128)S(1)}, u32[]{:S(2)}, u32[]{:S(2)}) collective-permute-start(f32[40]{0:T(128)S(1)} %add.139), channel_id=1, source_target_pairs={{0,16},{2,18},{4,20},{6,22},{8,24},{10,26},{12,28},{14,30},{16,0},... | collective-permute-start | bytes 488 | tf_op jit(solution)/shard_map/ppermute | solution.py:541
  70.5 3.5 collective-permute-start.4
  128.3 5.7 %collective-permute-start.15 = (f32[5888,128]{1,0:T(8,128)S(1)}, f32[5888,128]{1,0:T(8,128)}, u32[]{:S(2)}, u32[]{:S(2)}) collective-permute-start(f32[5888,128]{1,0:T(8,128)S(1)} %constant_dynamic-slice_fusion.4), channel_id=1, source_target_pairs={{0,2},{2,0},{4,6},{6,4},{8,10},{10,8},{12,14},{14,12},{16,18},{18,... | collective-permute-start | bytes 9043976 | tf_op jit(solution)/shard_map/ppermute | solution.py:541
  138.3 35.4 %collective-permute-start.16 = (f32[2944,128]{1,0:T(8,128)}, f32[2944,128]{1,0:T(8,128)}, u32[]{:S(2)}, u32[]{:S(2)}) collective-permute-start(f32[2944,128]{1,0:T(8,128)} %constant_dynamic-slice_fusion.3), channel_id=1, source_target_pairs={{0,4},{2,6},{4,0},{6,2},{8,12},{10,14},{12,8},{14,10},{16,20},{18,... | collective-permute-start | bytes 4521992 | tf_op jit(solution)/shard_map/ppermute | solution.py:541
  175.3 1.1 copy-start.1
  176.4 92.6 %collective-permute-start.17 = (f32[1472,128]{1,0:T(8,128)S(1)}, f32[1472,128]{1,0:T(8,128)S(1)}, u32[]{:S(2)}, u32[]{:S(2)}) collective-permute-start(f32[1472,128]{1,0:T(8,128)S(1)} %constant_dynamic-slice_fusion.2), channel_id=1, source_target_pairs={{0,8},{2,10},{4,12},{6,14},{8,0},{10,2},{12,4},{14,6},{16,24},{18,... | collective-permute-start | bytes 2261000 | tf_op jit(solution)/shard_map/ppermute | solution.py:541
  258.2 10.9 %copy-start.2 = (f32[2944,128]{1,0:T(8,128)S(1)}, f32[2944,128]{1,0:T(8,128)}, u32[]{:S(2)}) copy-start(f32[2944,128]{1,0:T(8,128)} %copy-done.1) | copy-start | bytes 4521988
  269.2 18.6 %collective-permute-start.18 = (f32[736,128]{1,0:T(8,128)S(1)}, f32[736,128]{1,0:T(8,128)S(1)}, u32[]{:S(2)}, u32[]{:S(2)}) collective-permute-start(f32[736,128]{1,0:T(8,128)S(1)} %constant_dynamic-slice_fusion.1), channel_id=1, source_target_pairs={{0,16},{2,18},{4,20},{6,22},{8,24},{10,26},{12,28},{14,30},{16,0},... | collective-permute-start | bytes 1130504 | tf_op jit(solution)/shard_map/ppermute | solution.py:541
  279.3 21.3 %collective-permute-start.5 = (f32[1920,128]{1,0:T(8,128)}, f32[1920,128]{1,0:T(8,128)}, u32[]{:S(2)}, u32[]{:S(2)}) collective-permute-start(f32[1920,128]{1,0:T(8,128)} %pad_dynamic-slice_fusion), channel_id=1, source_target_pairs={{0,2},{2,0},{4,6},{6,4},{8,10},{10,8},{12,14},{14,12},{16,18},{18,... | collective-permute-start | bytes 2949128 | tf_op jit(solution)/shard_map/ppermute | solution.py:541
  287.9 6.7 %collective-permute-start.19 = (f32[368,128]{1,0:T(8,128)S(1)}, f32[368,128]{1,0:T(8,128)S(1)}, u32[]{:S(2)}, u32[]{:S(2)}) collective-permute-start(f32[368,128]{1,0:T(8,128)S(1)} %constant_dynamic-slice_fusion), channel_id=1, source_target_pairs={{0,1},{1,0},{2,3},{3,2},{4,5},{5,4},{6,7},{7,6},{8,9},{9,8},{10,11... | collective-permute-start | bytes 565256 | tf_op jit(solution)/shard_map/ppermute | solution.py:541
  294.6 5.9 %collective-permute-start.20 = (f32[368,128]{1,0:T(8,128)S(1)}, f32[368,128]{1,0:T(8,128)S(1)}, u32[]{:S(2)}, u32[]{:S(2)}) collective-permute-start(f32[368,128]{1,0:T(8,128)S(1)} %dynamic-slice_add_fusion.6), channel_id=1, source_target_pairs={{0,1},{1,0},{2,3},{3,2},{4,5},{5,4},{6,7},{7,6},{8,9},{9,8},{10,11... | collective-permute-start | bytes 565256 | tf_op jit(solution)/shard_map/ppermute | solution.py:541
  300.5 15.0 %collective-permute-start.21 = (f32[736,128]{1,0:T(8,128)S(1)}, f32[736,128]{1,0:T(8,128)S(1)}, u32[]{:S(2)}, u32[]{:S(2)}) collective-permute-start(f32[736,128]{1,0:T(8,128)S(1)} %maximum_select_fusion.7), channel_id=1, source_target_pairs={{0,16},{2,18},{4,20},{6,22},{8,24},{10,26},{12,28},{14,30},{16,0},... | collective-permute-start | bytes 1130504 | tf_op jit(solution)/shard_map/ppermute | solution.py:541
  302.1 13.7 %collective-permute-start.6 = (f32[960,128]{1,0:T(8,128)S(1)}, f32[960,128]{1,0:T(8,128)S(1)}, u32[]{:S(2)}, u32[]{:S(2)}) collective-permute-start(f32[960,128]{1,0:T(8,128)S(1)} %constant_dynamic-slice_fusion.8), channel_id=1, source_target_pairs={{0,4},{2,6},{4,0},{6,2},{8,12},{10,14},{12,8},{14,10},{16,20},{18,... | collective-permute-start | bytes 1474568 | tf_op jit(solution)/shard_map/ppermute | solution.py:541
  315.6 2.3 copy-start.4
  315.7 19.9 %collective-permute-start.22 = (f32[1472,128]{1,0:T(8,128)S(1)}, f32[1472,128]{1,0:T(8,128)}, u32[]{:S(2)}, u32[]{:S(2)}) collective-permute-start(f32[1472,128]{1,0:T(8,128)S(1)} %maximum_select_fusion.5), channel_id=1, source_target_pairs={{0,8},{2,10},{4,12},{6,14},{8,0},{10,2},{12,4},{14,6},{16,24},{18,... | collective-permute-start | bytes 2261000 | tf_op jit(solution)/shard_map/ppermute | solution.py:541
  315.9 23.9 %collective-permute-start.7 = (f32[480,128]{1,0:T(8,128)S(1)}, f32[480,128]{1,0:T(8,128)S(1)}, u32[]{:S(2)}, u32[]{:S(2)}) collective-permute-start(f32[480,128]{1,0:T(8,128)S(1)} %constant_dynamic-slice_fusion.7), channel_id=1, source_target_pairs={{0,8},{2,10},{4,12},{6,14},{8,0},{10,2},{12,4},{14,6},{16,24},{18,... | collective-permute-start | bytes 737288 | tf_op jit(solution)/shard_map/ppermute | solution.py:541
  337.5 19.0 %copy-start.3 = (f32[2944,128]{1,0:T(8,128)}, f32[2944,128]{1,0:T(8,128)S(1)}, u32[]{:S(2)}) copy-start(f32[2944,128]{1,0:T(8,128)S(1)} %maximum_select_fusion.3) | copy-start | bytes 4521988
  337.5 33.3 %collective-permute-start.23 = (f32[2944,128]{1,0:T(8,128)S(1)}, f32[2944,128]{1,0:T(8,128)}, u32[]{:S(2)}, u32[]{:S(2)}) collective-permute-start(f32[2944,128]{1,0:T(8,128)S(1)} %maximum_select_fusion.3), channel_id=1, source_target_pairs={{0,4},{2,6},{4,0},{6,2},{8,12},{10,14},{12,8},{14,10},{16,20},{18,... | collective-permute-start | bytes 4521992 | tf_op jit(solution)/shard_map/ppermute | solution.py:541
  339.8 8.0 %collective-permute-start.8 = (f32[240,128]{1,0:T(8,128)S(1)}, f32[240,128]{1,0:T(8,128)S(1)}, u32[]{:S(2)}, u32[]{:S(2)}) collective-permute-start(f32[240,128]{1,0:T(8,128)S(1)} %constant_dynamic-slice_fusion.6), channel_id=1, source_target_pairs={{0,16},{2,18},{4,20},{6,22},{8,24},{10,26},{12,28},{14,30},{16,0},... | collective-permute-start | bytes 368648 | tf_op jit(solution)/shard_map/ppermute | solution.py:541
  347.8 4.3 collective-permute-start.9
  352.1 4.3 collective-permute-start.10
  356.4 17.6 %collective-permute-start.11 = (f32[240,128]{1,0:T(8,128)S(1)}, f32[240,128]{1,0:T(8,128)S(1)}, u32[]{:S(2)}, u32[]{:S(2)}) collective-permute-start(f32[240,128]{1,0:T(8,128)S(1)} %maximum_select_fusion.9), channel_id=1, source_target_pairs={{0,16},{2,18},{4,20},{6,22},{8,24},{10,26},{12,28},{14,30},{16,0},... | collective-permute-start | bytes 368648 | tf_op jit(solution)/shard_map/ppermute | solution.py:541
  374.0 38.0 %collective-permute-start.24 = (f32[5888,128]{1,0:T(8,128)S(1)}, f32[5888,128]{1,0:T(8,128)}, u32[]{:S(2)}, u32[]{:S(2)}) collective-permute-start(f32[5888,128]{1,0:T(8,128)S(1)} %maximum_select_fusion.1), channel_id=1, source_target_pairs={{0,2},{2,0},{4,6},{6,4},{8,10},{10,8},{12,14},{14,12},{16,18},{18,... | collective-permute-start | bytes 9043976 | tf_op jit(solution)/shard_map/ppermute | solution.py:541
  374.1 8.4 %collective-permute-start.12 = (f32[480,128]{1,0:T(8,128)S(1)}, f32[480,128]{1,0:T(8,128)S(1)}, u32[]{:S(2)}, u32[]{:S(2)}) collective-permute-start(f32[480,128]{1,0:T(8,128)S(1)} %maximum_select_fusion.8), channel_id=1, source_target_pairs={{0,8},{2,10},{4,12},{6,14},{8,0},{10,2},{12,4},{14,6},{16,24},{18,... | collective-permute-start | bytes 737288 | tf_op jit(solution)/shard_map/ppermute | solution.py:541
  382.5 12.9 %collective-permute-start.13 = (f32[960,128]{1,0:T(8,128)S(1)}, f32[960,128]{1,0:T(8,128)S(1)}, u32[]{:S(2)}, u32[]{:S(2)}) collective-permute-start(f32[960,128]{1,0:T(8,128)S(1)} %maximum_select_fusion.6), channel_id=1, source_target_pairs={{0,4},{2,6},{4,0},{6,2},{8,12},{10,14},{12,8},{14,10},{16,20},{18,... | collective-permute-start | bytes 1474568 | tf_op jit(solution)/shard_map/ppermute | solution.py:541
  396.4 2.9 collective-permute-start.14
  401.7 1.3 copy-start

commit v2 on v1

--- a/solution.py
+++ b/solution.py
@@ -184,10 +184,11 @@
 
 def middle_kernel(
     spans,
+    size,
     lead,
-    weight,
     x,
     mixed,
+    inverse,
     experts,
     upstream,
     embed,
@@ -204,10 +205,12 @@
     correction,
     blended,
     d_mid,
-    d_mixed,
+    d_across,
+    d_down,
     grads,
 ):
     features = x.shape[1]
+    step = x.shape[0]
     hidden_size = expand_w.shape[1]
     channels = correction.shape[1]
     chunk = features
@@ -259,8 +262,8 @@
     total = raised[0] + raised[1] + raised[2]
     shared = jnp.log(total)
     logs = [part - shared for part in parts]
-    inverse = 1.0 / total
-    gates = [value * inverse for value in raised]
+    share = 1.0 / total
+    gates = [value * share for value in raised]
 
     def widen(values):
         return jnp.concatenate(
@@ -274,18 +277,16 @@
     mix = gates[0] * frames[0] + gates[1] * frames[1] + gates[2] * frames[2]
     entropy = -(gates[0] * logs[0] + gates[1] * logs[1] + gates[2] * logs[2])
     blended[...] = mix[:, :channels] + correction[...]
-    frame_weight = weight[0]
     d_parts = [
         jnp.where(
             valid,
-            frame_weight
-            * gates[e]
+            gates[e]
             * (up * (frames[e] - mix) - PENALTY * (logs[e] + entropy)),
             0.0,
         )
         for e in range(3)
     ]
-    add("correction", frame_weight * column_sum(up))
+    add("correction", column_sum(up))
     d_logits = jnp.concatenate(d_parts, axis=1)
     add("router_bias", column_sum(d_logits))
     d_logits_low = d_logits.astype(low)
@@ -313,21 +314,41 @@
     add("merge_bias", column_sum(grad_mid))
     d_mid_low = grad_mid.astype(low)
     add("merge", mul(mixed[...], d_mid_low))
-    d_mixed[...] = mul(merge_w[...], d_mid_low, NT).astype(low)
-
-
-def middle(spans, height, lead, weight, x, mixed, experts, upstream, tables):
+    d_mixed = mul(merge_w[...], d_mid_low, NT).astype(low).astype(full)
+    row = lax.broadcasted_iota(jnp.int32, (size, step), 0)
+    stack = []
+    for head in range(features // size):
+        span = slice(head * size, (head + 1) * size)
+        side = head % 2
+        inv = inverse[head // 2, side : side + 1, :]
+        scaled = (d_mixed[span, :] * inv).astype(low)
+        stack.append(scaled)
+        centre = -column_sum(scaled.astype(full) * mixed[span, :].astype(full))
+        one = centre.astype(low).astype(full)
+        two = (centre - one).astype(low).astype(full)
+        extra = jnp.where(
+            row == 0,
+            one,
+            jnp.where(row == 1, two, jnp.where(row == 2, centre - one - two, 0.0)),
+        ).astype(low)
+        d_across[head, side * size : (side + 1) * size, :] = scaled
+        d_across[head, (1 - side) * size : (2 - side) * size, :] = extra
+    d_down[...] = jnp.concatenate(stack, axis=0).T
+
+
+def middle(spans, height, lead, x, mixed, inverse, experts, upstream, tables):
     rows, features = x.shape
+    size = features // HEADS
     channels = upstream.shape[1]
     step = 256
     return pl.pallas_call(
-        functools.partial(middle_kernel, spans),
+        functools.partial(middle_kernel, spans, size),
         grid=(rows // step,),
         in_specs=[
             SCALAR,
-            SCALAR,
             pl.BlockSpec((step, features), lambda i: (i, 0)),
             pl.BlockSpec((features, step), lambda i: (0, i)),
+            pl.BlockSpec((inverse.shape[0], 8, step), lambda i: (0, 0, i)),
             pl.BlockSpec((step, experts.shape[1]), lambda i: (i, 0)),
             pl.BlockSpec((step, channels), lambda i: (i, 0)),
         ]
@@ -335,38 +356,29 @@
         out_specs=[
             pl.BlockSpec((step, channels), lambda i: (i, 0)),
             pl.BlockSpec((step, features), lambda i: (i, 0)),
-            pl.BlockSpec((features, step), lambda i: (0, i)),
+            pl.BlockSpec((HEADS, LANES, step), lambda i: (0, 0, i)),
+            pl.BlockSpec((step, features), lambda i: (i, 0)),
             whole((height, LANES)),
         ],
         out_shape=[
             jax.ShapeDtypeStruct((rows, channels), full),
             jax.ShapeDtypeStruct((rows, features), full),
-            jax.ShapeDtypeStruct((features, rows), low),
+            jax.ShapeDtypeStruct((HEADS, LANES, rows), low),
+            jax.ShapeDtypeStruct((rows, features), low),
             jax.ShapeDtypeStruct((height, LANES), full),
         ],
         compiler_params=params(1),
         name="middle",
-    )(lead, weight, x, mixed, experts, upstream, *tables)
-
-
-def attend_back_kernel(
-    size,
-    q,
-    k,
-    v,
-    d_mixed,
-    mixed,
-    inverse,
-    first,
-    probs,
-    d_part,
-    grads,
-    d_across,
-    d_down,
-    d_query,
-):
+    )(lead, x, mixed, inverse, experts, upstream, *tables)
+
+
+def attend_back_kernel(size, first_part, last_part, *refs):
+    if first_part:
+        q, k, v, d_across, d_down, probs, d_query, d_pair = refs[:8]
+    else:
+        q, k, v, d_across, d_down, probs, carry, _, d_query, d_pair = refs[:10]
+    total = refs[-1] if last_part else d_query
     step = pl.program_id(0)
-    last = pl.num_programs(0) - 1
     rows = q.shape[0]
     block = k.shape[0]
     scaling = size ** (-0.5)
@@ -374,31 +386,7 @@
 
     @pl.when(step == 0)
     def _():
-        stack = []
-        for head in range(2):
-            span = slice(head * size, (head + 1) * size)
-            inv = inverse[0, head : head + 1, :]
-            scaled = (d_mixed[span, :].astype(full) * inv).astype(low)
-            stack.append(scaled)
-            centre = -column_sum(scaled.astype(full) * mixed[span, :].astype(full))
-            high = centre.astype(low)
-            rest = centre - high.astype(full)
-            mid = rest.astype(low)
-            last_bits = (rest - mid.astype(full)).astype(low)
-            row = lax.broadcasted_iota(jnp.int32, (size, rows), 0)
-            extra = jnp.where(
-                row == 0,
-                high.astype(full),
-                jnp.where(
-                    row == 1,
-                    mid.astype(full),
-                    jnp.where(row == 2, last_bits.astype(full), 0.0),
-                ),
-            ).astype(low)
-            d_across[head, span, :] = scaled
-            d_across[head, (1 - head) * size : (2 - head) * size, :] = extra
-        d_down[...] = jnp.concatenate(stack, axis=0).T
-        d_query[...] = jnp.zeros_like(d_query)
+        total[...] = jnp.zeros_like(total) if first_part else carry[...]
 
     k_across = k[...].T
     d_keys, d_values = [], []
@@ -414,70 +402,108 @@
             p = probs[0, head, :, span]
             d_p = mul(values, d_across[head, :, span])
             d_s = (p.astype(full) * d_p).astype(low)
-            d_query[head * size : (head + 1) * size, span] += mul(
+            total[head * size : (head + 1) * size, span] += mul(
                 k_across[head * size : (head + 1) * size, :], d_s
             )
             d_v = d_v + mul(p, d_down[span, :])
             d_k = d_k + mul(d_s, q[span, :])
         d_keys.append(d_k)
         d_values.append(d_v)
-    at = pl.ds(pl.multiple_of(step * block, block), block)
-    d_part[1, at, :] = (jnp.where(lane < size, *d_keys) * scaling).astype(low)
-    d_part[2, at, :] = jnp.where(lane < size, *d_values).astype(low)
-
-    @pl.when(step == last)
-    def _():
-        d_part[0] = (d_query[...].T * scaling).astype(low)
-        features = first.shape[1]
-        for kind in range(3):
-            grads[kind * features : (kind + 1) * features, :] = mul(
-                first[...], d_part[kind], TN
-            )
-
-
-def attend_back(pair, projected, d_mixed, mixed, inverse, first, probs):
+    d_pair[0] = (jnp.where(lane < size, *d_keys) * scaling).astype(low)
+    d_pair[1] = jnp.where(lane < size, *d_values).astype(low)
+
+    if last_part:
+
+        @pl.when(step == pl.num_programs(0) - 1)
+        def _():
+            d_query[...] = (total[...].T * scaling).astype(low)
+
+
+def attend_back(pair, part, parts, projected, d_across, d_down, probs, carried):
     rows, wide = projected.shape
     features = wide // 3
     pairs = features // LANES
     size = features // HEADS
+    steps = rows // STEP // parts
+    base = part * steps
+    first_part, last_part = part == 0, part == parts - 1
+    across = (rows, LANES) if last_part else (LANES, rows)
     return pl.pallas_call(
-        functools.partial(attend_back_kernel, size),
-        grid=(rows // STEP,),
+        functools.partial(attend_back_kernel, size, first_part, last_part),
+        grid=(steps,),
         in_specs=[
             pl.BlockSpec((rows, LANES), lambda i: (0, pair)),
-            pl.BlockSpec((STEP, LANES), lambda i: (i, pairs + pair)),
-            pl.BlockSpec((STEP, LANES), lambda i: (i, 2 * pairs + pair)),
-            pl.BlockSpec((LANES, rows), lambda i: (pair, 0)),
-            pl.BlockSpec((LANES, rows), lambda i: (pair, 0)),
-            pl.BlockSpec((1, 8, rows), lambda i: (pair, 0, 0)),
-            whole(first.shape),
-            pl.BlockSpec((1, 2, STEP, rows), lambda i: (pair, 0, i, 0)),
-        ],
+            pl.BlockSpec((STEP, LANES), lambda i: (base + i, pairs + pair)),
+            pl.BlockSpec((STEP, LANES), lambda i: (base + i, 2 * pairs + pair)),
+            pl.BlockSpec((2, LANES, rows), lambda i: (pair, 0, 0)),
+            pl.BlockSpec((rows, LANES), lambda i: (0, pair)),
+            pl.BlockSpec((1, 2, STEP, rows), lambda i: (pair, 0, base + i, 0)),
+        ]
+        + ([] if first_part else [whole((LANES, rows)), pl.BlockSpec(memory_space=pl.ANY)]),
         out_specs=[
-            whole((3, rows, LANES)),
-            whole((3 * features, LANES)),
+            whole(across),
+            pl.BlockSpec((2, STEP, LANES), lambda i: (0, base + i, 0)),
         ],
         out_shape=[
-            jax.ShapeDtypeStruct((3, rows, LANES), low),
-            jax.ShapeDtypeStruct((3 * features, LANES), full),
-        ],
-        scratch_shapes=[
-            pltpu.VMEM((2, LANES, rows), low),
-            pltpu.VMEM((rows, LANES), low),
-            pltpu.VMEM((LANES, rows), full),
-        ],
+            jax.ShapeDtypeStruct(across, low if last_part else full),
+            jax.ShapeDtypeStruct((2, rows, LANES), low),
+        ],
+        scratch_shapes=[pltpu.VMEM((LANES, rows), full)] if last_part else [],
+        input_output_aliases={} if first_part else {7: 1},
         compiler_params=params(1),
+        cost_estimate=pl.CostEstimate(
+            flops=10 * rows * rows * 256 // parts, bytes_accessed=rows * rows * 4 // parts, transcendentals=0
+        ),
         name="attend_back",
-    )(projected, projected, projected, d_mixed, mixed, inverse, first, probs)
-
-
-def finish_kernel(pairs, lead, x, embed, gain, weight, d_mid, *rest):
-    d_parts = rest[:pairs]
-    grad_input, sums = rest[pairs:]
-
-    @pl.when(pl.program_id(0) == 0)
+    )(projected, projected, projected, d_across, d_down, probs, *carried)
+
+
+def weigh_kernel(pairs, weight, first, *refs):
+    d_query, d_pair = refs[:pairs], refs[pairs : 2 * pairs]
+    grads, sums = refs[2 * pairs :]
+    features = first.shape[1]
+    grads[...] = jnp.zeros_like(grads)
+    sums[...] = jnp.zeros_like(sums)
+    for pair in range(pairs):
+        lanes = slice(pair * LANES, (pair + 1) * LANES)
+        for kind in range(3):
+            values = d_query[pair][...] if kind == 0 else d_pair[pair][kind - 1]
+            base = (kind * pairs + pair) * features
+            grads[base : base + features, :] = mul(first[...], values, TN) * weight[0]
+            if kind != 1:
+                sums[kind // 2 : kind // 2 + 1, lanes] = weight[0] * column_sum(
+                    values.astype(full)
+                )
+
+
+def weigh(height, weight, first, d_query, d_pair):
+    features = first.shape[1]
+    vmem = pl.BlockSpec(memory_space=pltpu.VMEM)
+    pairs = len(d_query)
+    return pl.pallas_call(
+        functools.partial(weigh_kernel, pairs),
+        in_specs=[SCALAR, vmem] + [vmem] * (2 * pairs),
+        out_specs=[vmem] * 2,
+        out_shape=[
+            jax.ShapeDtypeStruct((height, LANES), full),
+            jax.ShapeDtypeStruct((8, features), full),
+        ],
+        compiler_params=pltpu.CompilerParams(vmem_limit_bytes=LIMIT),
+        name="weigh",
+    )(weight, first, *d_query, *d_pair)
+
+
+def finish_kernel(pairs, last_part, lead, weight, x, embed, gain, wide, d_mid, *rest):
+    d_query, d_pair, rest = rest[:pairs], rest[pairs : 2 * pairs], rest[2 * pairs :]
+    if last_part:
+        earlier, biases, _, grad_input, vectors, sums = rest
+    else:
+        grad_input, sums = rest
+    step = pl.program_id(0)
+
+    @pl.when(step == 0)
     def _():
-        sums[...] = jnp.zeros_like(sums)
+        sums[...] = earlier[...] if last_part else jnp.zeros_like(sums)
 
     stream = x[...] + embed[pl.ds(lead[0], 1), :]
     unit, scale = normalize(stream)
@@ -485,89 +511,174 @@
     for pair in range(pairs):
         for kind in range(3):
             at = (kind * pairs + pair) * LANES
-            d_first = d_first + mul(
-                d_parts[pair][kind], weight[:, at : at + LANES], NT
-            )
-    d_stream = d_mid[...] + norm_back(d_first, unit, scale, gain[...])
+            values = d_query[pair][...] if kind == 0 else d_pair[pair][kind - 1]
+            d_first = d_first + mul(values, wide[:, at : at + LANES], NT)
+    d_stream = (d_mid[...] + norm_back(d_first, unit, scale, gain[...])) * weight[0]
     grad_input[...] = d_stream
-    lanes = [column_sum(d_parts[pair][0].astype(full)) for pair in range(pairs)]
-    values = [column_sum(d_parts[pair][2].astype(full)) for pair in range(pairs)]
-    sums[0:1, :] += column_sum(d_first * unit)
-    sums[1:2, :] += column_sum(d_first)
-    sums[2:3, :] += jnp.concatenate(lanes, axis=1)
-    sums[3:4, :] += jnp.concatenate(values, axis=1)
-    sums[4:5, :] += column_sum(d_stream)
-
-
-def finish(lead, x, embed, gain, weight, d_mid, d_parts):
+    sums[0:1, :] += column_sum(d_first * unit) * weight[0]
+    sums[1:2, :] += column_sum(d_first) * weight[0]
+    sums[2:3, :] += column_sum(d_stream)
+
+    if last_part:
+
+        @pl.when(step == pl.num_programs(0) - 1)
+        def _():
+            vectors[...] = jnp.zeros_like(vectors)
+            for block in range(pairs):
+                lanes = slice(block * LANES, (block + 1) * LANES)
+                for index, ref in enumerate((sums, sums, biases, biases)):
+                    at = index * pairs + block
+                    vectors[at : at + 1, :] = ref[index % 2 : index % 2 + 1, lanes]
+                vectors[pl.ds((4 + lead[0]) * pairs + block, 1), :] = sums[2:3, lanes]
+
+
+def finish(part, parts, lead, weight, x, embed, gain, wide, d_mid, d_query, d_pair, carried):
     rows, features = x.shape
-    pairs = len(d_parts)
+    pairs = len(d_query)
+    steps = rows // STEP // parts
+    base = part * steps
+    last_part = part == parts - 1
+    height = up_to((4 + embed.shape[0]) * pairs, 8)
+    row_spec = pl.BlockSpec((STEP, features), lambda i: (base + i, 0))
+    small = pl.BlockSpec((8, features), lambda i: (0, 0))
     return pl.pallas_call(
-        functools.partial(finish_kernel, pairs),
-        grid=(rows // STEP,),
+        functools.partial(finish_kernel, pairs, last_part),
+        grid=(steps,),
         in_specs=[
             SCALAR,
-            pl.BlockSpec((STEP, features), lambda i: (i, 0)),
+            SCALAR,
+            row_spec,
             whole(embed.shape),
             whole(gain.shape),
-            whole(weight.shape),
-            pl.BlockSpec((STEP, features), lambda i: (i, 0)),
+            whole(wide.shape),
+            row_spec,
         ]
-        + [pl.BlockSpec((3, STEP, LANES), lambda i: (0, i, 0))] * pairs,
-        out_specs=[
-            pl.BlockSpec((STEP, features), lambda i: (i, 0)),
-            whole((8, features)),
-        ],
+        + [pl.BlockSpec((STEP, LANES), lambda i: (base + i, 0))] * pairs
+        + [pl.BlockSpec((2, STEP, LANES), lambda i: (0, base + i, 0))] * pairs
+        + ([small, small, pl.BlockSpec(memory_space=pl.ANY)] if last_part else []),
+        out_specs=[row_spec, whole((height, LANES)) if last_part else small],
         out_shape=[
             jax.ShapeDtypeStruct((rows, features), full),
-            jax.ShapeDtypeStruct((8, features), full),
-        ],
+            jax.ShapeDtypeStruct((height, LANES) if last_part else (8, features), full),
+        ],
+        scratch_shapes=[pltpu.VMEM((8, features), full)] if last_part else [],
+        input_output_aliases={9 + 2 * pairs: 0} if last_part else {},
         compiler_params=params(1),
+        cost_estimate=pl.CostEstimate(
+            flops=2 * rows * features * features * 3 // parts, bytes_accessed=rows * features * 18 // parts, transcendentals=0
+        ),
         name="finish",
-    )(lead, x, embed, gain, weight, d_mid, *d_parts)
-
-
-def bits_of(sizes):
-    order = []
-    for axis in ("dp", "rep"):
-        bit = 1
-        while bit < sizes[axis]:
-            order.append((axis, bit))
-            bit *= 2
-    return order
-
-
-def swap(values, sizes, axis, bit):
-    return lax.ppermute(values, axis, [(i, i ^ bit) for i in range(sizes[axis])])
-
-
-def sum_small(values, sizes):
-    for axis, bit in bits_of(sizes):
-        values = values + swap(values, sizes, axis, bit)
-    return values
-
-
-def sum_all(values, sizes):
-    taken = []
-    for axis, bit in bits_of(sizes):
-        half = values.shape[0] // 2
-        side = (lax.axis_index(axis) // bit) % 2
-        keep = lax.dynamic_slice_in_dim(values, side * half, half, 0)
-        send = lax.dynamic_slice_in_dim(values, (1 - side) * half, half, 0)
-        values = keep + swap(send, sizes, axis, bit)
-        taken.append((axis, bit, side))
-    for axis, bit, side in reversed(taken):
-        other = swap(values, sizes, axis, bit)
-        values = jnp.where(
-            side == 0,
-            jnp.concatenate([values, other]),
-            jnp.concatenate([other, values]),
-        )
-    return values
+    )(lead, weight, x, embed, gain, wide, d_mid, *d_query, *d_pair, *carried)
 
 
 def up_to(value, step):
     return -(-value // step) * step
+
+
+def tie(value, *others):
+    return lax.optimization_barrier((value,) + others)[0]
+
+
+def routes(sizes):
+    inner = sizes["rep"]
+    outer = sizes["dp"]
+    if outer % 2:
+        return 0, ((), ())
+    far = [inner << n for n in range(1, outer.bit_length() - 1)]
+    near = [1 << n for n in range(inner.bit_length() - 1)]
+    even, odd = [], []
+    for n in range(max(len(far), len(near))):
+        even += far[n : n + 1] + near[n : n + 1]
+    odd = even[1:-1] + even[:1] + even[-1:]
+    if len(even) > 2 and len(even) % 2 == 0:
+        odd = even[1:3] + even[:1] + even[3:]
+    return inner, (tuple(even), tuple(odd))
+
+
+class Ring:
+    def __init__(self, sizes):
+        self.count = sizes["dp"] * sizes["rep"]
+        self.core_bit, self.orders = routes(sizes)
+        self.hops = len(self.orders[0]) + 1 if self.core_bit else 0
+        self.index = lax.axis_index(("dp", "rep"))
+
+    def bits(self, hop):
+        if hop == 0:
+            return self.core_bit, self.core_bit
+        return self.orders[0][hop - 1], self.orders[1][hop - 1]
+
+    def swap(self, values, hop):
+        pair = self.bits(hop)
+        moves = [
+            (i, i ^ pair[(i // self.core_bit) % 2]) for i in range(self.count)
+        ]
+        return lax.ppermute(values, ("dp", "rep"), moves)
+
+    def side(self, hop):
+        even, odd = self.bits(hop)
+        bit = even
+        if even != odd:
+            bit = jnp.where(self.index & self.core_bit == 0, even, odd)
+        return jnp.where(self.index & bit == 0, 0, 1)
+
+    def scatter(self, values, factor=None):
+        for hop in range(self.hops):
+            half = values.shape[0] // 2
+            side = self.side(hop)
+            send = lax.dynamic_slice_in_dim(values, (1 - side) * half, half, 0)
+            keep = lax.dynamic_slice_in_dim(values, side * half, half, 0)
+            if factor is not None:
+                send, keep, factor = send * factor, keep * factor, None
+            got = self.swap(send, hop)
+            beside = yield send
+            values = keep + (got if beside is None else tie(got, beside))
+        return values
+
+    def gather(self, values, extra=None):
+        for hop in reversed(range(self.hops)):
+            height = values.shape[0]
+            send = values if extra is None else jnp.concatenate([values, extra])
+            got = self.swap(send, hop)
+            beside = yield send
+            if beside is not None:
+                got = tie(got, beside)
+            if extra is not None:
+                extra = extra + got[height:]
+                got = got[:height]
+            side = self.side(hop)
+            values = jnp.where(
+                side == 0,
+                jnp.concatenate([values, got]),
+                jnp.concatenate([got, values]),
+            )
+        return values if extra is None else (values, extra)
+
+
+class Flow:
+    def __init__(self, steps):
+        self.steps = steps
+        self.done = False
+        self.sent = None
+        self.result = None
+        self.push(None)
+
+    def push(self, beside):
+        if self.done:
+            return
+        try:
+            self.sent = self.steps.send(beside)
+        except StopIteration as stop:
+            self.done, self.sent, self.result = True, None, stop.value
+
+    def drain(self):
+        while not self.done:
+            self.push(None)
+        return self.result
+
+
+def total_of(ring, values, factor):
+    part = yield from ring.scatter(values, factor)
+    return (yield from ring.gather(part))
 
 
 def body(sizes, *args):
@@ -602,15 +713,19 @@
     devices = sizes["dp"] * sizes["rep"]
     pairs = features // LANES
     grain = 8 * devices
-
-    lead_hot = (lead_index[0] == jnp.arange(leads, dtype=jnp.int32)).astype(full)
-    counts = sum_small(lead_hot, sizes)
+    ring = Ring(sizes)
+
+    tall = max(8, 2048 // devices)
+    mine = lead_index[0].astype(full)
+    leads_seen = lax.optimization_barrier(
+        lax.all_gather(
+            lax.optimization_barrier(jnp.full((tall, LANES), mine)), ("dp", "rep")
+        )
+    )
+    count = jnp.sum((leads_seen[:, 0, 0] == mine).astype(full))
     table = lead_frames.astype(full)
-    weight = (
-        jnp.sum(lead_hot * table)
-        * devices
-        / (jnp.sum(lead_hot * counts) * jnp.sum(table))
-    ).reshape(1)
+    chosen = jnp.sum(jnp.where(jnp.arange(leads) == lead_index[0], table, 0.0))
+    weight = (chosen * devices / (count * jnp.sum(table))).reshape(1)
 
     def row(vector):
         return vector.reshape(1, -1)
@@ -666,41 +781,60 @@
         wide_bias,
         row(correction),
     )
-    blended, d_mid, d_mixed, grads = middle(
+    blended, d_mid, d_across, d_down, grads = middle(
         spans,
         height,
         lead_index,
-        weight,
         block_input,
         mixed,
+        inverse,
         expert_out,
         upstream,
         tables,
     )
-    d_parts, d_weights = [], []
+    flow = Flow(total_of(ring, grads, weight[0]))
+    parts = 2
+    d_query, d_pair = [], []
     for pair in range(pairs):
-        d_part, d_weight = attend_back(
-            pair, projected, d_mixed, mixed, inverse, first, probs
+        carried = ()
+        for part in range(parts):
+            now = d_down if flow.sent is None else tie(d_down, flow.sent)
+            carried = attend_back(
+                pair, part, parts, projected, d_across, now, probs, carried
+            )
+            flow.push(carried[0])
+        d_query.append(carried[0])
+        d_pair.append(carried[1])
+    now = weight if flow.sent is None else tie(weight, flow.sent)
+    size = 3 * pairs * features
+    tail, biases = weigh(up_to(size, grain), now, first, d_query, d_pair)
+    flow.push(tail)
+    late = Flow(ring.scatter(tail))
+    carried = ()
+    parts = 2
+    for part in range(parts):
+        sent = [f.sent for f in (flow, late) if f.sent is not None]
+        now = tie(weight, *sent)
+        grad_input, sums = finish(
+            part,
+            parts,
+            lead_index,
+            now,
+            block_input,
+            lead_embed,
+            row(first_gain),
+            attend_weight,
+            d_mid,
+            d_query,
+            d_pair,
+            carried,
         )
-        d_parts.append(d_part)
-        d_weights.append(d_weight)
-    grad_input, sums = finish(
-        lead_index,
-        block_input,
-        lead_embed,
-        row(first_gain),
-        attend_weight,
-        d_mid,
-        d_parts,
-    )
-    grads = sum_all(grads, sizes)
-    embed_rows = lead_hot[:, None] * sums[4][None, :]
-    tail = jnp.concatenate(
-        d_weights + [sums[:4].reshape(-1, LANES), embed_rows.reshape(-1, LANES)]
-    )
-    tail_rows = tail.shape[0]
-    tail = jnp.pad(tail, ((0, up_to(tail_rows, grain) - tail_rows), (0, 0)))
-    tail = sum_all(tail, sizes)
+        carried = (sums, biases, grad_input)
+        flow.push(sums)
+        late.push(sums)
+    grads = flow.drain()
+    piece = late.drain()
+    tail, vectors = Flow(ring.gather(piece, sums)).drain()
 
     def matrix(values, height):
         return values.reshape(-1, height, LANES).transpose(1, 0, 2).reshape(height, -1)
@@ -712,24 +846,17 @@
     def clip(values):
         return values.reshape(-1, 3, LANES)[:, :, :channels].reshape(-1, 3 * channels)
 
-    size = pairs * 3 * features
-    attend_grad = (
-        tail[:size]
-        .reshape(pairs, 3, features, LANES)
-        .transpose(2, 1, 0, 3)
-        .reshape(features, 3 * features)
-    )
-    vectors = tail[size : size + 4 * pairs].reshape(4, features)
-    embed_grad = tail[size + 4 * pairs : tail_rows].reshape(leads, features)
+    small = vectors[: 4 * pairs].reshape(4, features)
+    embed_grad = vectors[4 * pairs : (4 + leads) * pairs].reshape(leads, features)
     return (
         blended,
         grad_input,
         embed_grad,
-        vectors[0],
-        vectors[1],
-        attend_grad,
-        vectors[2],
-        vectors[3],
+        small[0],
+        small[1],
+        matrix(tail[:size], features),
+        small[2],
+        small[3],
         matrix(take("merge"), features),
         take("merge_bias").reshape(-1),
         take("second_gain").reshape(-1),

time: 440 us -> 368 us (0.84)
  waiting for transfers between devices: 139 us -> 53.5 us
  Pallas kernels: 184 us -> 199 us
  between operations: 4.3 us -> 17.6 us
  starting transfers between devices: 31.3 us -> 23.2 us
  local copies, waits for them, and re-layouts: 52.1 us -> 44.5 us
    ppermute x25 -> x20, waiting for transfers between devices: 139 us -> 53.5 us  [swap(): return lax.ppermute(values, ('dp', 'rep'), moves)]
    pallas_call x5 -> x10, Pallas kernels: 139 us -> 155 us  [the longest x6 83.4 us: attend_back(): pl.pallas_call(functools.partial(attend_back_kernel, size, first_part, la...]
    ppermute x25 -> x20, starting transfers between devices: 31.3 us -> 23.1 us  [swap(): return lax.ppermute(values, ('dp', 'rep'), moves)]
    concatenate x1 -> x0, local copies, waits for them, and re-layouts: 6.23 us -> none  [body(): jnp.concatenate(d_weights + [sums[:4].reshape(-1, LANES), embed_rows.resh...]
    unnamed x39 -> x48, local copies, waits for them, and re-layouts: 16.3 us -> 17.8 us
  transfers between devices with their start and end apart: 25 -> 21, of which waited for: 19 -> 12; matrix products, arithmetic and copies ran while one was open for 10% -> 8% of each run, Pallas kernels for 31% -> 53%
where the time goes in v2:
time: 368 us; the launch traced here: 362 us
  Pallas kernels  199 us (54%)
  waiting for transfers between devices  53.5 us (15%)
  local copies, waits for them, and re-layouts  44.5 us (12%)
  other arithmetic  23.4 us (6%)
  starting transfers between devices  23.2 us (6%)
  between operations  17.6 us (5%)
    pallas_call x6, Pallas kernels, attend_back(): pl.pallas_call(functools.partial(attend_back_kernel, size, first_part, la...  83.4 us
    ppermute x20, waiting for transfers between devices, swap(): return lax.ppermute(values, ('dp', 'rep'), moves)  53.5 us
    pallas_call x1, Pallas kernels, middle(): pl.pallas_call(functools.partial(middle_kernel, spans, size), grid=(rows...  51.4 us
    pallas_call x1, Pallas kernels, attend(): pl.pallas_call(functools.partial(attend_kernel, size), grid=(pairs, rows...  37 us
    ppermute x20, starting transfers between devices, swap(): return lax.ppermute(values, ('dp', 'rep'), moves)  23.1 us
    unnamed x48, local copies, waits for them, and re-layouts  17.8 us
    pallas_call x2, Pallas kernels, finish(): pl.pallas_call(functools.partial(finish_kernel, pairs, last_part), grid=(...  12.4 us
    select_n x10, other arithmetic, gather(): jnp.where(side == 0, jnp.concatenate([values, got]), jnp.concatenate([got...  10.8 us
  transfers between devices with their start and end apart: 21, of which 12 were waited for; matrix products, arithmetic and copies ran while one was open for 8% of the time, Pallas kernels for 53%

profile of v2, /device:TPU:0, one launch (start us, length us, event | category | flops | bytes accessed | tf_op | source)
XLA Modules:
  0.0 361.6 jit_solution(12487750683625397900)
XLA Ops:
  8.5 1.2 reshape.144.gain
  9.8 1.2 reshape.145.shift
  11.0 0.7 pad_maximum_fusion.7
  12.3 7.3 %project.1 = (bf16[2048,384]{1,0:T(8,128)(2,1)}, bf16[2048,1152]{1,0:T(8,128)(2,1)}) custom-call(s32[1]{0:T(128)} %copy.117.lead, f32[2048,384]{1,0:T(8,128)} %x.11, f32[40,384]{1,0:T(8,128)} %embed.7, f32[1,384]{1,0:T(1,128)} %reshape.144.gain, f32[1,384]{1,0:T(1,128)} %reshape.145.shift, bf16[384,1152]{1,0:T(8,128)(2,1)} %wide.3, f32[1,1152]{1,0:T(1,128)} %reshape.146.bias), custom_call_target="tpu_custom_call" | custom-call | tf_op jit(solution)/shard_map/project/pallas_call | solution.py:75
  19.6 37.0 %attend.1 = (bf16[3,2,2048,2048]{3,2,1,0:T(8,128)(2,1)}, bf16[384,2048]{1,0:T(8,128)(2,1)}, f32[3,8,2048]{2,1,0:T(8,128)}) custom-call(bf16[2048,1152]{1,0:T(8,128)(2,1)} %get-tuple-element.67.q.k.v.refs_0_.refs_1_.refs_2_, bf16[2048,1152]{1,0:T(8,128)(2,1)} %get-tuple-element.67.q.k.v.refs_0_.refs_1_.refs_2_, ...), custom_call_target="tpu_custom_call" | custom-call | tf_op jit(solution)/shard_map/attend/pallas_call | solution.py:161
  56.7 1.8 copy.95.experts
  58.5 1.4 copy.96.upstream
  62.8 0.9 copy.97.router_w
  65.6 51.4 %middle.1 = (f32[2048,69]{1,0:T(8,128)}, f32[2048,384]{1,0:T(8,128)}, bf16[6,128,2048]{2,1,0:T(8,128)(2,1)}, bf16[2048,384]{1,0:T(8,128)(2,1)}, f32[11776,128]{1,0:T(8,128)}) custom-call(s32[1]{0:T(128)} %copy.117.lead, f32[2048,384]{1,0:T(8,128)} %x.11, bf16[384,2048]{1,0:T(8,128)(2,1)} %get-tuple-element.68.mixed, ...), custom_call_target="tpu_custom_call" | custom-call | tf_op jit(solution)/shard_map/middle/pallas_call | solution.py:344
  117.0 0.9 slice.135
  120.0 3.7 %dynamic-slice_multiply_fusion = f32[5888,128]{1,0:T(8,128)} fusion(f32[11776,128]{1,0:T(8,128)} %get-tuple-element.71, s32[]{:T(128)S(6)} %select_n.204, f32[]{:T(128)} %div.3), kind=kLoop, calls=%fused_computation.2 | loop fusion | flops 753664 | bytes 6029320 | tf_op jit(solution)/shard_map/mul | solution.py:631
  124.0 13.4 %attend_back.6 = (f32[128,2048]{1,0:T(8,128)}, bf16[2,2048,128]{2,1,0:T(8,128)(2,1)}) custom-call(bf16[2048,1152]{1,0:T(8,128)(2,1)} %get-tuple-element.67.q.k.v.refs_0_.refs_1_.refs_2_, bf16[2048,1152]{1,0:T(8,128)(2,1)} %get-tuple-element.67.q.k.v.refs_0_.refs_1_.refs_2_, bf16[2048,1152]{1,0:T(8,128)(2,1)} %get-tuple-element.67.q.k.v.refs_0_.refs_1_.refs_2_, ...), custom_call_target="tpu_custom_call" | custom-call | flops 5368709120 | bytes 8388608 | tf_op jit(solution)/shard_map/attend_back/pallas_call | solution.py:431
  137.5 1.6 copy-done.6
  139.1 3.1 multiply_add_fusion
  142.2 1.2 constant_dynamic-slice_fusion.8
  143.4 2.5 collective-permute-start.1
  145.9 14.4 %attend_back.7 = (bf16[2048,128]{1,0:T(8,128)(2,1)}, bf16[2,2048,128]{2,1,0:T(8,128)(2,1)}) custom-call(bf16[2048,1152]{1,0:T(8,128)(2,1)} %get-tuple-element.67.q.k.v.refs_0_.refs_1_.refs_2_, bf16[2048,1152]{1,0:T(8,128)(2,1)} %get-tuple-element.67.q.k.v.refs_0_.refs_1_.refs_2_, ...), custom_call_target="tpu_custom_call", output_to_operand_aliasing={{1}: (7, {})} | custom-call | flops 5368709120 | bytes 8388608 | tf_op jit(solution)/shard_map/attend_back/pallas_call | solution.py:431
  160.3 3.6 collective-permute-done.1
  163.9 1.5 dynamic-slice_add_fusion
  165.5 1.1 copy-done.4
  166.6 2.1 collective-permute-start.2
  168.7 13.5 %attend_back.8 = (f32[128,2048]{1,0:T(8,128)}, bf16[2,2048,128]{2,1,0:T(8,128)(2,1)}) custom-call(bf16[2048,1152]{1,0:T(8,128)(2,1)} %get-tuple-element.67.q.k.v.refs_0_.refs_1_.refs_2_, bf16[2048,1152]{1,0:T(8,128)(2,1)} %get-tuple-element.67.q.k.v.refs_0_.refs_1_.refs_2_, bf16[2048,1152]{1,0:T(8,128)(2,1)} %get-tuple-element.67.q.k.v.refs_0_.refs_1_.refs_2_, ...), custom_call_target="tpu_custom_call" | custom-call | flops 5368709120 | bytes 8388608 | tf_op jit(solution)/shard_map/attend_back/pallas_call | solution.py:431
  182.4 1.7 collective-permute-start.3
  184.0 14.2 %attend_back.9 = (bf16[2048,128]{1,0:T(8,128)(2,1)}, bf16[2,2048,128]{2,1,0:T(8,128)(2,1)}) custom-call(bf16[2048,1152]{1,0:T(8,128)(2,1)} %get-tuple-element.67.q.k.v.refs_0_.refs_1_.refs_2_, bf16[2048,1152]{1,0:T(8,128)(2,1)} %get-tuple-element.67.q.k.v.refs_0_.refs_1_.refs_2_, ...), custom_call_target="tpu_custom_call", output_to_operand_aliasing={{1}: (7, {})} | custom-call | flops 5368709120 | bytes 8388608 | tf_op jit(solution)/shard_map/attend_back/pallas_call | solution.py:431
  198.3 2.7 collective-permute-start.4
  201.0 13.6 %attend_back.10 = (f32[128,2048]{1,0:T(8,128)}, bf16[2,2048,128]{2,1,0:T(8,128)(2,1)}) custom-call(bf16[2048,1152]{1,0:T(8,128)(2,1)} %get-tuple-element.67.q.k.v.refs_0_.refs_1_.refs_2_, bf16[2048,1152]{1,0:T(8,128)(2,1)} %get-tuple-element.67.q.k.v.refs_0_.refs_1_.refs_2_, bf16[2048,1152]{1,0:T(8,128)(2,1)} %get-tuple-element.67.q.k.v.refs_0_.refs_1_.refs_2_, ...), custom_call_target="tpu_custom_call" | custom-call | flops 5368709120 | bytes 8388608 | tf_op jit(solution)/shard_map/attend_back/pallas_call | solution.py:431
  215.0 14.2 %attend_back.11 = (bf16[2048,128]{1,0:T(8,128)(2,1)}, bf16[2,2048,128]{2,1,0:T(8,128)(2,1)}) custom-call(bf16[2048,1152]{1,0:T(8,128)(2,1)} %get-tuple-element.67.q.k.v.refs_0_.refs_1_.refs_2_, bf16[2048,1152]{1,0:T(8,128)(2,1)} %get-tuple-element.67.q.k.v.refs_0_.refs_1_.refs_2_, ...), custom_call_target="tpu_custom_call", output_to_operand_aliasing={{1}: (7, {})} | custom-call | flops 5368709120 | bytes 8388608 | tf_op jit(solution)/shard_map/attend_back/pallas_call | solution.py:431
  229.3 7.9 %weigh.1 = (f32[3584,128]{1,0:T(8,128)}, f32[8,384]{1,0:T(8,128)}) custom-call(f32[1]{0:T(128)} %bitcast.4.weight, bf16[2048,384]{1,0:T(8,128)(2,1)} %get-tuple-element.97.first, bf16[2048,128]{1,0:T(8,128)(2,1)} %get-tuple-element.80.refs_0_.rest_0_, bf16[2048,128]{1,0:T(8,128)(2,1)} %get-tuple-element.87.refs_1_.rest_1_, ...), custom_call_target="tpu_custom_call" | custom-call | tf_op jit(solution)/shard_map/weigh/pallas_call | solution.py:483
  237.2 1.2 constant_dynamic-slice_fusion.4
  239.0 7.2 %collective-permute-done.6 = f32[736,128]{1,0:T(8,128)S(1)} collective-permute-done((f32[736,128]{1,0:T(8,128)S(1)}, f32[736,128]{1,0:T(8,128)S(1)}, u32[]{:S(2)}, u32[]{:S(2)}) %collective-permute-start.6) | collective-permute-done | bytes 376864 | tf_op jit(solution)/shard_map/ppermute | solution.py:615
  246.8 6.1 %finish.2 = (f32[2048,384]{1,0:T(8,128)}, f32[8,384]{1,0:T(8,128)}) custom-call(s32[1]{0:T(128)} %copy.117.lead, f32[1]{0:T(128)} %bitcast.4.weight, f32[2048,384]{1,0:T(8,128)} %x.11, f32[40,384]{1,0:T(8,128)} %embed.7, f32[1,384]{1,0:T(1,128)} %reshape.144.gain, bf16[384,1152]{1,0:T(8,128)(2,1)} %wide.3, f32[2048,384]{1,0:T(8,128)} %get-tuple-element.104.d_mid, ...), custom_call_target="tpu_custom_call" | custom-call | flops 905969664 | bytes 7077888 | tf_op jit(solution)/shard_map/finish/pallas_call | solution.py:544
  253.1 1.6 collective-permute-start.9
  254.6 6.3 %collective-permute-done.7 = f32[1472,128]{1,0:T(8,128)} collective-permute-done((f32[1472,128]{1,0:T(8,128)S(1)}, f32[1472,128]{1,0:T(8,128)}, u32[]{:S(2)}, u32[]{:S(2)}) %collective-permute-start.7) | collective-permute-done | bytes 753696 | tf_op jit(solution)/shard_map/ppermute | solution.py:615
  261.0 1.5 maximum_select_fusion.2
  262.5 6.3 %finish.3 = (f32[2048,384]{1,0:T(8,128)}, f32[136,128]{1,0:T(8,128)}) custom-call(s32[1]{0:T(128)} %copy.117.lead, f32[1]{0:T(128)} %bitcast.4.weight, f32[2048,384]{1,0:T(8,128)} %x.11, f32[40,384]{1,0:T(8,128)} %embed.7, f32[1,384]{1,0:T(1,128)} %reshape.144.gain, bf16[384,1152]{1,0:T(8,128)(2,1)} %wide.3, ...), custom_call_target="tpu_custom_call", output_to_operand_aliasing={{0}: (15, {})} | custom-call | flops 905969664 | bytes 7077888 | tf_op jit(solution)/shard_map/finish/pallas_call | solution.py:544
  269.6 5.4 %collective-permute-done.10 = f32[448,128]{1,0:T(8,128)S(1)} collective-permute-done((f32[448,128]{1,0:T(8,128)S(1)}, f32[448,128]{1,0:T(8,128)S(1)}, u32[]{:S(2)}, u32[]{:S(2)}) %collective-permute-start.10) | collective-permute-done | bytes 229408 | tf_op jit(solution)/shard_map/ppermute | solution.py:615
  275.1 4.8 %collective-permute-done.11 = f32[224,128]{1,0:T(8,128)S(1)} collective-permute-done((f32[224,128]{1,0:T(8,128)S(1)}, f32[224,128]{1,0:T(8,128)S(1)}, u32[]{:S(2)}, u32[]{:S(2)}) %collective-permute-start.11) | collective-permute-done | bytes 114720 | tf_op jit(solution)/shard_map/ppermute | solution.py:615
  280.0 3.3 collective-permute-start.12
  283.3 2.5 collective-permute-done.12
  285.8 2.7 collective-permute-start.13
  288.5 4.1 %collective-permute-done.13 = f32[248,128]{1,0:T(8,128)S(1)} collective-permute-done((f32[248,128]{1,0:T(8,128)S(1)}, f32[248,128]{1,0:T(8,128)S(1)}, u32[]{:S(2)}, u32[]{:S(2)}) %collective-permute-start.13) | collective-permute-done | bytes 127008 | tf_op jit(solution)/shard_map/ppermute | solution.py:615
  292.7 1.5 collective-permute-start.18
  294.3 4.0 %collective-permute-done.14 = f32[360,128]{1,0:T(8,128)S(1)} collective-permute-done((f32[360,128]{1,0:T(8,128)S(1)}, f32[360,128]{1,0:T(8,128)S(1)}, u32[]{:S(2)}, u32[]{:S(2)}) %collective-permute-start.14) | collective-permute-done | bytes 184352 | tf_op jit(solution)/shard_map/ppermute | solution.py:615
  299.0 9.4 %collective-permute-done.15 = f32[584,128]{1,0:T(8,128)S(1)} collective-permute-done((f32[584,128]{1,0:T(8,128)S(1)}, f32[584,128]{1,0:T(8,128)S(1)}, u32[]{:S(2)}, u32[]{:S(2)}) %collective-permute-start.15) | collective-permute-done | bytes 299040 | tf_op jit(solution)/shard_map/ppermute | solution.py:615
  308.6 1.5 collective-permute-start.16
  310.1 2.5 collective-permute-done.18
  312.6 2.3 maximum_select_fusion.1
  315.0 3.2 collective-permute-done.16
  318.4 0.9 copy-done
  319.3 1.0 pad_maximum_fusion.2
  320.3 2.4 copy.104
  323.2 0.9 slice_add_fusion
  324.7 1.3 slice.148
  326.2 1.4 fusion
  327.6 2.8 copy.99
  330.4 2.8 copy.105
  333.7 5.4 %maximum_select_fusion = f32[11776,128]{1,0:T(8,128)S(1)} fusion(f32[5888,128]{1,0:T(8,128)} %collective-permute-done.19, f32[5888,128]{1,0:T(8,128)S(1)} %maximum_select_fusion.1, pred[]{:T(512)S(6)} %eq.42), kind=kLoop, calls=%fused_computation | loop fusion | flops 4521984 | bytes 12058625 | tf_op jit(solution)/shard_map/jit(_where)/select_n | solution.py:649
  339.8 2.5 fusion.4
  343.6 1.1 copy.106
  344.7 2.0 copy.101
  346.7 2.0 copy.107
  348.7 2.0 copy.102
  350.7 2.0 copy.108
  352.9 0.8 reshape.173
  (117 shorter events, 15.6 us)
Async XLA Ops:
  7.2 109.8 %all-gather.3.cloned.1.call-start = ((), (), s32[]{:S(2)}) async-start(), calls=%async_computation | async-start | bytes 1081344 | tf_op jit(solution)/shard_map/all_gather | solution.py:721
  19.6 37.0 %copy-start.8 = (f32[2048,207]{0,1:T(8,128)S(1)}, f32[2048,207]{0,1:T(8,128)}, u32[]{:S(2)}) copy-start(f32[2048,207]{0,1:T(8,128)} %param.23) | copy-start | bytes 5087236
  56.6 1.9 copy-start.9
  56.6 3.2 copy-start.13
  56.6 3.8 %copy-start.14 = (f32[384]{0:T(512)S(1)}, f32[384]{0:T(512)}, u32[]{:S(2)}) copy-start(f32[384]{0:T(512)} %param.35) | copy-start | bytes 4612
  56.6 4.3 %copy-start.15 = (f32[384]{0:T(512)S(1)}, f32[384]{0:T(512)}, u32[]{:S(2)}) copy-start(f32[384]{0:T(512)} %param.36) | copy-start | bytes 4612
  56.7 4.9 %copy-start.12 = (f32[1536]{0:T(1024)S(1)}, f32[1536]{0:T(1024)}, u32[]{:S(2)}) copy-start(f32[1536]{0:T(1024)} %param.38) | copy-start | bytes 18436
  56.7 5.5 %copy-start.16 = (f32[384]{0:T(512)S(1)}, f32[384]{0:T(512)}, u32[]{:S(2)}) copy-start(f32[384]{0:T(512)} %param.40) | copy-start | bytes 4612
  56.7 6.0 %copy-start.11 = (bf16[384,207]{0,1:T(8,128)(2,1)S(1)}, bf16[384,207]{0,1:T(8,128)(2,1)}, u32[]{:S(2)}) copy-start(bf16[384,207]{0,1:T(8,128)(2,1)} %param.41) | copy-start | bytes 476932
  58.5 5.2 %copy-start.17 = (f32[207]{0:T(256)S(1)}, f32[207]{0:T(256)}, u32[]{:S(2)}) copy-start(f32[207]{0:T(256)} %param.42) | copy-start | bytes 2488
  58.5 5.9 %copy-start.18 = (s32[40]{0:T(128)S(1)}, s32[40]{0:T(128)}, u32[]{:S(2)}) copy-start(s32[40]{0:T(128)} %param.26) | copy-start | bytes 484
  123.6 13.8 %collective-permute-start = (f32[5888,128]{1,0:T(8,128)}, f32[5888,128]{1,0:T(8,128)S(1)}, u32[]{:S(2)}, u32[]{:S(2)}) collective-permute-start(f32[5888,128]{1,0:T(8,128)} %dynamic-slice_multiply_fusion), channel_id=1, source_target_pairs={{0,2},{1,3},{2,0},{3,1},{4,6},{5,7},{6,4},{7,5},{8,10},{9,11},{10,... | collective-permute-start | bytes 9043976 | tf_op jit(solution)/shard_map/ppermute | solution.py:615
  137.5 1.6 copy-start.6
  143.4 20.5 %collective-permute-start.1 = (f32[2944,128]{1,0:T(8,128)}, f32[2944,128]{1,0:T(8,128)}, u32[]{:S(2)}, u32[]{:S(2)}) collective-permute-start(f32[2944,128]{1,0:T(8,128)} %constant_dynamic-slice_fusion.8), channel_id=1, source_target_pairs={{0,4},{1,5},{2,3},{3,2},{4,0},{5,1},{6,7},{7,6},{8,12},{9,13},{10,... | collective-permute-start | bytes 4521992 | tf_op jit(solution)/shard_map/ppermute | solution.py:615
  165.4 1.1 copy-start.4
  166.6 15.6 %collective-permute-start.2 = (f32[1472,128]{1,0:T(8,128)S(1)}, f32[1472,128]{1,0:T(8,128)S(1)}, u32[]{:S(2)}, u32[]{:S(2)}) collective-permute-start(f32[1472,128]{1,0:T(8,128)S(1)} %constant_dynamic-slice_fusion.7), channel_id=1, source_target_pairs={{0,1},{1,0},{2,10},{3,11},{4,5},{5,4},{6,14},{7,15},{8,9},{9,8},{1... | collective-permute-start | bytes 2261000 | tf_op jit(solution)/shard_map/ppermute | solution.py:615
  168.7 13.5 %copy-start.5 = (f32[2944,128]{1,0:T(8,128)S(1)}, f32[2944,128]{1,0:T(8,128)}, u32[]{:S(2)}) copy-start(f32[2944,128]{1,0:T(8,128)} %copy-done.4) | copy-start | bytes 4521988
  182.4 15.9 %collective-permute-start.3 = (f32[736,128]{1,0:T(8,128)S(1)}, f32[736,128]{1,0:T(8,128)S(1)}, u32[]{:S(2)}, u32[]{:S(2)}) collective-permute-start(f32[736,128]{1,0:T(8,128)S(1)} %constant_dynamic-slice_fusion.6), channel_id=1, source_target_pairs={{0,8},{1,9},{2,6},{3,7},{4,12},{5,13},{6,2},{7,3},{8,0},{9,1},{10,... | collective-permute-start | bytes 1130504 | tf_op jit(solution)/shard_map/ppermute | solution.py:615
  198.3 16.3 %collective-permute-start.4 = (f32[368,128]{1,0:T(8,128)S(1)}, f32[368,128]{1,0:T(8,128)S(1)}, u32[]{:S(2)}, u32[]{:S(2)}) collective-permute-start(f32[368,128]{1,0:T(8,128)S(1)} %constant_dynamic-slice_fusion.5), channel_id=1, source_target_pairs={{0,16},{1,17},{2,18},{3,19},{4,20},{5,21},{6,22},{7,23},{8,24},{9,... | collective-permute-start | bytes 565256 | tf_op jit(solution)/shard_map/ppermute | solution.py:615
  214.6 14.6 %collective-permute-start.5 = (f32[368,128]{1,0:T(8,128)S(1)}, f32[368,128]{1,0:T(8,128)S(1)}, u32[]{:S(2)}, u32[]{:S(2)}) collective-permute-start(f32[368,128]{1,0:T(8,128)S(1)} %dynamic-slice_add_fusion.6), channel_id=1, source_target_pairs={{0,16},{1,17},{2,18},{3,19},{4,20},{5,21},{6,22},{7,23},{8,24},{9,... | collective-permute-start | bytes 565256 | tf_op jit(solution)/shard_map/ppermute | solution.py:615
  238.4 14.5 %collective-permute-start.8 = (f32[1792,128]{1,0:T(8,128)S(1)}, f32[1792,128]{1,0:T(8,128)S(1)}, u32[]{:S(2)}, u32[]{:S(2)}) collective-permute-start(f32[1792,128]{1,0:T(8,128)S(1)} %constant_dynamic-slice_fusion.4), channel_id=1, source_target_pairs={{0,2},{1,3},{2,0},{3,1},{4,6},{5,7},{6,4},{7,5},{8,10},{9,11},{10,... | collective-permute-start | bytes 2752520 | tf_op jit(solution)/shard_map/ppermute | solution.py:615
  238.5 7.7 %collective-permute-start.6 = (f32[736,128]{1,0:T(8,128)S(1)}, f32[736,128]{1,0:T(8,128)S(1)}, u32[]{:S(2)}, u32[]{:S(2)}) collective-permute-start(f32[736,128]{1,0:T(8,128)S(1)} %maximum_select_fusion.6), channel_id=1, source_target_pairs={{0,8},{1,9},{2,6},{3,7},{4,12},{5,13},{6,2},{7,3},{8,0},{9,1},{10,... | collective-permute-start | bytes 1130504 | tf_op jit(solution)/shard_map/ppermute | solution.py:615
  246.2 14.7 %collective-permute-start.7 = (f32[1472,128]{1,0:T(8,128)S(1)}, f32[1472,128]{1,0:T(8,128)}, u32[]{:S(2)}, u32[]{:S(2)}) collective-permute-start(f32[1472,128]{1,0:T(8,128)S(1)} %maximum_select_fusion.4), channel_id=1, source_target_pairs={{0,1},{1,0},{2,10},{3,11},{4,5},{5,4},{6,14},{7,15},{8,9},{9,8},{1... | collective-permute-start | bytes 2261000 | tf_op jit(solution)/shard_map/ppermute | solution.py:615
  246.8 6.1 %copy-start.7 = (f32[3584,128]{1,0:T(8,128)S(1)}, f32[3584,128]{1,0:T(8,128)}, u32[]{:S(2)}) copy-start(f32[3584,128]{1,0:T(8,128)} %get-tuple-element.101) | copy-start | bytes 5505028
  253.1 15.7 %collective-permute-start.9 = (f32[896,128]{1,0:T(8,128)S(1)}, f32[896,128]{1,0:T(8,128)S(1)}, u32[]{:S(2)}, u32[]{:S(2)}) collective-permute-start(f32[896,128]{1,0:T(8,128)S(1)} %constant_dynamic-slice_fusion.3), channel_id=1, source_target_pairs={{0,4},{1,5},{2,3},{3,2},{4,0},{5,1},{6,7},{7,6},{8,12},{9,13},{10,... | collective-permute-start | bytes 1376264 | tf_op jit(solution)/shard_map/ppermute | solution.py:615
  262.5 30.2 %copy-start.2 = (f32[2944,128]{1,0:T(8,128)}, f32[2944,128]{1,0:T(8,128)S(1)}, u32[]{:S(2)}) copy-start(f32[2944,128]{1,0:T(8,128)S(1)} %maximum_select_fusion.2) | copy-start | bytes 4521988
  268.8 17.0 %copy-start.10 = (f32[136,128]{1,0:T(8,128)S(1)}, f32[136,128]{1,0:T(8,128)}, u32[]{:S(2)}) copy-start(f32[136,128]{1,0:T(8,128)} %get-tuple-element.112) | copy-start | bytes 208900
  268.9 6.1 %collective-permute-start.10 = (f32[448,128]{1,0:T(8,128)S(1)}, f32[448,128]{1,0:T(8,128)S(1)}, u32[]{:S(2)}, u32[]{:S(2)}) collective-permute-start(f32[448,128]{1,0:T(8,128)S(1)} %constant_dynamic-slice_fusion.2), channel_id=1, source_target_pairs={{0,1},{1,0},{2,10},{3,11},{4,5},{5,4},{6,14},{7,15},{8,9},{9,8},{1... | collective-permute-start | bytes 688136 | tf_op jit(solution)/shard_map/ppermute | solution.py:615
  275.1 4.9 %collective-permute-start.11 = (f32[224,128]{1,0:T(8,128)S(1)}, f32[224,128]{1,0:T(8,128)S(1)}, u32[]{:S(2)}, u32[]{:S(2)}) collective-permute-start(f32[224,128]{1,0:T(8,128)S(1)} %constant_dynamic-slice_fusion.1), channel_id=1, source_target_pairs={{0,8},{1,9},{2,6},{3,7},{4,12},{5,13},{6,2},{7,3},{8,0},{9,1},{10,... | collective-permute-start | bytes 344072 | tf_op jit(solution)/shard_map/ppermute | solution.py:615
  280.0 5.8 %collective-permute-start.12 = (f32[112,128]{1,0:T(8,128)S(1)}, f32[112,128]{1,0:T(8,128)S(1)}, u32[]{:S(2)}, u32[]{:S(2)}) collective-permute-start(f32[112,128]{1,0:T(8,128)S(1)} %constant_dynamic-slice_fusion), channel_id=1, source_target_pairs={{0,16},{1,17},{2,18},{3,19},{4,20},{5,21},{6,22},{7,23},{8,24},{9,... | collective-permute-start | bytes 172040 | tf_op jit(solution)/shard_map/ppermute | solution.py:615
  285.8 6.8 %collective-permute-start.13 = (f32[248,128]{1,0:T(8,128)S(1)}, f32[248,128]{1,0:T(8,128)S(1)}, u32[]{:S(2)}, u32[]{:S(2)}) collective-permute-start(f32[248,128]{1,0:T(8,128)S(1)} %pad_maximum_fusion.6), channel_id=1, source_target_pairs={{0,16},{1,17},{2,18},{3,19},{4,20},{5,21},{6,22},{7,23},{8,24},{9,... | collective-permute-start | bytes 380936 | tf_op jit(solution)/shard_map/ppermute | solution.py:615
  292.6 5.6 %collective-permute-start.14 = (f32[360,128]{1,0:T(8,128)S(1)}, f32[360,128]{1,0:T(8,128)S(1)}, u32[]{:S(2)}, u32[]{:S(2)}) collective-permute-start(f32[360,128]{1,0:T(8,128)S(1)} %pad_maximum_fusion.5), channel_id=1, source_target_pairs={{0,8},{1,9},{2,6},{3,7},{4,12},{5,13},{6,2},{7,3},{8,0},{9,1},{10,... | collective-permute-start | bytes 552968 | tf_op jit(solution)/shard_map/ppermute | solution.py:615
  292.7 19.9 %collective-permute-start.18 = (f32[2944,128]{1,0:T(8,128)S(1)}, f32[2944,128]{1,0:T(8,128)}, u32[]{:S(2)}, u32[]{:S(2)}) collective-permute-start(f32[2944,128]{1,0:T(8,128)S(1)} %maximum_select_fusion.2), channel_id=1, source_target_pairs={{0,4},{1,5},{2,3},{3,2},{4,0},{5,1},{6,7},{7,6},{8,12},{9,13},{10,... | collective-permute-start | bytes 4521992 | tf_op jit(solution)/shard_map/ppermute | solution.py:615
  298.3 10.1 %collective-permute-start.15 = (f32[584,128]{1,0:T(8,128)S(1)}, f32[584,128]{1,0:T(8,128)S(1)}, u32[]{:S(2)}, u32[]{:S(2)}) collective-permute-start(f32[584,128]{1,0:T(8,128)S(1)} %pad_maximum_fusion.4), channel_id=1, source_target_pairs={{0,1},{1,0},{2,10},{3,11},{4,5},{5,4},{6,14},{7,15},{8,9},{9,8},{1... | collective-permute-start | bytes 897032 | tf_op jit(solution)/shard_map/ppermute | solution.py:615
  299.0 13.6 %copy-start.3 = (f32[2944,128]{1,0:T(8,128)S(1)}, f32[2944,128]{1,0:T(8,128)}, u32[]{:S(2)}) copy-start(f32[2944,128]{1,0:T(8,128)} %copy-done.2) | copy-start | bytes 4521988
  308.6 9.6 %collective-permute-start.16 = (f32[1032,128]{1,0:T(8,128)S(1)}, f32[1032,128]{1,0:T(8,128)S(1)}, u32[]{:S(2)}, u32[]{:S(2)}) collective-permute-start(f32[1032,128]{1,0:T(8,128)S(1)} %pad_maximum_fusion.3), channel_id=1, source_target_pairs={{0,4},{1,5},{2,3},{3,2},{4,0},{5,1},{6,7},{7,6},{8,12},{9,13},{10,... | collective-permute-start | bytes 1585160 | tf_op jit(solution)/shard_map/ppermute | solution.py:615
  314.9 18.8 %collective-permute-start.19 = (f32[5888,128]{1,0:T(8,128)S(1)}, f32[5888,128]{1,0:T(8,128)}, u32[]{:S(2)}, u32[]{:S(2)}) collective-permute-start(f32[5888,128]{1,0:T(8,128)S(1)} %maximum_select_fusion.1), channel_id=1, source_target_pairs={{0,2},{1,3},{2,0},{3,1},{4,6},{5,7},{6,4},{7,5},{8,10},{9,11},{10,... | collective-permute-start | bytes 9043976 | tf_op jit(solution)/shard_map/ppermute | solution.py:615
  318.3 0.9 copy-start
  320.3 2.9 collective-permute-start.17
  324.7 1.5 copy-start.1
Sparse Core Ops, SparseCore 0:
  11.5 56.7 all-gather.2

commit v3 on v2

v3 whole, which is shorter than its diff:
```python
import functools

import jax
import jax.numpy as jnp
from jax import lax
from jax.experimental import pallas as pl
from jax.experimental.pallas import tpu as pltpu
from jax.sharding import PartitionSpec as P

HEADS = 6
EPSILON = 1e-05
PENALTY = 1.0
GELU_COEF = 0.7978845608028654
GELU_CUBE = 0.044715
LOG2E = 1.4426950408889634
LANES = 128
ROWS = 512
KEYS = 512
LIMIT = 56 * 2**20

low = jnp.bfloat16
full = jnp.float32


def mul(left, right, dims=((1,), (0,))):
    return lax.dot_general(left, right, (dims, ((), ())), preferred_element_type=full)


NT = ((1,), (1,))
TN = ((0,), (0,))


def params(count):
    return pltpu.CompilerParams(
        dimension_semantics=("arbitrary",) * count, vmem_limit_bytes=LIMIT
    )


def whole(shape):
    return pl.BlockSpec(shape, lambda *step: (0,) * len(shape))


SCALAR = pl.BlockSpec(memory_space=pltpu.SMEM)


def normalize(values):
    centre = jnp.mean(values, axis=-1, keepdims=True)
    centred = values - centre
    spread = jnp.mean(centred * centred, axis=-1, keepdims=True)
    scale = lax.rsqrt(spread + EPSILON)
    return centred * scale, scale


def norm_back(grad, unit, scale, gain):
    e = grad * gain
    first = jnp.mean(e, axis=-1, keepdims=True)
    second = jnp.mean(e * unit, axis=-1, keepdims=True)
    return scale * (e - first - unit * second)


def column_sum(values):
    return jnp.sum(values, axis=0, keepdims=True)


def project_kernel(
    lead, x, embed, gain, shift, weight, query_b, value_b, first, projected
):
    stream = x[...] + embed[pl.ds(lead[0], 1), :]
    unit, _ = normalize(stream)
    rounded = (unit * gain[...][None, :] + shift[...][None, :]).astype(low)
    first[...] = rounded.T
    features = x.shape[1]
    query_row = query_b[...][None, :]
    bias = jnp.concatenate(
        [query_row, jnp.zeros_like(query_row), value_b[...][None, :]], axis=1
    )
    projected[...] = (mul(rounded, weight[...]) + bias).astype(low)


def project(lead, x, embed, gain, shift, weight, query_b, value_b):
    rows, features = x.shape
    wide = weight.shape[1]
    tables = (embed, gain, shift, weight, query_b, value_b)
    return pl.pallas_call(
        project_kernel,
        grid=(rows // ROWS,),
        in_specs=[SCALAR, pl.BlockSpec((ROWS, features), lambda i: (i, 0))]
        + [whole(table.shape) for table in tables],
        out_specs=[
            pl.BlockSpec((features, ROWS), lambda i: (0, i)),
            pl.BlockSpec((ROWS, wide), lambda i: (i, 0)),
        ],
        out_shape=[
            jax.ShapeDtypeStruct((features, rows), low),
            jax.ShapeDtypeStruct((rows, wide), low),
        ],
        compiler_params=params(1),
        name="project",
    )(lead, x, *tables)


def attend_kernel(size, q, k, v, probs, mixed, inverse, turned):
    keys = k.shape[0]
    count = q.shape[0]
    scaling = size ** (-0.5) * LOG2E

    @pl.when(pl.program_id(1) == 0)
    def _():
        across = v[...].T
        tail = lax.broadcasted_iota(jnp.int32, (16, keys), 0)
        ones = jnp.where(tail == 0, 1.0, 0.0).astype(low)
        for head in range(2):
            turned[head, 0:size, :] = across[head * size : (head + 1) * size, :]
            turned[head, size : size + 16, :] = ones

    lane = lax.broadcasted_iota(jnp.int32, (1, LANES), 1)

    def scores(head, start):
        mask = jnp.where(lane // size == head, 1.0, 0.0).astype(low)
        return mul(k[start : start + keys, :], q[...] * mask, NT) * scaling

    def finish(head, total):
        spread = total[size : size + 1, :]
        inv = 1.0 / spread
        inverse[0, head : head + 1, :] = inv
        mixed[head * size : (head + 1) * size, :] = (total[0:size, :] * inv).astype(low)
        return spread

    extremes = []
    for head in range(2):
        total = jnp.zeros((size + 16, count), full)
        for start in (0,):
            p = jnp.exp2(scores(head, start)).astype(low)
            probs[0, head, start : start + keys, :] = p
            total = total + mul(turned[head, :, start : start + keys], p)
        spread = finish(head, total)
        extremes.append(spread)

    both = jnp.concatenate(extremes, axis=0)
    inside = jnp.where((both > 1e-18) & (both < 1e18), 1.0, 0.0)

    @pl.when(jnp.min(inside) < 0.5)
    def _():
        for head in range(2):
            top = jnp.full((1, count), -jnp.inf, full)
            for start in (0,):
                top = jnp.maximum(
                    top, jnp.max(scores(head, start), axis=0, keepdims=True)
                )
            total = jnp.zeros((size + 16, count), full)
            for start in (0,):
                p = jnp.exp2(scores(head, start) - top).astype(low)
                probs[0, head, start : start + keys, :] = p
                total = total + mul(turned[head, :, start : start + keys], p)
            finish(head, total)


def attend(projected):
    rows, wide = projected.shape
    features = wide // 3
    pairs = features // LANES
    size = features // HEADS
    return pl.pallas_call(
        functools.partial(attend_kernel, size),
        grid=(pairs, rows // ROWS),
        in_specs=[
            pl.BlockSpec((ROWS, LANES), lambda p, i: (i, p)),
            pl.BlockSpec((rows, LANES), lambda p, i: (0, pairs + p)),
            pl.BlockSpec((rows, LANES), lambda p, i: (0, 2 * pairs + p)),
        ],
        out_specs=[
            pl.BlockSpec((1, 2, rows, ROWS), lambda p, i: (p, 0, 0, i)),
            pl.BlockSpec((LANES, ROWS), lambda p, i: (p, i)),
            pl.BlockSpec((1, 8, ROWS), lambda p, i: (p, 0, i)),
        ],
        out_shape=[
            jax.ShapeDtypeStruct((pairs, 2, rows, rows), low),
            jax.ShapeDtypeStruct((features, rows), low),
            jax.ShapeDtypeStruct((pairs, 8, rows), full),
        ],
        scratch_shapes=[pltpu.VMEM((2, size + 16, rows), low)],
        compiler_params=params(2),
        name="attend",
    )(projected, projected, projected)


def middle_kernel(
    spans,
    size,
    group,
    side,
    lead,
    x,
    mixed,
    inverse,
    experts,
    upstream,
    embed,
    merge_w,
    merge_b,
    gain,
    shift,
    expand_w,
    expand_b,
    shrink_w,
    shrink_b,
    router_w,
    columns,
    blended,
    d_mid,
    d_across,
    d_down,
    keep,
    send,
    grads,
    lanes,
    sems,
):
    features = x.shape[1]
    step = x.shape[0]
    hidden_size = expand_w.shape[1]
    channels = upstream.shape[0]
    chunk = hidden_size // 2

    @pl.when(pl.program_id(0) == 0)
    def _():
        grads[...] = jnp.zeros_like(grads)
        lanes[...] = jnp.zeros_like(lanes)

    def add(name, values, part=0):
        half, base = spans[name]
        height = values.shape[0]
        for block in range(values.shape[1] // LANES):
            start = base + (part + block) * height
            grads[half, start : start + height, :] += values[
                :, block * LANES : (block + 1) * LANES
            ]

    stream = x[...] + embed[pl.ds(lead[0], 1), :]
    mid = stream + mul(mixed[...], merge_w[...], TN) + merge_b[...][None, :]
    unit, scale = normalize(mid)
    gain_row = gain[...][None, :]
    second = (unit * gain_row + shift[...][None, :]).astype(low)
    output = mid + shrink_b[...][None, :]
    bias = expand_b[...][None, :]
    hidden, slope = [], []
    for start in range(0, hidden_size, chunk):
        part = slice(start, start + chunk)
        u = mul(second, expand_w[:, part]) + bias[:, part]
        square = u * u
        t = jnp.tanh(u * (GELU_COEF + GELU_COEF * GELU_CUBE * square))
        half = 0.5 + 0.5 * t
        act = u * half
        slope.append(
            half
            + act
            * (1.0 - half)
            * (2.0 * GELU_COEF + 6.0 * GELU_COEF * GELU_CUBE * square)
        )
        act = act.astype(low)
        hidden.append(act)
        output = output + mul(act, shrink_w[part, :])
    output_low = output.astype(low)
    logits = mul(router_w[...], output_low, NT) + columns[:, 0:1]
    valid = lax.broadcasted_iota(jnp.int32, (group, 1), 0) < channels
    parts = [logits[e * group : (e + 1) * group, :] for e in range(3)]
    largest = jnp.maximum(jnp.maximum(parts[0], parts[1]), parts[2])
    parts = [part - largest for part in parts]
    raised = [jnp.exp(part) for part in parts]
    total = raised[0] + raised[1] + raised[2]
    shared = jnp.log(total)
    logs = [part - shared for part in parts]
    share = 1.0 / total
    gates = [value * share for value in raised]

    def widen(values):
        return jnp.concatenate(
            [values, jnp.zeros((group - channels, step), full)], axis=0
        )

    frames = [
        widen(experts[e * channels : (e + 1) * channels, :]) for e in range(3)
    ]
    up = widen(upstream[...])
    mix = gates[0] * frames[0] + gates[1] * frames[1] + gates[2] * frames[2]
    entropy = -(gates[0] * logs[0] + gates[1] * logs[1] + gates[2] * logs[2])
    blended[...] = mix[:channels, :] + columns[:channels, 1:2]
    d_parts = [
        jnp.where(
            valid,
            gates[e] * (up * (frames[e] - mix) - PENALTY * (logs[e] + entropy)),
            0.0,
        )
        for e in range(3)
    ]
    for index, values in enumerate(d_parts + [up]):
        for start in range(0, step, LANES):
            lanes[index * group : (index + 1) * group, :] += values[
                :, start : start + LANES
            ]
    d_logits_low = jnp.concatenate(d_parts, axis=0).astype(low)
    add("router", mul(d_logits_low, output_low))
    d_output = mul(d_logits_low, router_w[...], TN)
    add("shrink_bias", column_sum(d_output))
    d_output_low = d_output.astype(low)
    d_turned = d_output_low.T
    second_turned = second.T
    d_second = jnp.zeros_like(d_output)
    for index, start in enumerate(range(0, hidden_size, chunk)):
        part = slice(start, start + chunk)
        d_pre = mul(d_output_low, shrink_w[part, :], NT) * slope[index]
        add("expand_bias", column_sum(d_pre), start // LANES)
        d_pre_low = d_pre.astype(low)
        d_second = d_second + mul(d_pre_low, expand_w[:, part], NT)
        add("expand", mul(second_turned, d_pre_low), start // LANES)
        add("shrink", mul(d_turned, hidden[index]), start // LANES)
    add("second_gain", column_sum(d_second * unit))
    add("second_shift", column_sum(d_second))
    grad_mid = d_output + norm_back(d_second, unit, scale, gain_row)
    d_mid[...] = grad_mid
    add("merge_bias", column_sum(grad_mid))
    d_mid_low = grad_mid.astype(low)
    add("merge", mul(mixed[...], d_mid_low))
    d_mixed = mul(merge_w[...], d_mid_low, NT).astype(low).astype(full)
    row = lax.broadcasted_iota(jnp.int32, (size, step), 0)
    stack = []
    for head in range(features // size):
        span = slice(head * size, (head + 1) * size)
        odd = head % 2
        inv = inverse[head // 2, odd : odd + 1, :]
        scaled = (d_mixed[span, :] * inv).astype(low)
        stack.append(scaled)
        centre = -column_sum(scaled.astype(full) * mixed[span, :].astype(full))
        one = centre.astype(low).astype(full)
        two = (centre - one).astype(low).astype(full)
        extra = jnp.where(
            row == 0,
            one,
            jnp.where(row == 1, two, jnp.where(row == 2, centre - one - two, 0.0)),
        ).astype(low)
        d_across[head, odd * size : (odd + 1) * size, :] = scaled
        d_across[head, (1 - odd) * size : (2 - odd) * size, :] = extra
    d_down[...] = jnp.concatenate(stack, axis=0).T

    @pl.when(pl.program_id(0) == pl.num_programs(0) - 1)
    def _():
        sums = column_sum(lanes[...].T)
        width = sums.shape[1]
        wide = up_to(width, LANES)
        sums = jnp.concatenate([sums, jnp.zeros((1, wide - width), full)], axis=1)
        add("head", sums)
        copies = [
            pltpu.make_async_copy(grads.at[side[0]], keep, sems.at[0]),
            pltpu.make_async_copy(grads.at[1 - side[0]], send, sems.at[1]),
        ]
        for copy in copies:
            copy.start()
        for copy in copies:
            copy.wait()


def middle(spans, height, group, side, lead, x, mixed, inverse, experts, upstream, tables):
    rows, features = x.shape
    size = features // HEADS
    channels = upstream.shape[0]
    step = ROWS
    anywhere = pl.BlockSpec(memory_space=pl.ANY)
    return pl.pallas_call(
        functools.partial(middle_kernel, spans, size, group),
        grid=(rows // step,),
        in_specs=[
            SCALAR,
            SCALAR,
            pl.BlockSpec((step, features), lambda i: (i, 0)),
            pl.BlockSpec((features, step), lambda i: (0, i)),
            pl.BlockSpec((inverse.shape[0], 8, step), lambda i: (0, 0, i)),
            pl.BlockSpec((experts.shape[0], step), lambda i: (0, i)),
            pl.BlockSpec((channels, step), lambda i: (0, i)),
        ]
        + [whole(table.shape) for table in tables],
        out_specs=[
            pl.BlockSpec((channels, step), lambda i: (0, i)),
            pl.BlockSpec((step, features), lambda i: (i, 0)),
            pl.BlockSpec((HEADS, LANES, step), lambda i: (0, 0, i)),
            pl.BlockSpec((step, features), lambda i: (i, 0)),
            anywhere,
            anywhere,
        ],
        out_shape=[
            jax.ShapeDtypeStruct((channels, rows), full),
            jax.ShapeDtypeStruct((rows, features), full),
            jax.ShapeDtypeStruct((HEADS, LANES, rows), low),
            jax.ShapeDtypeStruct((rows, features), low),
            jax.ShapeDtypeStruct((height, LANES), full),
            jax.ShapeDtypeStruct((height, LANES), full),
        ],
        scratch_shapes=[
            pltpu.VMEM((2, height, LANES), full),
            pltpu.VMEM((4 * group, LANES), full),
            pltpu.SemaphoreType.DMA((2,)),
        ],
        compiler_params=params(1),
        name="middle",
    )(side, lead, x, mixed, inverse, experts, upstream, *tables)


def attend_back_kernel(size, first_part, last_part, *refs):
    if first_part:
        q, k, v, d_across, d_down, probs, d_query, d_pair = refs[:8]
    else:
        q, k, v, d_across, d_down, probs, carry, _, d_query, d_pair = refs[:10]
    total = refs[-1] if last_part else d_query
    step = pl.program_id(0)
    rows = q.shape[0]
    block = k.shape[0]
    scaling = size ** (-0.5)
    lane = lax.broadcasted_iota(jnp.int32, (1, LANES), 1)

    @pl.when(step == 0)
    def _():
        total[...] = jnp.zeros_like(total) if first_part else carry[...]

    k_across = k[...].T
    d_keys, d_values = [], []
    for head in range(2):
        base = (1 - head) * size
        data = jnp.where(lane // size == head, 1.0, 0.0).astype(low)
        ones = jnp.where((lane >= base) & (lane < base + 3), 1.0, 0.0).astype(low)
        values = v[...] * data + ones
        d_k = jnp.zeros((block, LANES), full)
        d_v = jnp.zeros((block, LANES), full)
        for start in (0,):
            span = slice(start, start + rows)
            p = probs[0, head, :, span]
            d_p = mul(values, d_across[head, :, span])
            d_s = (p.astype(full) * d_p).astype(low)
            total[head * size : (head + 1) * size, span] += mul(
                k_across[head * size : (head + 1) * size, :], d_s
            )
            d_v = d_v + mul(p, d_down[span, :])
            d_k = d_k + mul(d_s, q[span, :])
        d_keys.append(d_k)
        d_values.append(d_v)
    d_pair[0] = (jnp.where(lane < size, *d_keys) * scaling).astype(low)
    d_pair[1] = jnp.where(lane < size, *d_values).astype(low)

    if last_part:

        @pl.when(step == pl.num_programs(0) - 1)
        def _():
            d_query[...] = (total[...].T * scaling).astype(low)


def attend_back(pair, base, steps, projected, d_across, d_down, probs, carried):
    rows, wide = projected.shape
    features = wide // 3
    pairs = features // LANES
    size = features // HEADS
    total = rows // KEYS
    first_part, last_part = base == 0, base + steps == total
    across = (rows, LANES) if last_part else (LANES, rows)
    return pl.pallas_call(
        functools.partial(attend_back_kernel, size, first_part, last_part),
        grid=(steps,),
        in_specs=[
            pl.BlockSpec((rows, LANES), lambda i: (0, pair)),
            pl.BlockSpec((KEYS, LANES), lambda i: (base + i, pairs + pair)),
            pl.BlockSpec((KEYS, LANES), lambda i: (base + i, 2 * pairs + pair)),
            pl.BlockSpec((2, LANES, rows), lambda i: (pair, 0, 0)),
            pl.BlockSpec((rows, LANES), lambda i: (0, pair)),
            pl.BlockSpec((1, 2, KEYS, rows), lambda i: (pair, 0, base + i, 0)),
        ]
        + ([] if first_part else [whole((LANES, rows)), pl.BlockSpec(memory_space=pl.ANY)]),
        out_specs=[
            whole(across),
            pl.BlockSpec((2, KEYS, LANES), lambda i: (0, base + i, 0)),
        ],
        out_shape=[
            jax.ShapeDtypeStruct(across, low if last_part else full),
            jax.ShapeDtypeStruct((2, rows, LANES), low),
        ],
        scratch_shapes=[pltpu.VMEM((LANES, rows), full)] if last_part else [],
        input_output_aliases={} if first_part else {7: 1},
        compiler_params=params(1),
        cost_estimate=pl.CostEstimate(
            flops=10 * rows * rows * 256 * steps // total,
            bytes_accessed=rows * rows * 4 * steps // total,
            transcendentals=0,
        ),
        name="attend_back",
    )(projected, projected, projected, d_across, d_down, probs, *carried)


def weigh_kernel(pairs, places, side, weight, first, *refs):
    d_query, d_pair = refs[:pairs], refs[pairs : 2 * pairs]
    keep, send, sums, grads, sems = refs[2 * pairs :]
    features = first.shape[0]
    grads[...] = jnp.zeros_like(grads)
    sums[...] = jnp.zeros_like(sums)
    parts = []
    for kind in range(3):
        for pair in range(pairs):
            values = d_query[pair][...] if kind == 0 else d_pair[pair][kind - 1]
            parts.append(values)
            if kind != 1:
                sums[
                    kind // 2 : kind // 2 + 1, pair * LANES : (pair + 1) * LANES
                ] = weight[0] * column_sum(values.astype(full))
    for start in range(0, len(parts), 2):
        some = parts[start : start + 2]
        product = mul(first[...], jnp.concatenate(some, axis=1)) * weight[0]
        for index in range(len(some)):
            half, base = places[start + index]
            grads[half, base : base + features, :] = product[
                :, index * LANES : (index + 1) * LANES
            ]
    copies = [
        pltpu.make_async_copy(grads.at[side[0]], keep, sems.at[0]),
        pltpu.make_async_copy(grads.at[1 - side[0]], send, sems.at[1]),
    ]
    for copy in copies:
        copy.start()
    for copy in copies:
        copy.wait()


def weigh(places, height, side, weight, first, d_query, d_pair):
    features = first.shape[0]
    vmem = pl.BlockSpec(memory_space=pltpu.VMEM)
    anywhere = pl.BlockSpec(memory_space=pl.ANY)
    pairs = len(d_query)
    return pl.pallas_call(
        functools.partial(weigh_kernel, pairs, places),
        in_specs=[SCALAR, SCALAR, vmem] + [vmem] * (2 * pairs),
        out_specs=[anywhere, anywhere, vmem],
        out_shape=[
            jax.ShapeDtypeStruct((height, LANES), full),
            jax.ShapeDtypeStruct((height, LANES), full),
            jax.ShapeDtypeStruct((8, features), full),
        ],
        scratch_shapes=[
            pltpu.VMEM((2, height, LANES), full),
            pltpu.SemaphoreType.DMA((2,)),
        ],
        compiler_params=pltpu.CompilerParams(vmem_limit_bytes=LIMIT),
        cost_estimate=pl.CostEstimate(
            flops=18 * d_query[0].shape[0] * features * features,
            bytes_accessed=d_query[0].shape[0] * features * 8,
            transcendentals=0,
        ),
        name="weigh",
    )(side, weight, first, *d_query, *d_pair)


def finish_kernel(pairs, last_part, lead, weight, x, embed, gain, wide, d_mid, *rest):
    d_query, d_pair, rest = rest[:pairs], rest[pairs : 2 * pairs], rest[2 * pairs :]
    if last_part:
        earlier, biases, _, grad_input, vectors, sums = rest
    else:
        grad_input, sums = rest
    step = pl.program_id(0)

    @pl.when(step == 0)
    def _():
        sums[...] = earlier[...] if last_part else jnp.zeros_like(sums)

    stream = x[...] + embed[pl.ds(lead[0], 1), :]
    unit, scale = normalize(stream)
    parts = []
    for kind in range(3):
        for pair in range(pairs):
            parts.append(d_query[pair][...] if kind == 0 else d_pair[pair][kind - 1])
    d_first = mul(jnp.concatenate(parts, axis=1), wide[...], NT)
    d_stream = (
        d_mid[...] + norm_back(d_first, unit, scale, gain[...][None, :])
    ) * weight[0]
    grad_input[...] = d_stream
    sums[0:1, :] += column_sum(d_first * unit) * weight[0]
    sums[1:2, :] += column_sum(d_first) * weight[0]
    sums[2:3, :] += column_sum(d_stream)

    if last_part:

        @pl.when(step == pl.num_programs(0) - 1)
        def _():
            vectors[...] = jnp.zeros_like(vectors)
            for block in range(pairs):
                lanes = slice(block * LANES, (block + 1) * LANES)
                for index, ref in enumerate((sums, sums, biases, biases)):
                    at = index * pairs + block
                    vectors[at : at + 1, :] = ref[index % 2 : index % 2 + 1, lanes]
                vectors[pl.ds((4 + lead[0]) * pairs + block, 1), :] = sums[2:3, lanes]


def finish(base, steps, lead, weight, x, embed, gain, wide, d_mid, d_query, d_pair, carried):
    rows, features = x.shape
    pairs = len(d_query)
    total = rows // ROWS
    last_part = base + steps == total
    height = up_to((4 + embed.shape[0]) * pairs, 8)
    row_spec = pl.BlockSpec((ROWS, features), lambda i: (base + i, 0))
    small = pl.BlockSpec((8, features), lambda i: (0, 0))
    return pl.pallas_call(
        functools.partial(finish_kernel, pairs, last_part),
        grid=(steps,),
        in_specs=[
            SCALAR,
            SCALAR,
            row_spec,
            whole(embed.shape),
            whole(gain.shape),
            whole(wide.shape),
            row_spec,
        ]
        + [pl.BlockSpec((ROWS, LANES), lambda i: (base + i, 0))] * pairs
        + [pl.BlockSpec((2, ROWS, LANES), lambda i: (0, base + i, 0))] * pairs
        + ([small, small, pl.BlockSpec(memory_space=pl.ANY)] if last_part else []),
        out_specs=[row_spec, whole((height, LANES)) if last_part else small],
        out_shape=[
            jax.ShapeDtypeStruct((rows, features), full),
            jax.ShapeDtypeStruct((height, LANES) if last_part else (8, features), full),
        ],
        scratch_shapes=[pltpu.VMEM((8, features), full)] if last_part else [],
        input_output_aliases={9 + 2 * pairs: 0} if last_part else {},
        compiler_params=params(1),
        cost_estimate=pl.CostEstimate(
            flops=6 * rows * features * features * steps // total,
            bytes_accessed=rows * features * 18 * steps // total,
            transcendentals=0,
        ),
        name="finish",
    )(lead, weight, x, embed, gain, wide, d_mid, *d_query, *d_pair, *carried)


def unpack_kernel(spans, group, channels, places, *refs):
    pieces = refs[:4]
    expand, shrink, merge, router, vectors, grads, sems = refs[4:]
    quarter = pieces[0].shape[0]
    height = 2 * quarter
    arrivals = [
        pltpu.make_async_copy(
            pieces[n], grads.at[pl.ds(places[n] * quarter, quarter)], sems.at[n]
        )
        for n in range(4)
    ]
    for copy in arrivals:
        copy.start()
    for copy in arrivals:
        copy.wait()

    def block(name, rows, index):
        half, base = spans[name]
        start = half * height + base + index * rows
        return grads.at[pl.ds(start, rows)]

    features, hidden = expand.shape
    leaving = []
    for target, name in ((expand, "expand"), (merge, "merge")):
        for index in range(target.shape[1] // LANES):
            leaving.append(
                pltpu.make_async_copy(
                    block(name, features, index),
                    target.at[:, pl.ds(index * LANES, LANES)],
                    sems.at[4 + len(leaving)],
                )
            )
    for copy in leaving:
        copy.start()
    for index in range(hidden // LANES):
        shrink[index * LANES : (index + 1) * LANES, :] = block("shrink", features, index)[
            ...
        ].T
    rows = 3 * group
    for index in range(features // LANES):
        values = block("router", rows, index)
        for e in range(3):
            router[
                e * channels : (e + 1) * channels, index * LANES : (index + 1) * LANES
            ] = values[e * group : e * group + channels, :]
    vectors[...] = block("expand_bias", vectors.shape[0], 0)[...]
    for copy in leaving:
        copy.wait()


def unpack(spans, group, channels, features, hidden, tall, places, pieces):
    vmem = pl.BlockSpec(memory_space=pltpu.VMEM)
    anywhere = pl.BlockSpec(memory_space=pl.ANY)
    quarter = pieces[0].shape[0]
    return pl.pallas_call(
        functools.partial(unpack_kernel, spans, group, channels),
        in_specs=[SCALAR] + [anywhere] * 4,
        out_specs=[anywhere, vmem, anywhere, vmem, vmem],
        out_shape=[
            jax.ShapeDtypeStruct((features, hidden), full),
            jax.ShapeDtypeStruct((hidden, features), full),
            jax.ShapeDtypeStruct((features, features), full),
            jax.ShapeDtypeStruct((3 * channels, features), full),
            jax.ShapeDtypeStruct((tall, LANES), full),
        ],
        scratch_shapes=[
            pltpu.VMEM((4 * quarter, LANES), full),
            pltpu.SemaphoreType.DMA((4 + (hidden + features) // LANES,)),
        ],
        compiler_params=pltpu.CompilerParams(vmem_limit_bytes=LIMIT),
        cost_estimate=pl.CostEstimate(
            flops=8 * 10**9, bytes_accessed=quarter * 8192, transcendentals=0
        ),
        name="unpack",
    )(places, *pieces)


def join_kernel(shared, side, mine, got, out):
    height = mine.shape[0] - shared
    out[:shared, :] = mine[:shared, :] + got[:shared, :]
    left = pl.multiple_of(shared + side[0] * height, 8)
    right = pl.multiple_of(shared + (1 - side[0]) * height, 8)
    out[pl.ds(left, height), :] = mine[shared:, :]
    out[pl.ds(right, height), :] = got[shared:, :]


def join(shared, side, mine, got):
    vmem = pl.BlockSpec(memory_space=pltpu.VMEM)
    height = 2 * mine.shape[0] - shared
    return pl.pallas_call(
        functools.partial(join_kernel, shared),
        in_specs=[SCALAR, vmem, vmem],
        out_specs=vmem,
        out_shape=jax.ShapeDtypeStruct((height, LANES), full),
        compiler_params=pltpu.CompilerParams(vmem_limit_bytes=LIMIT),
        name="join",
    )(side, mine, got)


def settle_kernel(places, side, mine, got, attend, embed, vectors, grads, sums, sems):
    shared = sums.shape[0]
    height = mine.shape[0] - shared
    features = attend.shape[0]
    leads = embed.shape[0]
    pairs = features // LANES
    arrivals = [
        pltpu.make_async_copy(
            mine.at[pl.ds(shared, height)], grads.at[side[0]], sems.at[0]
        ),
        pltpu.make_async_copy(
            got.at[pl.ds(shared, height)], grads.at[1 - side[0]], sems.at[1]
        ),
    ]
    for copy in arrivals:
        copy.start()
    sums[...] = mine[:shared, :] + got[:shared, :]
    vectors[...] = sums[: vectors.shape[0], :]
    for block in range(pairs):
        embed[:, block * LANES : (block + 1) * LANES] = sums[
            pl.ds(4 * pairs + block, leads, stride=pairs), :
        ]
    for copy in arrivals:
        copy.wait()
    leaving = []
    for index, (half, base) in enumerate(places):
        leaving.append(
            pltpu.make_async_copy(
                grads.at[half, pl.ds(base, features)],
                attend.at[:, pl.ds(index * LANES, LANES)],
                sems.at[2 + index],
            )
        )
    for copy in leaving:
        copy.start()
    for copy in leaving:
        copy.wait()


def settle(places, shared, leads, features, side, mine, got):
    vmem = pl.BlockSpec(memory_space=pltpu.VMEM)
    height = mine.shape[0] - shared
    return pl.pallas_call(
        functools.partial(settle_kernel, places),
        in_specs=[SCALAR, vmem, vmem],
        out_specs=[pl.BlockSpec(memory_space=pl.ANY), vmem, vmem],
        out_shape=[
            jax.ShapeDtypeStruct((features, 3 * features), full),
            jax.ShapeDtypeStruct((leads, features), full),
            jax.ShapeDtypeStruct((up_to(4 * features // LANES, 8), LANES), full),
        ],
        scratch_shapes=[
            pltpu.VMEM((2, height, LANES), full),
            pltpu.VMEM((shared, LANES), full),
            pltpu.SemaphoreType.DMA((2 + len(places),)),
        ],
        compiler_params=pltpu.CompilerParams(vmem_limit_bytes=LIMIT),
        name="settle",
    )(side, mine, got)


def up_to(value, step):
    return -(-value // step) * step


def tie(value, *others):
    return lax.optimization_barrier((value,) + others)[0]


def routes(sizes):
    inner = sizes["rep"]
    outer = sizes["dp"]
    if outer % 2:
        return 0, ((), ())
    far = [inner << n for n in range(1, outer.bit_length() - 1)]
    near = [1 << n for n in range(inner.bit_length() - 1)]
    even = []
    for n in range(max(len(far), len(near))):
        even += far[n : n + 1] + near[n : n + 1]
    odd = even[1:3] + even[:1] + even[3:]
    return inner, (tuple(even), tuple(odd))


class Ring:
    def __init__(self, sizes):
        self.count = sizes["dp"] * sizes["rep"]
        self.core_bit, self.orders = routes(sizes)
        self.hops = len(self.orders[0]) + 1 if self.core_bit else 0
        self.index = lax.axis_index(("dp", "rep"))

    def bits(self, hop):
        if hop == 0:
            return self.core_bit, self.core_bit
        return self.orders[0][hop - 1], self.orders[1][hop - 1]

    def swap(self, values, hop):
        pair = self.bits(hop)
        moves = [
            (i, i ^ pair[(i // self.core_bit) % 2]) for i in range(self.count)
        ]
        return lax.ppermute(values, ("dp", "rep"), moves)

    def side(self, hop, partner=False):
        if not self.hops:
            return jnp.int32(0)
        even, odd = self.bits(hop)
        if partner:
            even, odd = odd, even
        bit = even
        if even != odd:
            bit = jnp.where(self.index & self.core_bit == 0, even, odd)
        return jnp.where(self.index & bit == 0, 0, 1)

    def scatter(self, keep, send, factors=(None, None)):
        got = self.swap(send, 0)
        beside = yield send
        got = got if beside is None else tie(got, beside)
        terms = [[keep, 0, factors[0]], [got, 0, factors[1]]]
        length = keep.shape[0]

        def region(start, size):
            total = None
            for values, offset, factor in terms:
                part = lax.dynamic_slice_in_dim(values, offset + start, size, 0)
                part = part if factor is None else part * factor
                total = part if total is None else total + part
            return total

        for hop in range(1, self.hops):
            length //= 2
            side = self.side(hop)
            send = region((1 - side) * length, length)
            got = self.swap(send, hop)
            for term in terms:
                term[1] = term[1] + side * length
            beside = yield send
            terms.append([got if beside is None else tie(got, beside), 0, None])
        return region(0, length)

    def gather(self, values):
        for hop in reversed(range(2, self.hops)):
            got = self.swap(values, hop)
            beside = yield values
            if beside is not None:
                got = tie(got, beside)
            values = jnp.where(
                self.side(hop) == 0,
                jnp.concatenate([values, got]),
                jnp.concatenate([got, values]),
            )
        got = self.swap(values, 1)
        across = self.swap(values, 0)
        beside = yield values
        if beside is not None:
            got, across = tie(got, beside), tie(across, beside)
        final = self.swap(got, 0)
        beside = yield got
        if beside is not None:
            final = tie(final, beside)
        core, near, far = self.side(0), self.side(1), self.side(1, partner=True)
        places = jnp.stack(
            [
                2 * core + near,
                2 * core + 1 - near,
                2 * (1 - core) + far,
                2 * (1 - core) + 1 - far,
            ]
        )
        return places, (values, got, across, final)


class Flow:
    def __init__(self, steps):
        self.steps = steps
        self.done = False
        self.sent = None
        self.result = None
        self.push(None)

    def push(self, beside):
        if self.done:
            return
        try:
            self.sent = self.steps.send(beside)
        except StopIteration as stop:
            self.done, self.sent, self.result = True, None, stop.value

    def drain(self):
        while not self.done:
            self.push(None)
        return self.result


def total_of(ring, keep, send, factors):
    part = yield from ring.scatter(keep, send, factors)
    return (yield from ring.gather(part))


def body(sizes, *args):
    (
        block_input,
        expert_out,
        upstream,
        lead_index,
        lead_frames,
        lead_embed,
        first_gain,
        first_shift,
        attend_weight,
        query_bias,
        value_bias,
        merge_weight,
        merge_bias,
        second_gain,
        second_shift,
        expand_weight,
        expand_bias,
        shrink_weight,
        shrink_bias,
        router_weight,
        router_bias,
        correction,
    ) = args
    rows, features = block_input.shape
    channels = correction.shape[0]
    leads = lead_embed.shape[0]
    hidden = expand_bias.shape[0]
    devices = sizes["dp"] * sizes["rep"]
    pairs = features // LANES
    grain = 4 * devices
    ring = Ring(sizes)
    core = ring.side(0).reshape(1)

    tall = max(8, 2048 // devices)
    mine = lead_index[0].astype(full)
    leads_seen = lax.optimization_barrier(
        lax.all_gather(
            lax.optimization_barrier(jnp.full((tall, LANES), mine)), ("dp", "rep")
        )
    )[:, 0, 0]
    table = lead_frames.astype(full)

    def weight_of(lead):
        count = jnp.sum((leads_seen == lead).astype(full))
        chosen = jnp.sum(
            jnp.where(jnp.arange(leads, dtype=jnp.int32).astype(full) == lead, table, 0.0)
        )
        return chosen * devices / (count * jnp.sum(table))

    scale = weight_of(mine)
    other = scale
    if ring.hops:
        position = ring.index ^ ring.core_bit
        other = weight_of(
            jnp.sum(jnp.where(jnp.arange(devices) == position, leads_seen, 0.0))
        )
    weight = scale.reshape(1)

    first, projected = project(
        lead_index,
        block_input,
        lead_embed,
        first_gain,
        first_shift,
        attend_weight,
        query_bias,
        value_bias,
    )
    probs, mixed, inverse = attend(projected)

    group = up_to(channels, 16)
    spans, heights = {}, [0, 0]
    for name, half, height in (
        ("expand", 0, features * hidden // LANES),
        ("merge", 0, features * features // LANES),
        ("shrink", 1, features * hidden // LANES),
        ("router", 1, features * 3 * group // LANES),
        ("expand_bias", 1, hidden // LANES),
        ("shrink_bias", 1, pairs),
        ("merge_bias", 1, pairs),
        ("second_gain", 1, pairs),
        ("second_shift", 1, pairs),
        ("head", 1, up_to(4 * group, LANES) // LANES),
    ):
        spans[name] = (half, heights[half])
        heights[half] += height
    vector_rows = up_to(heights[1] - spans["expand_bias"][1], 8)
    height = up_to(max(heights[0], spans["expand_bias"][1] + vector_rows), grain)
    wide_router = jnp.pad(
        router_weight.T.reshape(3, channels, features),
        ((0, 0), (0, group - channels), (0, 0)),
    ).reshape(3 * group, features)
    columns = jnp.stack(
        [
            jnp.pad(
                router_bias.reshape(3, channels), ((0, 0), (0, group - channels))
            ).reshape(-1),
            jnp.pad(correction, (0, 3 * group - channels)),
        ],
        axis=1,
    )
    tables = (
        lead_embed,
        merge_weight,
        merge_bias,
        second_gain,
        second_shift,
        expand_weight,
        expand_bias,
        shrink_weight,
        shrink_bias,
        wide_router,
        columns,
    )
    blended, d_mid, d_across, d_down, keep, send = middle(
        spans,
        height,
        group,
        core,
        lead_index,
        block_input,
        mixed,
        inverse,
        expert_out.T,
        upstream.T,
        tables,
    )
    flow = None
    if ring.hops:
        flow = Flow(total_of(ring, keep, tie(send, leads_seen), (scale, other)))
    plan = ((1, 2, 1), (1, 1, 1, 1), (1, 2, 1))
    d_query, d_pair = [], []
    for pair in range(pairs):
        carried = ()
        base = 0
        for steps in plan[pair]:
            now = d_down if flow is None or flow.done else tie(d_down, flow.sent)
            carried = attend_back(
                pair, base, steps, projected, d_across, now, probs, carried
            )
            base += steps
            if flow is not None:
                flow.push(carried[0])
        d_query.append(carried[0])
        d_pair.append(carried[1])
    places = tuple(
        (n // 5, (n % 5) * features) for n in range(3 * pairs)
    )
    tail_height = up_to(5 * features, grain)
    now = weight if flow is None else tie(weight, flow.drain()[1][3])
    tail_keep, tail_send, biases = weigh(
        places, tail_height, core, now, first, d_query, d_pair
    )
    late = None
    if ring.hops:
        late = Flow(ring.scatter(tail_keep, tail_send))
    carried = ()
    base = 0
    for steps in (2, 2):
        now = weight if late is None else tie(weight, late.sent)
        grad_input, sums = finish(
            base,
            steps,
            lead_index,
            now,
            block_input,
            lead_embed,
            first_gain,
            attend_weight,
            d_mid,
            d_query,
            d_pair,
            carried,
        )
        base += steps
        carried = (sums, biases, grad_input)
        if late is not None:
            late.push(sums)
    shared = sums.shape[0]
    if ring.hops:
        where, pieces = flow.result
        where = tie(where, late.sent)
    else:
        where = jnp.arange(4, dtype=jnp.int32)
        pieces = [
            half[start : start + height // 2] * scale
            for half in (keep, send)
            for start in (0, height // 2)
        ]
    grad_expand, grad_shrink, grad_merge, grad_router, vectors = unpack(
        spans, group, channels, features, hidden, vector_rows, where, pieces
    )
    first_vector = spans["expand_bias"][1]

    def take(name, length):
        start = spans[name][1] - first_vector
        return vectors[start : start + length // LANES].reshape(-1)

    head = take("head", up_to(4 * group, LANES))
    middle_vectors = (
        take("merge_bias", features),
        take("second_gain", features),
        take("second_shift", features),
        take("expand_bias", hidden),
        take("shrink_bias", features),
        head[: 3 * group].reshape(3, group)[:, :channels].reshape(-1),
        head[3 * group : 3 * group + channels],
    )
    if ring.hops:
        late.push(vectors)
        piece = jnp.concatenate([sums, late.drain()])
        for hop in reversed(range(1, ring.hops)):
            got = ring.swap(piece, hop)
            piece = join(shared, ring.side(hop).reshape(1), piece, got)
        got = ring.swap(piece, 0)
    else:
        piece = jnp.concatenate([sums, tail_keep])
        got = jnp.concatenate([jnp.zeros_like(sums), tail_send])
    grad_attend, grad_embed, small = settle(
        places, shared, leads, features, core, piece, got
    )
    small = small[: 4 * pairs].reshape(4, features)
    merge_b, gain_b, shift_b, expand_b, shrink_b, router_b, correct = middle_vectors
    return (
        blended.T,
        grad_input,
        grad_embed,
        small[0],
        small[1],
        grad_attend,
        small[2],
        small[3],
        grad_merge,
        merge_b,
        gain_b,
        shift_b,
        grad_expand,
        expand_b,
        grad_shrink,
        shrink_b,
        grad_router.T,
        router_b,
        correct,
    )


def solution(mesh):
    split = P(("dp", "rep"), None)
    sizes = dict(mesh.shape)
    return jax.shard_map(
        functools.partial(body, sizes),
        mesh=mesh,
        in_specs=(split, split, split, P(("dp", "rep"))) + (P(),) * 18,
        out_specs=(split, split) + (P(),) * 17,
        check_vma=False,
    )
```

time: 368 us -> 335 us (0.910)
  local copies, waits for them, and re-layouts: 44.5 us -> 11.3 us
  other arithmetic: 23.4 us -> 17.8 us
    reshape x17 -> x5, local copies, waits for them, and re-layouts: 15.9 us -> 1.97 us  [the longest x2 1.19 us: take(): return vectors[start:start + length // LANES].reshape(-1)]
    unnamed x48 -> x34, local copies, waits for them, and re-layouts: 17.8 us -> 3.9 us
    select_n x10 -> x3, other arithmetic: 10.8 us -> 0.25 us  [gather(): jnp.where(self.side(hop) == 0, jnp.concatenate([values, got]), jnp.concat...]
    add x15 -> x10, other arithmetic: 5.89 us -> 13.8 us  [region(): total = part if total is None else total + part]
    pallas_call x6 -> x10, Pallas kernels: 83.4 us -> 90.6 us  [attend_back(): pl.pallas_call(functools.partial(attend_back_kernel, size, first_part, la...]
    pallas_call x1, Pallas kernels: 37 us -> 30 us  [attend(): pl.pallas_call(functools.partial(attend_kernel, size), grid=(pairs, rows...]
    slice x11 -> x3, local copies, waits for them, and re-layouts: 5.62 us -> 1.81 us  [the longest x1 1.23 us: body(): lax.optimization_barrier(lax.all_gather(lax.optimization_barrier(jnp.full...]
    pallas_call x3 -> x9, Pallas kernels: 66.5 us -> 69.9 us  [the longest x1 36.8 us: middle(): pl.pallas_call(functools.partial(middle_kernel, spans, size, group), grid...]
  transfers between devices with their start and end apart: 21 -> 22, of which waited for: 12 -> 13; matrix products, arithmetic and copies ran while one was open for 8% -> 3% of each run, Pallas kernels for 53% -> 55%
where the time goes in v3:
time: 335 us; the launch traced here: 329 us
  Pallas kernels  201 us (60%)
  waiting for transfers between devices  56.5 us (17%)
  starting transfers between devices  22.7 us (7%)
  between operations  19.2 us (6%)
  other arithmetic  17.8 us (5%)
  local copies, waits for them, and re-layouts  11.3 us (3%)
    pallas_call x10, Pallas kernels, attend_back(): pl.pallas_call(functools.partial(attend_back_kernel, size, first_part, la...  90.6 us
    ppermute x21, waiting for transfers between devices, swap(): return lax.ppermute(values, ('dp', 'rep'), moves)  56.4 us
    pallas_call x1, Pallas kernels, middle(): pl.pallas_call(functools.partial(middle_kernel, spans, size, group), grid...  36.8 us
    pallas_call x1, Pallas kernels, attend(): pl.pallas_call(functools.partial(attend_kernel, size), grid=(pairs, rows...  30 us
    ppermute x21, starting transfers between devices, swap(): return lax.ppermute(values, ('dp', 'rep'), moves)  22.7 us
    add x10, other arithmetic, region(): total = part if total is None else total + part  13.8 us
    pallas_call x2, Pallas kernels, finish(): pl.pallas_call(functools.partial(finish_kernel, pairs, last_part), grid=(...  10.7 us
    pallas_call x4, Pallas kernels, join(): pl.pallas_call(functools.partial(join_kernel, shared), in_specs=[SCALAR,...  7.64 us
  transfers between devices with their start and end apart: 22, of which 13 were waited for; matrix products, arithmetic and copies ran while one was open for 3% of the time, Pallas kernels for 55%

profile of v3, /device:TPU:0, one launch (start us, length us, event | category | flops | bytes accessed | tf_op | source)
XLA Modules:
  0.0 328.7 jit_solution(17949006520521812631)
XLA Ops:
  8.5 7.4 %project.1 = (bf16[384,2048]{1,0:T(8,128)(2,1)}, bf16[2048,1152]{1,0:T(8,128)(2,1)}) custom-call(s32[1]{0:T(128)S(6)} %copy.62.lead, f32[2048,384]{1,0:T(8,128)} %x.13, f32[40,384]{1,0:T(8,128)} %embed.7, f32[384]{0:T(512)} %gain.7, f32[384]{0:T(512)} %shift.2, bf16[384,1152]{1,0:T(8,128)(2,1)} %wide.3, f32[384]{0:T(512)} %query_b.1, f32[384]{0:T(512)} %value_b.1), custom_call_target="tpu_custom_call" | custom-call | tf_op jit(solution)/shard_map/project/pallas_call | solution.py:84
  15.9 30.0 %attend.1 = (bf16[3,2,2048,2048]{3,2,1,0:T(8,128)(2,1)}, bf16[384,2048]{1,0:T(8,128)(2,1)}, f32[3,8,2048]{2,1,0:T(8,128)}) custom-call(bf16[2048,1152]{1,0:T(8,128)(2,1)} %get-tuple-element.94.q.k.v.refs_0_.refs_1_.refs_2_, bf16[2048,1152]{1,0:T(8,128)(2,1)} %get-tuple-element.94.q.k.v.refs_0_.refs_1_.refs_2_, ...), custom_call_target="tpu_custom_call" | custom-call | tf_op jit(solution)/shard_map/attend/pallas_call | solution.py:163
  46.2 0.8 copy.53.columns
  47.0 0.7 pad.12
  47.7 36.8 %middle.1 = (f32[69,2048]{1,0:T(8,128)}, f32[2048,384]{1,0:T(8,128)}, bf16[6,128,2048]{2,1,0:T(8,128)(2,1)}, bf16[2048,384]{1,0:T(8,128)(2,1)}, f32[5760,128]{1,0:T(8,128)}, /*index=5*/f32[5760,128]{1,0:T(8,128)}) custom-call(s32[1]{0:T(128)} %bitcast.side, s32[1]{0:T(128)S(6)} %copy.62.lead, f32[2048,384]{1,0:T(8,128)} %x.13, ...), custom_call_target="tpu_custom_call" | custom-call | tf_op jit(solution)/shard_map/middle/pallas_call | solution.py:368
  84.5 1.2 slice_reduce_fusion
  86.8 1.2 fusion.4
  88.0 1.3 fusion.3
  93.3 8.0 %attend_back.10 = (f32[128,2048]{1,0:T(8,128)}, bf16[2,2048,128]{2,1,0:T(8,128)(2,1)}) custom-call(bf16[2048,1152]{1,0:T(8,128)(2,1)} %get-tuple-element.94.q.k.v.refs_0_.refs_1_.refs_2_, bf16[2048,1152]{1,0:T(8,128)(2,1)} %get-tuple-element.94.q.k.v.refs_0_.refs_1_.refs_2_, bf16[2048,1152]{1,0:T(8,128)(2,1)} %get-tuple-element.94.q.k.v.refs_0_.refs_1_.refs_2_, ...), custom_call_target="tpu_custom_call" | custom-call | flops 2684354560 | bytes 4194304 | tf_op jit(solution)/shard_map/attend_back/pallas_call | solution.py:462
  101.3 2.6 multiply_add_fusion
  103.9 2.5 collective-permute-start.1
  106.4 12.8 %attend_back.11 = (f32[128,2048]{1,0:T(8,128)}, bf16[2,2048,128]{2,1,0:T(8,128)(2,1)}) custom-call(bf16[2048,1152]{1,0:T(8,128)(2,1)} %get-tuple-element.94.q.k.v.refs_0_.refs_1_.refs_2_, bf16[2048,1152]{1,0:T(8,128)(2,1)} %get-tuple-element.94.q.k.v.refs_0_.refs_1_.refs_2_, ...), custom_call_target="tpu_custom_call", output_to_operand_aliasing={{1}: (7, {})} | custom-call | flops 5368709120 | bytes 8388608 | tf_op jit(solution)/shard_map/attend_back/pallas_call | solution.py:462
  119.3 4.8 %collective-permute-done.1 = f32[2880,128]{1,0:T(8,128)} collective-permute-done((f32[2880,128]{1,0:T(8,128)}, f32[2880,128]{1,0:T(8,128)}, u32[]{:S(2)}, u32[]{:S(2)}) %collective-permute-start.1) | collective-permute-done | bytes 1474592 | tf_op jit(solution)/shard_map/ppermute | solution.py:834
  124.1 2.3 dynamic-slice_add_fusion
  126.4 2.0 collective-permute-start.2
  128.4 8.2 %attend_back.12 = (bf16[2048,128]{1,0:T(8,128)(2,1)}, bf16[2,2048,128]{2,1,0:T(8,128)(2,1)}) custom-call(bf16[2048,1152]{1,0:T(8,128)(2,1)} %get-tuple-element.94.q.k.v.refs_0_.refs_1_.refs_2_, bf16[2048,1152]{1,0:T(8,128)(2,1)} %get-tuple-element.94.q.k.v.refs_0_.refs_1_.refs_2_, ...), custom_call_target="tpu_custom_call", output_to_operand_aliasing={{1}: (7, {})} | custom-call | flops 2684354560 | bytes 4194304 | tf_op jit(solution)/shard_map/attend_back/pallas_call | solution.py:462
  136.7 1.5 collective-permute-done.2
  138.2 2.0 dynamic-slice_add_fusion.2
  140.2 2.1 collective-permute-start.3
  142.3 7.8 %attend_back.13 = (f32[128,2048]{1,0:T(8,128)}, bf16[2,2048,128]{2,1,0:T(8,128)(2,1)}) custom-call(bf16[2048,1152]{1,0:T(8,128)(2,1)} %get-tuple-element.94.q.k.v.refs_0_.refs_1_.refs_2_, bf16[2048,1152]{1,0:T(8,128)(2,1)} %get-tuple-element.94.q.k.v.refs_0_.refs_1_.refs_2_, bf16[2048,1152]{1,0:T(8,128)(2,1)} %get-tuple-element.94.q.k.v.refs_0_.refs_1_.refs_2_, ...), custom_call_target="tpu_custom_call" | custom-call | flops 2684354560 | bytes 4194304 | tf_op jit(solution)/shard_map/attend_back/pallas_call | solution.py:462
  150.1 1.2 dynamic-slice_add_fusion.4
  151.3 2.6 collective-permute-start.4
  153.9 8.1 %attend_back.14 = (f32[128,2048]{1,0:T(8,128)}, bf16[2,2048,128]{2,1,0:T(8,128)(2,1)}) custom-call(bf16[2048,1152]{1,0:T(8,128)(2,1)} %get-tuple-element.94.q.k.v.refs_0_.refs_1_.refs_2_, bf16[2048,1152]{1,0:T(8,128)(2,1)} %get-tuple-element.94.q.k.v.refs_0_.refs_1_.refs_2_, ...), custom_call_target="tpu_custom_call", output_to_operand_aliasing={{1}: (7, {})} | custom-call | flops 2684354560 | bytes 4194304 | tf_op jit(solution)/shard_map/attend_back/pallas_call | solution.py:462
  162.0 1.2 add_add_fusion
  163.6 8.2 %attend_back.15 = (f32[128,2048]{1,0:T(8,128)}, bf16[2,2048,128]{2,1,0:T(8,128)(2,1)}) custom-call(bf16[2048,1152]{1,0:T(8,128)(2,1)} %get-tuple-element.94.q.k.v.refs_0_.refs_1_.refs_2_, bf16[2048,1152]{1,0:T(8,128)(2,1)} %get-tuple-element.94.q.k.v.refs_0_.refs_1_.refs_2_, ...), custom_call_target="tpu_custom_call", output_to_operand_aliasing={{1}: (7, {})} | custom-call | flops 2684354560 | bytes 4194304 | tf_op jit(solution)/shard_map/attend_back/pallas_call | solution.py:462
  171.8 0.9 collective-permute-done.5
  172.8 2.0 collective-permute-start.6
  174.8 8.3 %attend_back.16 = (bf16[2048,128]{1,0:T(8,128)(2,1)}, bf16[2,2048,128]{2,1,0:T(8,128)(2,1)}) custom-call(bf16[2048,1152]{1,0:T(8,128)(2,1)} %get-tuple-element.94.q.k.v.refs_0_.refs_1_.refs_2_, bf16[2048,1152]{1,0:T(8,128)(2,1)} %get-tuple-element.94.q.k.v.refs_0_.refs_1_.refs_2_, ...), custom_call_target="tpu_custom_call", output_to_operand_aliasing={{1}: (7, {})} | custom-call | flops 2684354560 | bytes 4194304 | tf_op jit(solution)/shard_map/attend_back/pallas_call | solution.py:462
  183.1 1.6 collective-permute-start.7
  184.7 7.8 %attend_back.17 = (f32[128,2048]{1,0:T(8,128)}, bf16[2,2048,128]{2,1,0:T(8,128)(2,1)}) custom-call(bf16[2048,1152]{1,0:T(8,128)(2,1)} %get-tuple-element.94.q.k.v.refs_0_.refs_1_.refs_2_, bf16[2048,1152]{1,0:T(8,128)(2,1)} %get-tuple-element.94.q.k.v.refs_0_.refs_1_.refs_2_, bf16[2048,1152]{1,0:T(8,128)(2,1)} %get-tuple-element.94.q.k.v.refs_0_.refs_1_.refs_2_, ...), custom_call_target="tpu_custom_call" | custom-call | flops 2684354560 | bytes 4194304 | tf_op jit(solution)/shard_map/attend_back/pallas_call | solution.py:462
  192.5 2.1 collective-permute-done.7
  195.4 12.6 %attend_back.18 = (f32[128,2048]{1,0:T(8,128)}, bf16[2,2048,128]{2,1,0:T(8,128)(2,1)}) custom-call(bf16[2048,1152]{1,0:T(8,128)(2,1)} %get-tuple-element.94.q.k.v.refs_0_.refs_1_.refs_2_, bf16[2048,1152]{1,0:T(8,128)(2,1)} %get-tuple-element.94.q.k.v.refs_0_.refs_1_.refs_2_, ...), custom_call_target="tpu_custom_call", output_to_operand_aliasing={{1}: (7, {})} | custom-call | flops 5368709120 | bytes 8388608 | tf_op jit(solution)/shard_map/attend_back/pallas_call | solution.py:462
  208.0 6.2 %collective-permute-done.8.refs_1_ = f32[2880,128]{1,0:T(8,128)S(1)} collective-permute-done((f32[2880,128]{1,0:T(8,128)S(1)}, f32[2880,128]{1,0:T(8,128)S(1)}, u32[]{:S(2)}, u32[]{:S(2)}) %collective-permute-start.8) | collective-permute-done | bytes 1474592 | tf_op jit(solution)/shard_map/ppermute | solution.py:834
  214.2 8.8 %attend_back.19 = (bf16[2048,128]{1,0:T(8,128)(2,1)}, bf16[2,2048,128]{2,1,0:T(8,128)(2,1)}) custom-call(bf16[2048,1152]{1,0:T(8,128)(2,1)} %get-tuple-element.94.q.k.v.refs_0_.refs_1_.refs_2_, bf16[2048,1152]{1,0:T(8,128)(2,1)} %get-tuple-element.94.q.k.v.refs_0_.refs_1_.refs_2_, ...), custom_call_target="tpu_custom_call", output_to_operand_aliasing={{1}: (7, {})} | custom-call | flops 2684354560 | bytes 4194304 | tf_op jit(solution)/shard_map/attend_back/pallas_call | solution.py:462
  223.0 7.4 %weigh.1 = (f32[1920,128]{1,0:T(8,128)}, f32[1920,128]{1,0:T(8,128)}, f32[8,384]{1,0:T(8,128)}) custom-call(s32[1]{0:T(128)} %bitcast.side, f32[1]{0:T(128)} %bitcast.9.weight, bf16[384,2048]{1,0:T(8,128)(2,1)} %get-tuple-element.142.first, bf16[2048,128]{1,0:T(8,128)(2,1)} %get-tuple-element.113.refs_0_.rest_0_, ...), custom_call_target="tpu_custom_call" | custom-call | flops 5435817984 | bytes 6291456 | tf_op jit(solution)/shard_map/weigh/pallas_call | solution.py:532
  231.1 5.4 %finish.2 = (f32[2048,384]{1,0:T(8,128)}, f32[8,384]{1,0:T(8,128)}) custom-call(s32[1]{0:T(128)S(6)} %copy.62.lead, f32[1]{0:T(128)} %bitcast.9.weight, f32[2048,384]{1,0:T(8,128)} %x.13, f32[40,384]{1,0:T(8,128)} %embed.7, f32[384]{0:T(512)} %gain.7, bf16[384,1152]{1,0:T(8,128)(2,1)} %wide.3, f32[2048,384]{1,0:T(8,128)} %get-tuple-element.149.d_mid, ...), custom_call_target="tpu_custom_call" | custom-call | flops 905969664 | bytes 7077888 | tf_op jit(solution)/shard_map/finish/pallas_call | solution.py:603
  236.4 0.8 dynamic-slice_add_fusion.1
  238.4 5.4 %finish.3 = (f32[2048,384]{1,0:T(8,128)}, f32[136,128]{1,0:T(8,128)}) custom-call(s32[1]{0:T(128)S(6)} %copy.62.lead, f32[1]{0:T(128)} %bitcast.9.weight, f32[2048,384]{1,0:T(8,128)} %x.13, f32[40,384]{1,0:T(8,128)} %embed.7, f32[384]{0:T(512)} %gain.7, bf16[384,1152]{1,0:T(8,128)(2,1)} %wide.3, ...), custom_call_target="tpu_custom_call", output_to_operand_aliasing={{0}: (15, {})} | custom-call | flops 905969664 | bytes 7077888 | tf_op jit(solution)/shard_map/finish/pallas_call | solution.py:603
  243.8 2.6 collective-permute-done.11
  246.4 1.0 dynamic-slice_add_fusion.3
  247.4 1.6 collective-permute-start.12
  249.0 6.6 %unpack.1 = (f32[384,1536]{1,0:T(8,128)}, f32[1536,384]{1,0:T(8,128)}, f32[384,384]{1,0:T(8,128)}, f32[207,384]{1,0:T(8,128)}, f32[32,128]{1,0:T(8,128)}) custom-call(s32[4]{0:T(128)} %pad_add_fusion.places, f32[2880,128]{1,0:T(8,128)} %copy-done.1, f32[2880,128]{1,0:T(8,128)} %copy-done.15, f32[2880,128]{1,0:T(8,128)} %collective-permute-done.13.refs_2_, ...), custom_call_target="tpu_custom_call" | custom-call | flops 8000000000 | bytes 23592960 | tf_op jit(solution)/shard_map/unpack/pallas_call | solution.py:689
  255.7 1.0 dynamic-slice_add_fusion.5
  256.8 4.8 %collective-permute-done.14 = f32[240,128]{1,0:T(8,128)S(1)} collective-permute-done((f32[240,128]{1,0:T(8,128)S(1)}, f32[240,128]{1,0:T(8,128)S(1)}, u32[]{:S(2)}, u32[]{:S(2)}) %collective-permute-start.14) | collective-permute-done | bytes 122912 | tf_op jit(solution)/shard_map/ppermute | solution.py:834
  261.6 0.8 dynamic-slice_add_fusion.6
  262.4 0.8 collective-permute-start.15
  263.3 4.9 %collective-permute-done.15 = f32[120,128]{1,0:T(8,128)S(1)} collective-permute-done((f32[120,128]{1,0:T(8,128)S(1)}, f32[120,128]{1,0:T(8,128)S(1)}, u32[]{:S(2)}, u32[]{:S(2)}) %collective-permute-start.15) | collective-permute-done | bytes 61472 | tf_op jit(solution)/shard_map/ppermute | solution.py:834
  268.1 0.9 add_add_fusion.1
  269.5 5.9 %collective-permute-done.16.got = f32[256,128]{1,0:T(8,128)S(1)} collective-permute-done((f32[256,128]{1,0:T(8,128)S(1)}, f32[256,128]{1,0:T(8,128)S(1)}, u32[]{:S(2)}, u32[]{:S(2)}) %collective-permute-start.16) | collective-permute-done | bytes 131104 | tf_op jit(solution)/shard_map/ppermute | solution.py:834
  276.0 1.7 join.4.mine
  277.7 6.7 %collective-permute-done.17.got = f32[376,128]{1,0:T(8,128)S(1)} collective-permute-done((f32[376,128]{1,0:T(8,128)}, f32[376,128]{1,0:T(8,128)S(1)}, u32[]{:S(2)}, u32[]{:S(2)}) %collective-permute-start.17) | collective-permute-done | bytes 192544 | tf_op jit(solution)/shard_map/ppermute | solution.py:834
  284.4 0.7 copy-done.7
  285.0 1.8 join.5.mine
  286.8 1.0 collective-permute-start.18
  287.8 7.8 %collective-permute-done.18.got = f32[616,128]{1,0:T(8,128)S(1)} collective-permute-done((f32[616,128]{1,0:T(8,128)}, f32[616,128]{1,0:T(8,128)S(1)}, u32[]{:S(2)}, u32[]{:S(2)}) %collective-permute-start.18) | collective-permute-done | bytes 315424 | tf_op jit(solution)/shard_map/ppermute | solution.py:834
  295.7 0.7 copy-done.6
  296.4 1.9 join.6.mine
  298.3 3.1 collective-permute-start.19
  301.4 7.8 %collective-permute-done.19.got = f32[1096,128]{1,0:T(8,128)S(1)} collective-permute-done((f32[1096,128]{1,0:T(8,128)}, f32[1096,128]{1,0:T(8,128)S(1)}, u32[]{:S(2)}, u32[]{:S(2)}) %collective-permute-start.19) | collective-permute-done | bytes 561184 | tf_op jit(solution)/shard_map/ppermute | solution.py:834
  309.2 0.8 copy-done.4
  310.0 2.3 join.7.mine
  315.2 1.0 copy-done.2
  316.1 4.1 %settle.1 = (f32[384,1152]{1,0:T(8,128)}, f32[40,384]{1,0:T(8,128)}, f32[16,128]{1,0:T(8,128)}) custom-call(s32[1]{0:T(128)} %bitcast.side, f32[2056,128]{1,0:T(8,128)} %join.7.mine, f32[2056,128]{1,0:T(8,128)} %copy-done.2), custom_call_target="tpu_custom_call" | custom-call | tf_op jit(solution)/shard_map/settle/pallas_call | solution.py:776
  320.2 1.4 slice_bitcast_fusion.6
  (72 shorter events, 9.3 us)
Async XLA Ops:
  7.2 77.3 %all-gather.3.cloned.1.call-start = ((), (), s32[]{:S(2)}) async-start(), calls=%async_computation | async-start | bytes 1081344 | tf_op jit(solution)/shard_map/all_gather | solution.py:970
  15.9 30.0 %copy-start.8 = (bf16[384,207]{0,1:T(8,128)(2,1)S(1)}, bf16[384,207]{0,1:T(8,128)(2,1)}, u32[]{:S(2)}) copy-start(bf16[384,207]{0,1:T(8,128)(2,1)} %param.41) | copy-start | bytes 476932
  15.9 30.0 %copy-start.12 = (f32[207]{0:T(256)S(1)}, f32[207]{0:T(256)}, u32[]{:S(2)}) copy-start(f32[207]{0:T(256)} %param.42) | copy-start | bytes 2488
  15.9 30.2 %copy-start.13 = (f32[69]{0:T(128)S(1)}, f32[69]{0:T(128)}, u32[]{:S(2)}) copy-start(f32[69]{0:T(128)} %param.43) | copy-start | bytes 832
  47.7 40.4 %copy-start.14 = (s32[40]{0:T(128)S(1)}, s32[40]{0:T(128)}, u32[]{:S(2)}) copy-start(s32[40]{0:T(128)} %param.26) | copy-start | bytes 484
  85.7 15.6 %collective-permute-start = (f32[5760,128]{1,0:T(8,128)}, f32[5760,128]{1,0:T(8,128)}, u32[]{:S(2)}, u32[]{:S(2)}) collective-permute-start(f32[5760,128]{1,0:T(8,128)} %get-tuple-element.100), channel_id=1, source_target_pairs={{0,2},{1,3},{2,0},{3,1},{4,6},{5,7},{6,4},{7,5},{8,10},{9,11},{10,... | collective-permute-start | bytes 8847368 | tf_op jit(solution)/shard_map/ppermute | solution.py:834
  93.2 8.0 %copy-start = (f32[5760,128]{1,0:T(8,128)S(1)}, f32[5760,128]{1,0:T(8,128)}, u32[]{:S(2)}) copy-start(f32[5760,128]{1,0:T(8,128)} %get-tuple-element.98) | copy-start | bytes 8847364
  103.9 20.2 %collective-permute-start.1 = (f32[2880,128]{1,0:T(8,128)}, f32[2880,128]{1,0:T(8,128)}, u32[]{:S(2)}, u32[]{:S(2)}) collective-permute-start(f32[2880,128]{1,0:T(8,128)} %multiply_add_fusion), channel_id=1, source_target_pairs={{0,4},{1,5},{2,3},{3,2},{4,0},{5,1},{6,7},{7,6},{8,12},{9,13},{10,... | collective-permute-start | bytes 4423688 | tf_op jit(solution)/shard_map/ppermute | solution.py:834
  126.4 11.8 %collective-permute-start.2 = (f32[1440,128]{1,0:T(8,128)}, f32[1440,128]{1,0:T(8,128)}, u32[]{:S(2)}, u32[]{:S(2)}) collective-permute-start(f32[1440,128]{1,0:T(8,128)} %dynamic-slice_add_fusion), channel_id=1, source_target_pairs={{0,1},{1,0},{2,10},{3,11},{4,5},{5,4},{6,14},{7,15},{8,9},{9,8},{1... | collective-permute-start | bytes 2211848 | tf_op jit(solution)/shard_map/ppermute | solution.py:834
  140.2 9.9 %collective-permute-start.3 = (f32[720,128]{1,0:T(8,128)}, f32[720,128]{1,0:T(8,128)S(1)}, u32[]{:S(2)}, u32[]{:S(2)}) collective-permute-start(f32[720,128]{1,0:T(8,128)} %dynamic-slice_add_fusion.2), channel_id=1, source_target_pairs={{0,8},{1,9},{2,6},{3,7},{4,12},{5,13},{6,2},{7,3},{8,0},{9,1},{10,... | collective-permute-start | bytes 1105928 | tf_op jit(solution)/shard_map/ppermute | solution.py:834
  151.3 10.7 %collective-permute-start.4 = (f32[360,128]{1,0:T(8,128)S(1)}, f32[360,128]{1,0:T(8,128)S(1)}, u32[]{:S(2)}, u32[]{:S(2)}) collective-permute-start(f32[360,128]{1,0:T(8,128)S(1)} %dynamic-slice_add_fusion.4), channel_id=1, source_target_pairs={{0,16},{1,17},{2,18},{3,19},{4,20},{5,21},{6,22},{7,23},{8,24},{9,... | collective-permute-start | bytes 552968 | tf_op jit(solution)/shard_map/ppermute | solution.py:834
  163.2 9.6 %collective-permute-start.5 = (f32[360,128]{1,0:T(8,128)S(1)}, f32[360,128]{1,0:T(8,128)S(1)}, u32[]{:S(2)}, u32[]{:S(2)}) collective-permute-start(f32[360,128]{1,0:T(8,128)S(1)} %add_add_fusion), channel_id=1, source_target_pairs={{0,16},{1,17},{2,18},{3,19},{4,20},{5,21},{6,22},{7,23},{8,24},{9,... | collective-permute-start | bytes 552968 | tf_op jit(solution)/shard_map/ppermute | solution.py:834
  172.8 10.2 %collective-permute-start.6 = (f32[720,128]{1,0:T(8,128)S(1)}, f32[720,128]{1,0:T(8,128)S(1)}, u32[]{:S(2)}, u32[]{:S(2)}) collective-permute-start(f32[720,128]{1,0:T(8,128)S(1)} %maximum_select_fusion.2), channel_id=1, source_target_pairs={{0,8},{1,9},{2,6},{3,7},{4,12},{5,13},{6,2},{7,3},{8,0},{9,1},{10,... | collective-permute-start | bytes 1105928 | tf_op jit(solution)/shard_map/ppermute | solution.py:834
  183.1 11.5 %collective-permute-start.7 = (f32[1440,128]{1,0:T(8,128)S(1)}, f32[1440,128]{1,0:T(8,128)S(1)}, u32[]{:S(2)}, u32[]{:S(2)}) collective-permute-start(f32[1440,128]{1,0:T(8,128)S(1)} %maximum_select_fusion.1), channel_id=1, source_target_pairs={{0,1},{1,0},{2,10},{3,11},{4,5},{5,4},{6,14},{7,15},{8,9},{9,8},{1... | collective-permute-start | bytes 2211848 | tf_op jit(solution)/shard_map/ppermute | solution.py:834
  194.8 35.8 %copy-start.1 = (f32[2880,128]{1,0:T(8,128)}, f32[2880,128]{1,0:T(8,128)S(1)}, u32[]{:S(2)}) copy-start(f32[2880,128]{1,0:T(8,128)S(1)} %maximum_select_fusion.refs_0_) | copy-start | bytes 4423684
  194.8 19.4 %collective-permute-start.8 = (f32[2880,128]{1,0:T(8,128)S(1)}, f32[2880,128]{1,0:T(8,128)S(1)}, u32[]{:S(2)}, u32[]{:S(2)}) collective-permute-start(f32[2880,128]{1,0:T(8,128)S(1)} %maximum_select_fusion.refs_0_), channel_id=1, source_target_pairs={{0,4},{1,5},{2,3},{3,2},{4,0},{5,1},{6,7},{7,6},{8,12},{9,13},{10,... | collective-permute-start | bytes 4423688 | tf_op jit(solution)/shard_map/ppermute | solution.py:834
  214.2 8.8 %copy-start.15 = (f32[2880,128]{1,0:T(8,128)}, f32[2880,128]{1,0:T(8,128)S(1)}, u32[]{:S(2)}) copy-start(f32[2880,128]{1,0:T(8,128)S(1)} %collective-permute-done.8.refs_1_) | copy-start | bytes 4423684
  214.2 8.8 %collective-permute-start.9 = (f32[2880,128]{1,0:T(8,128)S(1)}, f32[2880,128]{1,0:T(8,128)S(1)}, u32[]{:S(2)}, u32[]{:S(2)}) collective-permute-start(f32[2880,128]{1,0:T(8,128)S(1)} %collective-permute-done.8.refs_1_), channel_id=1, source_target_pairs={{0,2},{1,3},{2,0},{3,1},{4,6},{5,7},{6,4},{7,5},{8,10},{9,11},{10,... | collective-permute-start | bytes 4423688 | tf_op jit(solution)/shard_map/ppermute | solution.py:834
  223.0 7.4 %copy-start.16 = (f32[2880,128]{1,0:T(8,128)}, f32[2880,128]{1,0:T(8,128)S(1)}, u32[]{:S(2)}) copy-start(f32[2880,128]{1,0:T(8,128)S(1)} %collective-permute-done.9.refs_3_) | copy-start | bytes 4423684
  230.5 5.9 %collective-permute-start.10 = (f32[1920,128]{1,0:T(8,128)}, f32[1920,128]{1,0:T(8,128)S(1)}, u32[]{:S(2)}, u32[]{:S(2)}) collective-permute-start(f32[1920,128]{1,0:T(8,128)} %get-tuple-element.147), channel_id=1, source_target_pairs={{0,2},{1,3},{2,0},{3,1},{4,6},{5,7},{6,4},{7,5},{8,10},{9,11},{10,... | collective-permute-start | bytes 2949128 | tf_op jit(solution)/shard_map/ppermute | solution.py:834
  230.6 7.9 %collective-permute-start.13 = (f32[2880,128]{1,0:T(8,128)S(1)}, f32[2880,128]{1,0:T(8,128)}, u32[]{:S(2)}, u32[]{:S(2)}) collective-permute-start(f32[2880,128]{1,0:T(8,128)S(1)} %maximum_select_fusion.refs_0_), channel_id=1, source_target_pairs={{0,2},{1,3},{2,0},{3,1},{4,6},{5,7},{6,4},{7,5},{8,10},{9,11},{10,... | collective-permute-start | bytes 4423688 | tf_op jit(solution)/shard_map/ppermute | solution.py:834
  231.1 5.4 %copy-start.3 = (f32[1920,128]{1,0:T(8,128)S(1)}, f32[1920,128]{1,0:T(8,128)}, u32[]{:S(2)}) copy-start(f32[1920,128]{1,0:T(8,128)} %get-tuple-element.146) | copy-start | bytes 2949124
  237.3 9.1 %collective-permute-start.11 = (f32[960,128]{1,0:T(8,128)}, f32[960,128]{1,0:T(8,128)}, u32[]{:S(2)}, u32[]{:S(2)}) collective-permute-start(f32[960,128]{1,0:T(8,128)} %dynamic-slice_add_fusion.1), channel_id=1, source_target_pairs={{0,4},{1,5},{2,3},{3,2},{4,0},{5,1},{6,7},{7,6},{8,12},{9,13},{10,... | collective-permute-start | bytes 1474568 | tf_op jit(solution)/shard_map/ppermute | solution.py:834
  247.4 8.3 %collective-permute-start.12 = (f32[480,128]{1,0:T(8,128)S(1)}, f32[480,128]{1,0:T(8,128)S(1)}, u32[]{:S(2)}, u32[]{:S(2)}) collective-permute-start(f32[480,128]{1,0:T(8,128)S(1)} %dynamic-slice_add_fusion.3), channel_id=1, source_target_pairs={{0,1},{1,0},{2,10},{3,11},{4,5},{5,4},{6,14},{7,15},{8,9},{9,8},{1... | collective-permute-start | bytes 737288 | tf_op jit(solution)/shard_map/ppermute | solution.py:834
  255.7 13.3 %copy-start.10 = (f32[136,128]{1,0:T(8,128)S(1)}, f32[136,128]{1,0:T(8,128)}, u32[]{:S(2)}) copy-start(f32[136,128]{1,0:T(8,128)} %get-tuple-element.156) | copy-start | bytes 208900
  256.7 4.9 %collective-permute-start.14 = (f32[240,128]{1,0:T(8,128)S(1)}, f32[240,128]{1,0:T(8,128)S(1)}, u32[]{:S(2)}, u32[]{:S(2)}) collective-permute-start(f32[240,128]{1,0:T(8,128)S(1)} %dynamic-slice_add_fusion.5), channel_id=1, source_target_pairs={{0,8},{1,9},{2,6},{3,7},{4,12},{5,13},{6,2},{7,3},{8,0},{9,1},{10,... | collective-permute-start | bytes 368648 | tf_op jit(solution)/shard_map/ppermute | solution.py:834
  262.4 5.7 %collective-permute-start.15 = (f32[120,128]{1,0:T(8,128)S(1)}, f32[120,128]{1,0:T(8,128)S(1)}, u32[]{:S(2)}, u32[]{:S(2)}) collective-permute-start(f32[120,128]{1,0:T(8,128)S(1)} %dynamic-slice_add_fusion.6), channel_id=1, source_target_pairs={{0,16},{1,17},{2,18},{3,19},{4,20},{5,21},{6,22},{7,23},{8,24},{9,... | collective-permute-start | bytes 184328 | tf_op jit(solution)/shard_map/ppermute | solution.py:834
  269.0 6.4 %copy-start.5 = (f32[256,128]{1,0:T(8,128)}, f32[256,128]{1,0:T(8,128)S(1)}, u32[]{:S(2)}) copy-start(f32[256,128]{1,0:T(8,128)S(1)} %pad_maximum_fusion.mine) | copy-start | bytes 393220
  269.0 6.3 %collective-permute-start.16 = (f32[256,128]{1,0:T(8,128)S(1)}, f32[256,128]{1,0:T(8,128)S(1)}, u32[]{:S(2)}, u32[]{:S(2)}) collective-permute-start(f32[256,128]{1,0:T(8,128)S(1)} %pad_maximum_fusion.mine), channel_id=1, source_target_pairs={{0,16},{1,17},{2,18},{3,19},{4,20},{5,21},{6,22},{7,23},{8,24},{9,... | collective-permute-start | bytes 393224 | tf_op jit(solution)/shard_map/ppermute | solution.py:834
  275.4 0.6 copy-start.9
  277.7 6.7 %collective-permute-start.17 = (f32[376,128]{1,0:T(8,128)}, f32[376,128]{1,0:T(8,128)S(1)}, u32[]{:S(2)}, u32[]{:S(2)}) collective-permute-start(f32[376,128]{1,0:T(8,128)} %join.4.mine), channel_id=1, source_target_pairs={{0,8},{1,9},{2,6},{3,7},{4,12},{5,13},{6,2},{7,3},{8,0},{9,1},{10,... | collective-permute-start | bytes 577544 | tf_op jit(solution)/shard_map/ppermute | solution.py:834
  284.4 0.7 copy-start.7
  286.8 8.9 %collective-permute-start.18 = (f32[616,128]{1,0:T(8,128)}, f32[616,128]{1,0:T(8,128)S(1)}, u32[]{:S(2)}, u32[]{:S(2)}) collective-permute-start(f32[616,128]{1,0:T(8,128)} %join.5.mine), channel_id=1, source_target_pairs={{0,1},{1,0},{2,10},{3,11},{4,5},{5,4},{6,14},{7,15},{8,9},{9,8},{1... | collective-permute-start | bytes 946184 | tf_op jit(solution)/shard_map/ppermute | solution.py:834
  295.7 0.7 copy-start.6
  296.4 15.9 %copy-start.11 = (f32[32,128]{1,0:T(8,128)S(1)}, f32[32,128]{1,0:T(8,128)}, u32[]{:S(2)}) copy-start(f32[32,128]{1,0:T(8,128)} %get-tuple-element.160) | copy-start | bytes 49156
  298.3 10.9 %collective-permute-start.19 = (f32[1096,128]{1,0:T(8,128)}, f32[1096,128]{1,0:T(8,128)S(1)}, u32[]{:S(2)}, u32[]{:S(2)}) collective-permute-start(f32[1096,128]{1,0:T(8,128)} %join.6.mine), channel_id=1, source_target_pairs={{0,4},{1,5},{2,3},{3,2},{4,0},{5,1},{6,7},{7,6},{8,12},{9,13},{10,... | collective-permute-start | bytes 1683464 | tf_op jit(solution)/shard_map/ppermute | solution.py:834
  309.2 0.8 copy-start.4
  312.3 2.9 collective-permute-start.20
  315.2 1.0 copy-start.2
Sparse Core Ops, SparseCore 0:
  11.5 56.6 all-gather.2

commit v4 on v3

--- a/solution.py
+++ b/solution.py
@@ -404,91 +404,99 @@
     )(side, lead, x, mixed, inverse, experts, upstream, *tables)
 
 
-def attend_back_kernel(size, first_part, last_part, *refs):
-    if first_part:
-        q, k, v, d_across, d_down, probs, d_query, d_pair = refs[:8]
+def attend_back_kernel(size, pair, base, steps, last_part, token, *refs):
+    if base == 0:
+        projected, d_across, d_down, probs, d_query, d_pair, total, held, sems = refs
+        carry = None
     else:
-        q, k, v, d_across, d_down, probs, carry, _, d_query, d_pair = refs[:10]
-    total = refs[-1] if last_part else d_query
-    step = pl.program_id(0)
-    rows = q.shape[0]
-    block = k.shape[0]
+        projected, d_across, d_down, probs, carry, earlier, *refs = refs
+        d_query, d_pair, total, held, sems = refs
+        d_pair[:, : base * KEYS, :] = earlier[:, : base * KEYS, :]
+    rows = projected.shape[0]
+    pairs = projected.shape[1] // (3 * LANES)
     scaling = size ** (-0.5)
     lane = lax.broadcasted_iota(jnp.int32, (1, LANES), 1)
 
-    @pl.when(step == 0)
-    def _():
-        total[...] = jnp.zeros_like(total) if first_part else carry[...]
-
-    k_across = k[...].T
-    d_keys, d_values = [], []
-    for head in range(2):
-        base = (1 - head) * size
-        data = jnp.where(lane // size == head, 1.0, 0.0).astype(low)
-        ones = jnp.where((lane >= base) & (lane < base + 3), 1.0, 0.0).astype(low)
-        values = v[...] * data + ones
-        d_k = jnp.zeros((block, LANES), full)
-        d_v = jnp.zeros((block, LANES), full)
-        for start in (0,):
-            span = slice(start, start + rows)
-            p = probs[0, head, :, span]
-            d_p = mul(values, d_across[head, :, span])
+    def fetch(step, slot):
+        return pltpu.make_async_copy(
+            probs.at[pair, :, pl.ds((base + step) * KEYS, KEYS), :],
+            held.at[slot],
+            sems.at[slot],
+        )
+
+    fetch(0, 0).start()
+    total[...] = jnp.zeros_like(total) if carry is None else carry[...]
+
+    def one_step(step, unused):
+        slot = lax.rem(step, 2)
+
+        @pl.when(step + 1 < steps)
+        def _():
+            fetch(step + 1, 1 - slot).start()
+
+        fetch(step, slot).wait()
+        at = pl.ds(pl.multiple_of((base + step) * KEYS, KEYS), KEYS)
+        k = projected[at, (pairs + pair) * LANES : (pairs + pair + 1) * LANES]
+        v = projected[at, (2 * pairs + pair) * LANES : (2 * pairs + pair + 1) * LANES]
+        q = projected[:, pair * LANES : (pair + 1) * LANES]
+        down = d_down[:, pair * LANES : (pair + 1) * LANES]
+        k_across = k.T
+        d_keys, d_values = [], []
+        for head in range(2):
+            other = (1 - head) * size
+            data = jnp.where(lane // size == head, 1.0, 0.0).astype(low)
+            ones = jnp.where((lane >= other) & (lane < other + 3), 1.0, 0.0)
+            values = v * data + ones.astype(low)
+            p = held[slot, head]
+            d_p = mul(values, d_across[2 * pair + head])
             d_s = (p.astype(full) * d_p).astype(low)
-            total[head * size : (head + 1) * size, span] += mul(
-                k_across[head * size : (head + 1) * size, :], d_s
-            )
-            d_v = d_v + mul(p, d_down[span, :])
-            d_k = d_k + mul(d_s, q[span, :])
-        d_keys.append(d_k)
-        d_values.append(d_v)
-    d_pair[0] = (jnp.where(lane < size, *d_keys) * scaling).astype(low)
-    d_pair[1] = jnp.where(lane < size, *d_values).astype(low)
-
+            span = slice(head * size, (head + 1) * size)
+            total[span, :] += mul(k_across[span, :], d_s)
+            d_values.append(mul(p, down))
+            d_keys.append(mul(d_s, q))
+        d_pair[0, at, :] = (jnp.where(lane < size, *d_keys) * scaling).astype(low)
+        d_pair[1, at, :] = jnp.where(lane < size, *d_values).astype(low)
+        return unused
+
+    lax.fori_loop(0, steps, one_step, 0)
     if last_part:
-
-        @pl.when(step == pl.num_programs(0) - 1)
-        def _():
-            d_query[...] = (total[...].T * scaling).astype(low)
-
-
-def attend_back(pair, base, steps, projected, d_across, d_down, probs, carried):
+        d_query[...] = (total[...].T * scaling).astype(low)
+    else:
+        d_query[...] = total[...]
+
+
+def attend_back(
+    pair, base, steps, token, projected, d_across, d_down, probs, carried
+):
     rows, wide = projected.shape
     features = wide // 3
-    pairs = features // LANES
     size = features // HEADS
-    total = rows // KEYS
-    first_part, last_part = base == 0, base + steps == total
+    all_steps = rows // KEYS
+    last_part = base + steps == all_steps
     across = (rows, LANES) if last_part else (LANES, rows)
+    vmem = pl.BlockSpec(memory_space=pltpu.VMEM)
     return pl.pallas_call(
-        functools.partial(attend_back_kernel, size, first_part, last_part),
-        grid=(steps,),
-        in_specs=[
-            pl.BlockSpec((rows, LANES), lambda i: (0, pair)),
-            pl.BlockSpec((KEYS, LANES), lambda i: (base + i, pairs + pair)),
-            pl.BlockSpec((KEYS, LANES), lambda i: (base + i, 2 * pairs + pair)),
-            pl.BlockSpec((2, LANES, rows), lambda i: (pair, 0, 0)),
-            pl.BlockSpec((rows, LANES), lambda i: (0, pair)),
-            pl.BlockSpec((1, 2, KEYS, rows), lambda i: (pair, 0, base + i, 0)),
-        ]
-        + ([] if first_part else [whole((LANES, rows)), pl.BlockSpec(memory_space=pl.ANY)]),
-        out_specs=[
-            whole(across),
-            pl.BlockSpec((2, KEYS, LANES), lambda i: (0, base + i, 0)),
-        ],
+        functools.partial(attend_back_kernel, size, pair, base, steps, last_part),
+        in_specs=[SCALAR, vmem, vmem, vmem, pl.BlockSpec(memory_space=pl.ANY)]
+        + [vmem] * len(carried),
+        out_specs=[vmem, vmem],
         out_shape=[
             jax.ShapeDtypeStruct(across, low if last_part else full),
             jax.ShapeDtypeStruct((2, rows, LANES), low),
         ],
-        scratch_shapes=[pltpu.VMEM((LANES, rows), full)] if last_part else [],
-        input_output_aliases={} if first_part else {7: 1},
-        compiler_params=params(1),
+        scratch_shapes=[
+            pltpu.VMEM((LANES, rows), full),
+            pltpu.VMEM((2, 2, KEYS, rows), low),
+            pltpu.SemaphoreType.DMA((2,)),
+        ],
+        compiler_params=pltpu.CompilerParams(vmem_limit_bytes=32 * 2**20),
         cost_estimate=pl.CostEstimate(
-            flops=10 * rows * rows * 256 * steps // total,
-            bytes_accessed=rows * rows * 4 * steps // total,
+            flops=10 * rows * rows * 256 * steps // all_steps,
+            bytes_accessed=rows * rows * 4 * steps // all_steps,
             transcendentals=0,
         ),
         name="attend_back",
-    )(projected, projected, projected, d_across, d_down, probs, *carried)
+    )(token, projected, d_across, d_down, probs, *carried)
 
 
 def weigh_kernel(pairs, places, side, weight, first, *refs):
@@ -584,12 +592,14 @@
         @pl.when(step == pl.num_programs(0) - 1)
         def _():
             vectors[...] = jnp.zeros_like(vectors)
-            for block in range(pairs):
-                lanes = slice(block * LANES, (block + 1) * LANES)
-                for index, ref in enumerate((sums, sums, biases, biases)):
-                    at = index * pairs + block
-                    vectors[at : at + 1, :] = ref[index % 2 : index % 2 + 1, lanes]
-                vectors[pl.ds((4 + lead[0]) * pairs + block, 1), :] = sums[2:3, lanes]
+            for index, (ref, at) in enumerate(
+                ((sums, 0), (sums, 1), (biases, 0), (biases, 1), (sums, 2))
+            ):
+                for block in range(pairs):
+                    row = index * pairs + block
+                    vectors[row : row + 1, :] = ref[
+                        at : at + 1, block * LANES : (block + 1) * LANES
+                    ]
 
 
 def finish(base, steps, lead, weight, x, embed, gain, wide, d_mid, d_query, d_pair, carried):
@@ -597,7 +607,7 @@
     pairs = len(d_query)
     total = rows // ROWS
     last_part = base + steps == total
-    height = up_to((4 + embed.shape[0]) * pairs, 8)
+    height = up_to(5 * pairs, 8)
     row_spec = pl.BlockSpec((ROWS, features), lambda i: (base + i, 0))
     small = pl.BlockSpec((8, features), lambda i: (0, 0))
     return pl.pallas_call(
@@ -632,16 +642,15 @@
     )(lead, weight, x, embed, gain, wide, d_mid, *d_query, *d_pair, *carried)
 
 
-def unpack_kernel(spans, group, channels, places, *refs):
-    pieces = refs[:4]
-    expand, shrink, merge, router, vectors, grads, sems = refs[4:]
-    quarter = pieces[0].shape[0]
-    height = 2 * quarter
+def unpack_kernel(spans, group, channels, owners, *refs):
+    chunks, expand, shrink, merge, router, vectors, grads, sems = refs
+    chunk = chunks.shape[1]
+    height = len(owners) * chunk // 2
     arrivals = [
         pltpu.make_async_copy(
-            pieces[n], grads.at[pl.ds(places[n] * quarter, quarter)], sems.at[n]
+            chunks.at[owner], grads.at[pl.ds(n * chunk, chunk)], sems.at[n]
         )
-        for n in range(4)
+        for n, owner in enumerate(owners)
     ]
     for copy in arrivals:
         copy.start()
@@ -661,7 +670,7 @@
                 pltpu.make_async_copy(
                     block(name, features, index),
                     target.at[:, pl.ds(index * LANES, LANES)],
-                    sems.at[4 + len(leaving)],
+                    sems.at[len(owners) + len(leaving)],
                 )
             )
     for copy in leaving:
@@ -682,13 +691,13 @@
         copy.wait()
 
 
-def unpack(spans, group, channels, features, hidden, tall, places, pieces):
+def unpack(spans, group, channels, owners, features, hidden, tall, chunks):
     vmem = pl.BlockSpec(memory_space=pltpu.VMEM)
     anywhere = pl.BlockSpec(memory_space=pl.ANY)
-    quarter = pieces[0].shape[0]
+    height = len(owners) * chunks.shape[1]
     return pl.pallas_call(
-        functools.partial(unpack_kernel, spans, group, channels),
-        in_specs=[SCALAR] + [anywhere] * 4,
+        functools.partial(unpack_kernel, spans, group, channels, owners),
+        in_specs=[anywhere],
         out_specs=[anywhere, vmem, anywhere, vmem, vmem],
         out_shape=[
             jax.ShapeDtypeStruct((features, hidden), full),
@@ -698,98 +707,208 @@
             jax.ShapeDtypeStruct((tall, LANES), full),
         ],
         scratch_shapes=[
-            pltpu.VMEM((4 * quarter, LANES), full),
-            pltpu.SemaphoreType.DMA((4 + (hidden + features) // LANES,)),
+            pltpu.VMEM((height, LANES), full),
+            pltpu.SemaphoreType.DMA((len(owners) + (hidden + features) // LANES,)),
         ],
         compiler_params=pltpu.CompilerParams(vmem_limit_bytes=LIMIT),
         cost_estimate=pl.CostEstimate(
-            flops=8 * 10**9, bytes_accessed=quarter * 8192, transcendentals=0
+            flops=8 * 10**9, bytes_accessed=height * 1024, transcendentals=0
         ),
         name="unpack",
-    )(places, *pieces)
-
-
-def join_kernel(shared, side, mine, got, out):
-    height = mine.shape[0] - shared
-    out[:shared, :] = mine[:shared, :] + got[:shared, :]
-    left = pl.multiple_of(shared + side[0] * height, 8)
-    right = pl.multiple_of(shared + (1 - side[0]) * height, 8)
-    out[pl.ds(left, height), :] = mine[shared:, :]
-    out[pl.ds(right, height), :] = got[shared:, :]
-
-
-def join(shared, side, mine, got):
-    vmem = pl.BlockSpec(memory_space=pltpu.VMEM)
-    height = 2 * mine.shape[0] - shared
+    )(chunks)
+
+
+def join_kernel(hop, sides, mine, got, out, sems):
+    height = mine.shape[0]
+    copies = []
+    for index, (rows, at) in enumerate(
+        ((mine, sides[hop]), (got, 1 - sides[hop]))
+    ):
+        start = pl.multiple_of(at * height, 8)
+        copies.append(
+            pltpu.make_async_copy(rows, out.at[pl.ds(start, height)], sems.at[index])
+        )
+    for copy in copies:
+        copy.start()
+    for copy in copies:
+        copy.wait()
+
+
+def join(hop, sides, mine, got):
+    anywhere = pl.BlockSpec(memory_space=pl.ANY)
     return pl.pallas_call(
-        functools.partial(join_kernel, shared),
-        in_specs=[SCALAR, vmem, vmem],
-        out_specs=vmem,
-        out_shape=jax.ShapeDtypeStruct((height, LANES), full),
-        compiler_params=pltpu.CompilerParams(vmem_limit_bytes=LIMIT),
+        functools.partial(join_kernel, hop),
+        in_specs=[SCALAR, anywhere, anywhere],
+        out_specs=anywhere,
+        out_shape=jax.ShapeDtypeStruct((2 * mine.shape[0], LANES), full),
+        scratch_shapes=[pltpu.SemaphoreType.DMA((2,))],
+        compiler_params=pltpu.CompilerParams(vmem_limit_bytes=2**20),
         name="join",
-    )(side, mine, got)
-
-
-def settle_kernel(places, side, mine, got, attend, embed, vectors, grads, sums, sems):
-    shared = sums.shape[0]
-    height = mine.shape[0] - shared
+    )(sides, mine, got)
+
+
+def settle_kernel(
+    places,
+    owners,
+    chunk,
+    extra,
+    side,
+    leads,
+    mine,
+    got,
+    attend,
+    embed,
+    vectors,
+    held,
+    table,
+    sems,
+):
     features = attend.shape[0]
-    leads = embed.shape[0]
     pairs = features // LANES
     arrivals = [
-        pltpu.make_async_copy(
-            mine.at[pl.ds(shared, height)], grads.at[side[0]], sems.at[0]
-        ),
-        pltpu.make_async_copy(
-            got.at[pl.ds(shared, height)], grads.at[1 - side[0]], sems.at[1]
-        ),
+        pltpu.make_async_copy(mine, held.at[side[0]], sems.at[0]),
+        pltpu.make_async_copy(got, held.at[1 - side[0]], sems.at[1]),
     ]
     for copy in arrivals:
         copy.start()
-    sums[...] = mine[:shared, :] + got[:shared, :]
-    vectors[...] = sums[: vectors.shape[0], :]
-    for block in range(pairs):
-        embed[:, block * LANES : (block + 1) * LANES] = sums[
-            pl.ds(4 * pairs + block, leads, stride=pairs), :
-        ]
+    table[...] = jnp.zeros_like(table)
     for copy in arrivals:
         copy.wait()
+    stride = chunk + extra
+    count = mine.shape[0] // stride
     leaving = []
     for index, (half, base) in enumerate(places):
-        leaving.append(
-            pltpu.make_async_copy(
-                grads.at[half, pl.ds(base, features)],
-                attend.at[:, pl.ds(index * LANES, LANES)],
-                sems.at[2 + index],
+        done = 0
+        while done < features:
+            at = base + done
+            inside = at % chunk
+            size = min(features - done, chunk - inside)
+            leaving.append(
+                pltpu.make_async_copy(
+                    held.at[half, pl.ds(at // chunk * stride + inside, size)],
+                    attend.at[pl.ds(done, size), pl.ds(index * LANES, LANES)],
+                    sems.at[2 + len(leaving)],
+                )
             )
-        )
+            done += size
     for copy in leaving:
         copy.start()
+    total = jnp.zeros((extra, LANES), full)
+    row = lax.broadcasted_iota(jnp.int32, (table.shape[1], LANES), 0).astype(full)
+    for half in range(2):
+        for n in range(count):
+            rows = held[half, n * stride + chunk : (n + 1) * stride, :]
+            total = total + rows
+            owner = owners[half * count + n]
+            here = row == leads[owner : owner + 1, :]
+            for block in range(pairs):
+                at = 4 * pairs + block
+                table[block] += jnp.where(here, rows[at : at + 1, :], 0.0)
+    vectors[...] = total
+    for block in range(pairs):
+        embed[:, block * LANES : (block + 1) * LANES] = table[block]
     for copy in leaving:
         copy.wait()
 
 
-def settle(places, shared, leads, features, side, mine, got):
+def settle(places, owners, chunk, extra, leads, features, side, seen, mine, got):
     vmem = pl.BlockSpec(memory_space=pltpu.VMEM)
-    height = mine.shape[0] - shared
+    anywhere = pl.BlockSpec(memory_space=pl.ANY)
+    moves = 0
+    for _, base in places:
+        moves += (base + features - 1) // chunk - base // chunk + 1
     return pl.pallas_call(
-        functools.partial(settle_kernel, places),
-        in_specs=[SCALAR, vmem, vmem],
-        out_specs=[pl.BlockSpec(memory_space=pl.ANY), vmem, vmem],
+        functools.partial(settle_kernel, places, owners, chunk, extra),
+        in_specs=[SCALAR, vmem, anywhere, anywhere],
+        out_specs=[anywhere, vmem, vmem],
         out_shape=[
             jax.ShapeDtypeStruct((features, 3 * features), full),
             jax.ShapeDtypeStruct((leads, features), full),
-            jax.ShapeDtypeStruct((up_to(4 * features // LANES, 8), LANES), full),
+            jax.ShapeDtypeStruct((extra, LANES), full),
         ],
         scratch_shapes=[
-            pltpu.VMEM((2, height, LANES), full),
-            pltpu.VMEM((shared, LANES), full),
-            pltpu.SemaphoreType.DMA((2 + len(places),)),
-        ],
-        compiler_params=pltpu.CompilerParams(vmem_limit_bytes=LIMIT),
+            pltpu.VMEM((2, mine.shape[0], LANES), full),
+            pltpu.VMEM((features // LANES, leads, LANES), full),
+            pltpu.SemaphoreType.DMA((2 + moves,)),
+        ],
+        compiler_params=pltpu.CompilerParams(vmem_limit_bytes=32 * 2**20),
         name="settle",
-    )(side, mine, got)
+    )(side, seen, mine, got)
+
+
+def fold_kernel(count, sides, factors, *refs):
+    total = refs[0][...] * factors[0]
+    for index in range(1, count):
+        total = total + refs[index][...] * factors[min(index, 2)]
+    refs[count][...] = total
+
+
+def fold(hop, hops, sides, factors, unit, terms):
+    def spec(made):
+        def index(i, sides, factors):
+            at = i
+            for step in range(made + 1, hop):
+                at = at + sides[step] * 2 ** (hops - 1 - step)
+            if hop < hops:
+                at = at + (1 - sides[hop]) * 2 ** (hops - 1 - hop)
+            return at, 0
+
+        return pl.BlockSpec((unit, LANES), index)
+
+    length = 2 ** (hops - 1 - hop) if hop < hops else 1
+    return pl.pallas_call(
+        functools.partial(fold_kernel, len(terms)),
+        grid_spec=pltpu.PrefetchScalarGridSpec(
+            num_scalar_prefetch=2,
+            grid=(length,),
+            in_specs=[spec(max(index - 1, 0)) for index in range(len(terms))],
+            out_specs=pl.BlockSpec((unit, LANES), lambda i, *tables: (i, 0)),
+        ),
+        out_shape=jax.ShapeDtypeStruct((length * unit, LANES), full),
+        compiler_params=pltpu.CompilerParams(
+            dimension_semantics=("arbitrary",), vmem_limit_bytes=8 * 2**20
+        ),
+        name="fold",
+    )(sides, factors, *terms)
+
+
+def weights_kernel(index, frames, seen, weights, leads, held, sem):
+    copy = pltpu.make_async_copy(seen.at[:, pl.ds(0, 8), :], held, sem)
+    copy.start()
+    total = lax.fori_loop(
+        0, frames.shape[0], lambda n, sofar: sofar + frames[n], jnp.int32(0)
+    ).astype(full)
+    copy.wait()
+    count = held.shape[0]
+    rows = held[:, 0, :]
+    leads[...] = rows
+    device = lax.broadcasted_iota(jnp.int32, rows.shape, 0)
+    for side in range(2):
+        lead = jnp.max(jnp.where(device == index[side], rows, 0.0))
+        same = jnp.sum(jnp.where(rows == lead, 1.0, 0.0)) / LANES
+        chosen = frames[lead.astype(jnp.int32)].astype(full)
+        weights[side] = chosen * count / (same * total)
+    weights[2] = jnp.float32(1.0)
+
+
+def weights_of(index, frames, seen):
+    count = seen.shape[0]
+    smem = pl.BlockSpec(memory_space=pltpu.SMEM)
+    return pl.pallas_call(
+        weights_kernel,
+        in_specs=[smem, smem, pl.BlockSpec(memory_space=pl.ANY)],
+        out_specs=[smem, pl.BlockSpec(memory_space=pltpu.VMEM)],
+        out_shape=[
+            jax.ShapeDtypeStruct((3,), full),
+            jax.ShapeDtypeStruct((count, LANES), full),
+        ],
+        scratch_shapes=[
+            pltpu.VMEM((count, 8, LANES), full),
+            pltpu.SemaphoreType.DMA,
+        ],
+        compiler_params=pltpu.CompilerParams(vmem_limit_bytes=8 * 2**20),
+        name="weights",
+    )(index, frames, seen)
 
 
 def up_to(value, step):
@@ -833,73 +952,35 @@
         ]
         return lax.ppermute(values, ("dp", "rep"), moves)
 
-    def side(self, hop, partner=False):
+    def sides(self):
         if not self.hops:
-            return jnp.int32(0)
-        even, odd = self.bits(hop)
-        if partner:
-            even, odd = odd, even
-        bit = even
-        if even != odd:
-            bit = jnp.where(self.index & self.core_bit == 0, even, odd)
-        return jnp.where(self.index & bit == 0, 0, 1)
-
-    def scatter(self, keep, send, factors=(None, None)):
-        got = self.swap(send, 0)
-        beside = yield send
-        got = got if beside is None else tie(got, beside)
-        terms = [[keep, 0, factors[0]], [got, 0, factors[1]]]
-        length = keep.shape[0]
-
-        def region(start, size):
-            total = None
-            for values, offset, factor in terms:
-                part = lax.dynamic_slice_in_dim(values, offset + start, size, 0)
-                part = part if factor is None else part * factor
-                total = part if total is None else total + part
-            return total
-
-        for hop in range(1, self.hops):
-            length //= 2
-            side = self.side(hop)
-            send = region((1 - side) * length, length)
+            return jnp.zeros((1,), jnp.int32)
+        even, odd = (
+            jnp.array((self.core_bit,) + order, jnp.int32) for order in self.orders
+        )
+        bits = jnp.where(self.index & self.core_bit == 0, even, odd)
+        return jnp.where(self.index & bits == 0, 0, 1).astype(jnp.int32)
+
+    def scatter(self, sides, factors, keep, send):
+        unit = keep.shape[0] >> (self.hops - 1)
+        terms = [keep]
+        for hop in range(self.hops):
+            if hop:
+                send = fold(hop, self.hops, sides, factors, unit, terms)
             got = self.swap(send, hop)
-            for term in terms:
-                term[1] = term[1] + side * length
             beside = yield send
-            terms.append([got if beside is None else tie(got, beside), 0, None])
-        return region(0, length)
-
-    def gather(self, values):
-        for hop in reversed(range(2, self.hops)):
-            got = self.swap(values, hop)
-            beside = yield values
-            if beside is not None:
-                got = tie(got, beside)
-            values = jnp.where(
-                self.side(hop) == 0,
-                jnp.concatenate([values, got]),
-                jnp.concatenate([got, values]),
-            )
-        got = self.swap(values, 1)
-        across = self.swap(values, 0)
-        beside = yield values
-        if beside is not None:
-            got, across = tie(got, beside), tie(across, beside)
-        final = self.swap(got, 0)
-        beside = yield got
-        if beside is not None:
-            final = tie(final, beside)
-        core, near, far = self.side(0), self.side(1), self.side(1, partner=True)
-        places = jnp.stack(
-            [
-                2 * core + near,
-                2 * core + 1 - near,
-                2 * (1 - core) + far,
-                2 * (1 - core) + 1 - far,
-            ]
-        )
-        return places, (values, got, across, final)
+            terms.append(got if beside is None else tie(got, beside))
+        return fold(self.hops, self.hops, sides, factors, unit, terms)
+
+    def owners(self):
+        found = [0] * self.count
+        for device in range(self.count):
+            core = (device // self.core_bit) % 2
+            chunk = 0
+            for hop in range(self.hops):
+                chunk = 2 * chunk + (1 if device & self.bits(hop)[core] else 0)
+            found[chunk] = device
+        return tuple(found)
 
 
 class Flow:
@@ -922,11 +1003,6 @@
         while not self.done:
             self.push(None)
         return self.result
-
-
-def total_of(ring, keep, send, factors):
-    part = yield from ring.scatter(keep, send, factors)
-    return (yield from ring.gather(part))
 
 
 def body(sizes, *args):
@@ -962,32 +1038,20 @@
     pairs = features // LANES
     grain = 4 * devices
     ring = Ring(sizes)
-    core = ring.side(0).reshape(1)
+    sides = ring.sides()
 
     tall = max(8, 2048 // devices)
     mine = lead_index[0].astype(full)
-    leads_seen = lax.optimization_barrier(
+    seen = lax.optimization_barrier(
         lax.all_gather(
             lax.optimization_barrier(jnp.full((tall, LANES), mine)), ("dp", "rep")
         )
-    )[:, 0, 0]
-    table = lead_frames.astype(full)
-
-    def weight_of(lead):
-        count = jnp.sum((leads_seen == lead).astype(full))
-        chosen = jnp.sum(
-            jnp.where(jnp.arange(leads, dtype=jnp.int32).astype(full) == lead, table, 0.0)
-        )
-        return chosen * devices / (count * jnp.sum(table))
-
-    scale = weight_of(mine)
-    other = scale
-    if ring.hops:
-        position = ring.index ^ ring.core_bit
-        other = weight_of(
-            jnp.sum(jnp.where(jnp.arange(devices) == position, leads_seen, 0.0))
-        )
-    weight = scale.reshape(1)
+    )
+    weight, leads_seen = weights_of(
+        jnp.stack([ring.index, ring.index ^ ring.core_bit]).astype(jnp.int32),
+        lead_frames,
+        seen,
+    )
 
     first, projected = project(
         lead_index,
@@ -1049,7 +1113,7 @@
         spans,
         height,
         group,
-        core,
+        sides,
         lead_index,
         block_input,
         mixed,
@@ -1060,16 +1124,16 @@
     )
     flow = None
     if ring.hops:
-        flow = Flow(total_of(ring, keep, tie(send, leads_seen), (scale, other)))
-    plan = ((1, 2, 1), (1, 1, 1, 1), (1, 2, 1))
+        flow = Flow(ring.scatter(sides, weight, keep, tie(send, seen)))
+    plan = ((1, 3), (2, 1, 1), (4,))
     d_query, d_pair = [], []
     for pair in range(pairs):
         carried = ()
         base = 0
         for steps in plan[pair]:
-            now = d_down if flow is None or flow.done else tie(d_down, flow.sent)
+            token = sides if flow is None or flow.done else tie(sides, flow.sent)
             carried = attend_back(
-                pair, base, steps, projected, d_across, now, probs, carried
+                pair, base, steps, token, projected, d_across, d_down, probs, carried
             )
             base += steps
             if flow is not None:
@@ -1080,13 +1144,14 @@
         (n // 5, (n % 5) * features) for n in range(3 * pairs)
     )
     tail_height = up_to(5 * features, grain)
-    now = weight if flow is None else tie(weight, flow.drain()[1][3])
+    now = weight if flow is None else tie(weight, flow.drain())
     tail_keep, tail_send, biases = weigh(
-        places, tail_height, core, now, first, d_query, d_pair
+        places, tail_height, sides, now, first, d_query, d_pair
     )
     late = None
     if ring.hops:
-        late = Flow(ring.scatter(tail_keep, tail_send))
+        ones = jnp.ones((3,), full)
+        late = Flow(ring.scatter(sides, ones, tail_keep, tail_send))
     carried = ()
     base = 0
     for steps in (2, 2):
@@ -1109,19 +1174,27 @@
         carried = (sums, biases, grad_input)
         if late is not None:
             late.push(sums)
-    shared = sums.shape[0]
+    extra = sums.shape[0]
     if ring.hops:
-        where, pieces = flow.result
-        where = tie(where, late.sent)
+        owners = ring.owners()
+        chunks = lax.all_gather(flow.result, ("dp", "rep"))
+        piece = jnp.concatenate([late.drain(), sums])
+        for hop in reversed(range(1, ring.hops)):
+            got = ring.swap(piece, hop)
+            if hop == 1:
+                chunks = tie(chunks, piece)
+            piece = join(hop, sides, piece, got)
+        got = ring.swap(piece, 0)
+        chunk = 2 * tail_height // devices
     else:
-        where = jnp.arange(4, dtype=jnp.int32)
-        pieces = [
-            half[start : start + height // 2] * scale
-            for half in (keep, send)
-            for start in (0, height // 2)
-        ]
+        owners = (0, 1)
+        chunks = jnp.stack([keep, send]) * weight[0]
+        chunk = tail_height
+        piece = jnp.concatenate([tail_keep, sums])
+        got = jnp.concatenate([tail_send, jnp.zeros_like(sums)])
+        leads_seen = jnp.concatenate([leads_seen, leads_seen + leads])
     grad_expand, grad_shrink, grad_merge, grad_router, vectors = unpack(
-        spans, group, channels, features, hidden, vector_rows, where, pieces
+        spans, group, channels, owners, features, hidden, vector_rows, chunks
     )
     first_vector = spans["expand_bias"][1]
 
@@ -1140,17 +1213,18 @@
         head[3 * group : 3 * group + channels],
     )
     if ring.hops:
-        late.push(vectors)
-        piece = jnp.concatenate([sums, late.drain()])
-        for hop in reversed(range(1, ring.hops)):
-            got = ring.swap(piece, hop)
-            piece = join(shared, ring.side(hop).reshape(1), piece, got)
-        got = ring.swap(piece, 0)
-    else:
-        piece = jnp.concatenate([sums, tail_keep])
-        got = jnp.concatenate([jnp.zeros_like(sums), tail_send])
+        got = tie(got, vectors)
     grad_attend, grad_embed, small = settle(
-        places, shared, leads, features, core, piece, got
+        places,
+        owners,
+        chunk,
+        extra,
+        leads,
+        features,
+        sides,
+        leads_seen,
+        piece,
+        got,
     )
     small = small[: 4 * pairs].reshape(4, features)
     merge_b, gain_b, shift_b, expand_b, shrink_b, router_b, correct = middle_vectors

time: 335 us -> 298 us (0.89)
  Pallas kernels: 201 us -> 183 us
  other arithmetic: 17.8 us -> 0.61 us
  local copies, waits for them, and re-layouts: 11.3 us -> 21.8 us
  starting transfers between devices: 22.7 us -> 16.1 us
  between operations: 19.2 us -> 15.5 us
    pallas_call x16 -> x23, Pallas kernels: 109 us -> 90.2 us  [the longest x6 68.4 us: attend_back(): pl.pallas_call(functools.partial(attend_back_kernel, size, pair, base, st...]
    add x10 -> x0, other arithmetic: 13.8 us -> none  [region(): total = part if total is None else total + part]
    unnamed x34 -> x54, local copies, waits for them, and re-layouts: 3.9 us -> 14.9 us
    ppermute x21 -> x15, starting transfers between devices: 22.7 us -> 16 us  [swap(): return lax.ppermute(values, ('dp', 'rep'), moves)]
    ppermute x21 -> x15, waiting for transfers between devices: 56.4 us -> 55 us  [swap(): return lax.ppermute(values, ('dp', 'rep'), moves)]
  transfers between devices with their start and end apart: 22 -> 17, of which waited for: 13 -> 9; matrix products, arithmetic and copies ran while one was open for 3% -> 2% of each run, Pallas kernels for 55% -> 60%
where the time goes in v4:
time: 298 us; the launch traced here: 292 us
  Pallas kernels  183 us (61%)
  waiting for transfers between devices  55 us (18%)
  local copies, waits for them, and re-layouts  21.8 us (7%)
  starting transfers between devices  16.1 us (5%)
  between operations  15.5 us (5%)
    pallas_call x6, Pallas kernels, attend_back(): pl.pallas_call(functools.partial(attend_back_kernel, size, pair, base, st...  68.4 us
    ppermute x15, waiting for transfers between devices, swap(): return lax.ppermute(values, ('dp', 'rep'), moves)  55 us
    pallas_call x1, Pallas kernels, middle(): pl.pallas_call(functools.partial(middle_kernel, spans, size, group), grid...  37.2 us
    pallas_call x1, Pallas kernels, attend(): pl.pallas_call(functools.partial(attend_kernel, size), grid=(pairs, rows...  30 us
    ppermute x15, starting transfers between devices, swap(): return lax.ppermute(values, ('dp', 'rep'), moves)  16 us
    unnamed x54, local copies, waits for them, and re-layouts  14.9 us
    pallas_call x2, Pallas kernels, finish(): pl.pallas_call(functools.partial(finish_kernel, pairs, last_part), grid=(...  11.1 us
    pallas_call x10, Pallas kernels, fold(): pl.pallas_call(functools.partial(fold_kernel, len(terms)), grid_spec=pltp...  7.67 us
  transfers between devices with their start and end apart: 17, of which 9 were waited for; matrix products, arithmetic and copies ran while one was open for 2% of the time, Pallas kernels for 60%

profile of v4, /device:TPU:0, one launch (start us, length us, event | category | flops | bytes accessed | tf_op | source)
XLA Modules:
  0.0 292.0 jit_solution(10850630309969296782)
XLA Ops:
  7.9 0.6 broadcast_in_dim.10
  8.6 7.4 %project.1 = (bf16[384,2048]{1,0:T(8,128)(2,1)}, bf16[2048,1152]{1,0:T(8,128)(2,1)}) custom-call(s32[1]{0:T(128)S(6)} %copy.48.lead, f32[2048,384]{1,0:T(8,128)} %x.13, f32[40,384]{1,0:T(8,128)} %embed.7, f32[384]{0:T(512)} %gain.7, f32[384]{0:T(512)} %shift.2, bf16[384,1152]{1,0:T(8,128)(2,1)} %wide.3, f32[384]{0:T(512)} %query_b.1, f32[384]{0:T(512)} %value_b.1), custom_call_target="tpu_custom_call" | custom-call | tf_op jit(solution)/shard_map/project/pallas_call | solution.py:84
  16.0 30.0 %attend.1 = (bf16[3,2,2048,2048]{3,2,1,0:T(8,128)(2,1)}, bf16[384,2048]{1,0:T(8,128)(2,1)}, f32[3,8,2048]{2,1,0:T(8,128)}) custom-call(bf16[2048,1152]{1,0:T(8,128)(2,1)} %get-tuple-element.77.q.k.v.refs_0_, bf16[2048,1152]{1,0:T(8,128)(2,1)} %get-tuple-element.77.q.k.v.refs_0_, bf16[2048,1152]{1,0:T(8,128)(2,1)} %get-tuple-element.77.q.k.v.refs_0_), custom_call_target="tpu_custom_call" | custom-call | tf_op jit(solution)/shard_map/attend/pallas_call | solution.py:163
  46.3 0.8 copy.46.columns
  47.1 0.7 pad.12
  48.3 37.2 %middle.1 = (f32[69,2048]{1,0:T(8,128)}, f32[2048,384]{1,0:T(8,128)}, bf16[6,128,2048]{2,1,0:T(8,128)(2,1)}, bf16[2048,384]{1,0:T(8,128)(2,1)}, f32[5760,128]{1,0:T(8,128)}, /*index=5*/f32[5760,128]{1,0:T(8,128)}) custom-call(s32[5]{0:T(128)} %compare_select_fusion.side.token.sides, s32[1]{0:T(128)S(6)} %copy.48.lead, f32[2048,384]{1,0:T(8,128)} %x.13, ...), custom_call_target="tpu_custom_call" | custom-call | tf_op jit(solution)/shard_map/middle/pallas_call | solution.py:368
  86.1 1.2 copy-done.16
  87.3 1.9 weights.1
  89.2 2.3 copy-done
  91.6 1.9 copy-done.2
  93.5 1.4 copy-done.7
  94.9 7.2 %attend_back.6 = (f32[128,2048]{1,0:T(8,128)S(1)}, bf16[2,2048,128]{2,1,0:T(8,128)(2,1)S(1)}) custom-call(s32[5]{0:T(128)S(1)} %copy-done.17, bf16[2048,1152]{1,0:T(8,128)(2,1)S(1)} %copy-done, bf16[6,128,2048]{2,1,0:T(8,128)(2,1)S(1)} %copy-done.2, bf16[2048,384]{1,0:T(8,128)(2,1)S(1)} %copy-done.7, bf16[3,2,2048,2048]{3,2,1,0:T(8,128)(2,1)} %get-tuple-element.88.refs_3_), custom_call_target="tpu_custom_call" | custom-call | flops 2684354560 | bytes 4194304 | tf_op jit(solution)/shard_map/attend_back/pallas_call | solution.py:478
  102.1 0.9 fold.10
  103.0 2.6 collective-permute-start.1
  105.5 15.7 %attend_back.7 = (bf16[2048,128]{1,0:T(8,128)(2,1)S(1)}, bf16[2,2048,128]{2,1,0:T(8,128)(2,1)S(1)}) custom-call(s32[5]{0:T(128)S(1)} %copy-done.17, bf16[2048,1152]{1,0:T(8,128)(2,1)S(1)} %copy-done, bf16[6,128,2048]{2,1,0:T(8,128)(2,1)S(1)} %copy-done.2, bf16[2048,384]{1,0:T(8,128)(2,1)S(1)} %copy-done.7, ...), custom_call_target="tpu_custom_call" | custom-call | flops 8053063680 | bytes 12582912 | tf_op jit(solution)/shard_map/attend_back/pallas_call | solution.py:478
  121.2 1.6 collective-permute-done.1.refs_2_
  122.9 0.8 fold.11
  123.7 2.1 collective-permute-start.2
  125.8 11.2 %attend_back.8 = (f32[128,2048]{1,0:T(8,128)S(1)}, bf16[2,2048,128]{2,1,0:T(8,128)(2,1)S(1)}) custom-call(s32[5]{0:T(128)S(1)} %copy-done.17, bf16[2048,1152]{1,0:T(8,128)(2,1)S(1)} %copy-done, bf16[6,128,2048]{2,1,0:T(8,128)(2,1)S(1)} %copy-done.2, bf16[2048,384]{1,0:T(8,128)(2,1)S(1)} %copy-done.7, bf16[3,2,2048,2048]{3,2,1,0:T(8,128)(2,1)} %get-tuple-element.88.refs_3_), custom_call_target="tpu_custom_call" | custom-call | flops 5368709120 | bytes 8388608 | tf_op jit(solution)/shard_map/attend_back/pallas_call | solution.py:478
  137.0 0.9 fold.12
  137.9 1.7 collective-permute-start.3
  139.6 7.0 %attend_back.9 = (f32[128,2048]{1,0:T(8,128)S(1)}, bf16[2,2048,128]{2,1,0:T(8,128)(2,1)S(1)}) custom-call(s32[5]{0:T(128)S(1)} %copy-done.17, bf16[2048,1152]{1,0:T(8,128)(2,1)S(1)} %copy-done, bf16[6,128,2048]{2,1,0:T(8,128)(2,1)S(1)} %copy-done.2, bf16[2048,384]{1,0:T(8,128)(2,1)S(1)} %copy-done.7, bf16[3,2,2048,2048]{3,2,1,0:T(8,128)(2,1)} %get-tuple-element.88.refs_3_, ...), custom_call_target="tpu_custom_call" | custom-call | flops 2684354560 | bytes 4194304 | tf_op jit(solution)/shard_map/attend_back/pallas_call | solution.py:478
  146.6 0.6 fold.13
  147.2 2.6 collective-permute-start.4
  149.8 7.3 %attend_back.10 = (bf16[2048,128]{1,0:T(8,128)(2,1)S(1)}, bf16[2,2048,128]{2,1,0:T(8,128)(2,1)S(1)}) custom-call(s32[5]{0:T(128)S(1)} %copy-done.17, bf16[2048,1152]{1,0:T(8,128)(2,1)S(1)} %copy-done, bf16[6,128,2048]{2,1,0:T(8,128)(2,1)S(1)} %copy-done.2, bf16[2048,384]{1,0:T(8,128)(2,1)S(1)} %copy-done.7, ...), custom_call_target="tpu_custom_call" | custom-call | flops 2684354560 | bytes 4194304 | tf_op jit(solution)/shard_map/attend_back/pallas_call | solution.py:478
  157.1 1.0 copy-done.11
  158.1 0.8 copy-done.14
  159.0 1.3 fold.14
  160.3 0.6 copy-done.3
  160.9 2.3 copy-done.1
  163.3 1.4 copy-done.8
  164.7 20.1 %attend_back.11 = (bf16[2048,128]{1,0:T(8,128)(2,1)S(1)}, bf16[2,2048,128]{2,1,0:T(8,128)(2,1)S(1)}) custom-call(s32[5]{0:T(128)S(1)} %copy-done.17, bf16[2048,1152]{1,0:T(8,128)(2,1)S(1)} %copy-done.1, bf16[6,128,2048]{2,1,0:T(8,128)(2,1)S(1)} %copy-done.3, bf16[2048,384]{1,0:T(8,128)(2,1)S(1)} %copy-done.8, ...), custom_call_target="tpu_custom_call" | custom-call | flops 10737418240 | bytes 16777216 | tf_op jit(solution)/shard_map/attend_back/pallas_call | solution.py:478
  184.8 1.0 copy-done.12
  185.7 0.8 copy-done.15
  186.5 7.0 %weigh.1 = (f32[1920,128]{1,0:T(8,128)}, f32[1920,128]{1,0:T(8,128)}, f32[8,384]{1,0:T(8,128)}) custom-call(s32[5]{0:T(128)} %compare_select_fusion.side.token.sides, f32[3]{0:T(128)} %copy-done.19, bf16[384,2048]{1,0:T(8,128)(2,1)} %get-tuple-element.107.first, bf16[2048,128]{1,0:T(8,128)(2,1)} %copy-done.13, bf16[2048,128]{1,0:T(8,128)(2,1)} %copy-done.14, ...), custom_call_target="tpu_custom_call" | custom-call | flops 5435817984 | bytes 6291456 | tf_op jit(solution)/shard_map/weigh/pallas_call | solution.py:540
  193.6 5.4 %finish.2 = (f32[2048,384]{1,0:T(8,128)}, f32[8,384]{1,0:T(8,128)}) custom-call(s32[1]{0:T(128)S(6)} %copy.48.lead, f32[3]{0:T(128)} %copy-done.19, f32[2048,384]{1,0:T(8,128)} %x.13, f32[40,384]{1,0:T(8,128)} %embed.7, f32[384]{0:T(512)} %gain.7, bf16[384,1152]{1,0:T(8,128)(2,1)} %wide.3, f32[2048,384]{1,0:T(8,128)} %get-tuple-element.115.d_mid, ...), custom_call_target="tpu_custom_call" | custom-call | flops 905969664 | bytes 7077888 | tf_op jit(solution)/shard_map/finish/pallas_call | solution.py:613
  199.1 0.8 fold.15
  199.8 1.6 collective-permute-start.6
  201.4 5.7 %finish.3 = (f32[2048,384]{1,0:T(8,128)}, f32[16,128]{1,0:T(8,128)}) custom-call(s32[1]{0:T(128)S(6)} %copy.48.lead, f32[3]{0:T(128)} %copy-done.19, f32[2048,384]{1,0:T(8,128)} %x.13, f32[40,384]{1,0:T(8,128)} %embed.7, f32[384]{0:T(512)} %gain.7, bf16[384,1152]{1,0:T(8,128)(2,1)} %wide.3, ...), custom_call_target="tpu_custom_call", output_to_operand_aliasing={{0}: (15, {})} | custom-call | flops 905969664 | bytes 7077888 | tf_op jit(solution)/shard_map/finish/pallas_call | solution.py:613
  207.1 9.6 %collective-permute-done.6.refs_2_ = f32[960,128]{1,0:T(8,128)S(1)} collective-permute-done((f32[960,128]{1,0:T(8,128)S(1)}, f32[960,128]{1,0:T(8,128)S(1)}, u32[]{:S(2)}, u32[]{:S(2)}) %collective-permute-start.6) | collective-permute-done | bytes 491552 | tf_op jit(solution)/shard_map/ppermute | solution.py:953
  216.8 0.7 fold.16
  217.5 6.2 %collective-permute-done.7.refs_3_ = f32[480,128]{1,0:T(8,128)S(1)} collective-permute-done((f32[480,128]{1,0:T(8,128)S(1)}, f32[480,128]{1,0:T(8,128)S(1)}, u32[]{:S(2)}, u32[]{:S(2)}) %collective-permute-start.7) | collective-permute-done | bytes 245792 | tf_op jit(solution)/shard_map/ppermute | solution.py:953
  223.7 0.6 fold.17
  224.4 4.9 %collective-permute-done.8.refs_4_ = f32[240,128]{1,0:T(8,128)S(1)} collective-permute-done((f32[240,128]{1,0:T(8,128)S(1)}, f32[240,128]{1,0:T(8,128)S(1)}, u32[]{:S(2)}, u32[]{:S(2)}) %collective-permute-start.8) | collective-permute-done | bytes 122912 | tf_op jit(solution)/shard_map/ppermute | solution.py:953
  229.3 0.6 fold.18
  229.9 0.6 collective-permute-start.9
  230.5 4.7 %collective-permute-done.9.refs_5_ = f32[120,128]{1,0:T(8,128)S(1)} collective-permute-done((f32[120,128]{1,0:T(8,128)S(1)}, f32[120,128]{1,0:T(8,128)S(1)}, u32[]{:S(2)}, u32[]{:S(2)}) %collective-permute-start.9) | collective-permute-done | bytes 61472 | tf_op jit(solution)/shard_map/ppermute | solution.py:953
  235.2 0.6 fold.19
  236.3 4.9 %collective-permute-done.10.got = f32[136,128]{1,0:T(8,128)S(1)} collective-permute-done((f32[136,128]{1,0:T(8,128)S(1)}, f32[136,128]{1,0:T(8,128)S(1)}, u32[]{:S(2)}, u32[]{:S(2)}) %collective-permute-start.10) | collective-permute-done | bytes 69664 | tf_op jit(solution)/shard_map/ppermute | solution.py:953
  241.2 0.7 join.4.mine
  242.0 6.5 %collective-permute-done.11.got = f32[272,128]{1,0:T(8,128)S(1)} collective-permute-done((f32[272,128]{1,0:T(8,128)S(1)}, f32[272,128]{1,0:T(8,128)S(1)}, u32[]{:S(2)}, u32[]{:S(2)}) %collective-permute-start.11) | collective-permute-done | bytes 139296 | tf_op jit(solution)/shard_map/ppermute | solution.py:953
  248.5 0.9 join.5.mine
  250.0 9.0 %collective-permute-done.12.got = f32[544,128]{1,0:T(8,128)S(1)} collective-permute-done((f32[544,128]{1,0:T(8,128)S(1)}, f32[544,128]{1,0:T(8,128)S(1)}, u32[]{:S(2)}, u32[]{:S(2)}) %collective-permute-start.12) | collective-permute-done | bytes 278560 | tf_op jit(solution)/shard_map/ppermute | solution.py:953
  259.0 0.6 join.6.mine
  259.7 3.0 %collective-permute-start.13 = (f32[1088,128]{1,0:T(8,128)S(1)}, f32[1088,128]{1,0:T(8,128)S(1)}, u32[]{:S(2)}, u32[]{:S(2)}) collective-permute-start(f32[1088,128]{1,0:T(8,128)S(1)} %join.6.mine), channel_id=1, source_target_pairs={{0,4},{1,5},{2,3},{3,2},{4,0},{5,1},{6,7},{7,6},{8,12},{9,13},{10,... | collective-permute-start | bytes 1671176 | tf_op jit(solution)/shard_map/ppermute | solution.py:953
  262.6 7.5 %collective-permute-done.13.got = f32[1088,128]{1,0:T(8,128)S(1)} collective-permute-done((f32[1088,128]{1,0:T(8,128)S(1)}, f32[1088,128]{1,0:T(8,128)S(1)}, u32[]{:S(2)}, u32[]{:S(2)}) %collective-permute-start.13) | collective-permute-done | bytes 557088 | tf_op jit(solution)/shard_map/ppermute | solution.py:953
  270.1 0.7 join.7.mine
  271.0 6.3 %unpack.1 = (f32[384,1536]{1,0:T(8,128)}, f32[1536,384]{1,0:T(8,128)}, f32[384,384]{1,0:T(8,128)}, f32[207,384]{1,0:T(8,128)}, f32[32,128]{1,0:T(8,128)}) custom-call(f32[32,360,128]{2,1,0:T(8,128)} %bitcast.40), custom_call_target="tpu_custom_call" | custom-call | flops 8000000000 | bytes 11796480 | tf_op jit(solution)/shard_map/unpack/pallas_call | solution.py:698
  277.2 1.4 slice_bitcast_fusion.1
  278.7 0.6 slice.60
  279.2 1.3 slice_bitcast_fusion
  280.5 3.0 %settle.1 = (f32[384,1152]{1,0:T(8,128)}, f32[40,384]{1,0:T(8,128)}, f32[16,128]{1,0:T(8,128)S(1)}) custom-call(s32[5]{0:T(128)S(1)} %copy-done.18, f32[32,128]{1,0:T(8,128)S(1)} %get-tuple-element.122.leads, f32[2176,128]{1,0:T(8,128)S(1)} %join.7.mine, f32[2176,128]{1,0:T(8,128)S(1)} %collective-permute-done.14.got), custom_call_target="tpu_custom_call" | custom-call | tf_op jit(solution)/shard_map/settle/pallas_call | solution.py:820
  283.5 0.6 slice_bitcast_fusion.6
  284.2 0.6 reshape.91
  (75 shorter events, 3.1 us)
Async XLA Ops:
  7.2 78.3 %all-gather.5.cloned.1.call-start = ((), (), s32[]{:S(2)}) async-start(), calls=%async_computation | async-start | bytes 1081344 | tf_op jit(solution)/shard_map/all_gather | solution.py:1046
  8.5 262.4 %all-gather.7.cloned.1.call-start = ((), (), s32[]{:S(2)}) async-start(), calls=%async_computation.1 | async-start | bytes 6082560 | tf_op jit(solution)/shard_map/all_gather | solution.py:1180
  16.0 30.1 %copy-start.21 = (bf16[384,207]{0,1:T(8,128)(2,1)S(1)}, bf16[384,207]{0,1:T(8,128)(2,1)}, u32[]{:S(2)}) copy-start(bf16[384,207]{0,1:T(8,128)(2,1)} %param.43) | copy-start | bytes 476932
  16.0 30.1 %copy-start.23 = (f32[207]{0:T(256)S(1)}, f32[207]{0:T(256)}, u32[]{:S(2)}) copy-start(f32[207]{0:T(256)} %param.44) | copy-start | bytes 2488
  16.0 30.3 %copy-start.26 = (f32[69]{0:T(128)S(1)}, f32[69]{0:T(128)}, u32[]{:S(2)}) copy-start(f32[69]{0:T(128)} %param.45) | copy-start | bytes 832
  16.0 31.8 %copy-start.24 = (s32[5]{0:T(128)S(1)}, s32[5]{0:T(128)}, u32[]{:S(2)}) copy-start(s32[5]{0:T(128)} %constant.25.clone) | copy-start | bytes 64
  16.0 31.8 %copy-start.25 = (s32[5]{0:T(128)S(1)}, s32[5]{0:T(128)}, u32[]{:S(2)}) copy-start(s32[5]{0:T(128)} %constant.26.clone) | copy-start | bytes 64
  48.3 37.8 %copy-start.20 = (s32[40]{0:T(128)S(1)}, s32[40]{0:T(128)}, u32[]{:S(2)}) copy-start(s32[40]{0:T(128)} %frames.1) | copy-start | bytes 484
  48.3 40.9 %copy-start.17 = (s32[5]{0:T(128)S(1)}, s32[5]{0:T(128)}, u32[]{:S(2)}) copy-start(s32[5]{0:T(128)} %compare_select_fusion.side.token.sides) | copy-start | bytes 64
  85.5 16.5 %collective-permute-start = (f32[5760,128]{1,0:T(8,128)}, f32[5760,128]{1,0:T(8,128)S(1)}, u32[]{:S(2)}, u32[]{:S(2)}) collective-permute-start(f32[5760,128]{1,0:T(8,128)} %get-tuple-element.84), channel_id=1, source_target_pairs={{0,2},{1,3},{2,0},{3,1},{4,6},{5,7},{6,4},{7,5},{8,10},{9,11},{10,... | collective-permute-start | bytes 8847368 | tf_op jit(solution)/shard_map/ppermute | solution.py:953
  86.1 1.2 copy-start.16
  89.2 69.8 %copy-start.19 = (f32[3]{0:T(128)}, f32[3]{0:T(128)S(1)}, u32[]{:S(2)}) copy-start(f32[3]{0:T(128)S(1)} %get-tuple-element.118.factors.weight) | copy-start | bytes 40
  89.2 2.3 copy-start
  91.6 1.9 copy-start.2
  93.5 1.4 copy-start.7
  94.9 7.2 %copy-start.4 = (f32[5760,128]{1,0:T(8,128)S(1)}, f32[5760,128]{1,0:T(8,128)}, u32[]{:S(2)}) copy-start(f32[5760,128]{1,0:T(8,128)} %get-tuple-element.82.refs_0_) | copy-start | bytes 8847364
  102.1 44.5 %copy-start.5 = (f32[5760,128]{1,0:T(8,128)}, f32[5760,128]{1,0:T(8,128)S(1)}, u32[]{:S(2)}) copy-start(f32[5760,128]{1,0:T(8,128)S(1)} %collective-permute-done.refs_1_) | copy-start | bytes 8847364
  103.0 19.9 %collective-permute-start.1 = (f32[2880,128]{1,0:T(8,128)S(1)}, f32[2880,128]{1,0:T(8,128)S(1)}, u32[]{:S(2)}, u32[]{:S(2)}) collective-permute-start(f32[2880,128]{1,0:T(8,128)S(1)} %fold.10), channel_id=1, source_target_pairs={{0,4},{1,5},{2,3},{3,2},{4,0},{5,1},{6,7},{7,6},{8,12},{9,13},{10,... | collective-permute-start | bytes 4423688 | tf_op jit(solution)/shard_map/ppermute | solution.py:953
  121.2 2.4 copy-start.10
  121.2 2.4 copy-start.13
  123.7 13.3 %collective-permute-start.2 = (f32[1440,128]{1,0:T(8,128)S(1)}, f32[1440,128]{1,0:T(8,128)S(1)}, u32[]{:S(2)}, u32[]{:S(2)}) collective-permute-start(f32[1440,128]{1,0:T(8,128)S(1)} %fold.11), channel_id=1, source_target_pairs={{0,1},{1,0},{2,10},{3,11},{4,5},{5,4},{6,14},{7,15},{8,9},{9,8},{1... | collective-permute-start | bytes 2211848 | tf_op jit(solution)/shard_map/ppermute | solution.py:953
  137.9 8.6 %collective-permute-start.3 = (f32[720,128]{1,0:T(8,128)S(1)}, f32[720,128]{1,0:T(8,128)S(1)}, u32[]{:S(2)}, u32[]{:S(2)}) collective-permute-start(f32[720,128]{1,0:T(8,128)S(1)} %fold.12), channel_id=1, source_target_pairs={{0,8},{1,9},{2,6},{3,7},{4,12},{5,13},{6,2},{7,3},{8,0},{9,1},{10,... | collective-permute-start | bytes 1105928 | tf_op jit(solution)/shard_map/ppermute | solution.py:953
  147.2 11.8 %collective-permute-start.4 = (f32[360,128]{1,0:T(8,128)S(1)}, f32[360,128]{1,0:T(8,128)S(1)}, u32[]{:S(2)}, u32[]{:S(2)}) collective-permute-start(f32[360,128]{1,0:T(8,128)S(1)} %fold.13), channel_id=1, source_target_pairs={{0,16},{1,17},{2,18},{3,19},{4,20},{5,21},{6,22},{7,23},{8,24},{9,... | collective-permute-start | bytes 552968 | tf_op jit(solution)/shard_map/ppermute | solution.py:953
  149.8 9.1 %copy-start.6 = (f32[5760,128]{1,0:T(8,128)S(1)}, f32[5760,128]{1,0:T(8,128)}, u32[]{:S(2)}) copy-start(f32[5760,128]{1,0:T(8,128)} %copy-done.5) | copy-start | bytes 8847364
  157.1 1.0 copy-start.11
  158.1 0.8 copy-start.14
  159.0 2.0 copy-start.3
  160.9 2.3 copy-start.1
  163.3 1.4 copy-start.8
  184.8 1.0 copy-start.12
  185.7 0.8 copy-start.15
  193.5 5.5 %collective-permute-start.5 = (f32[1920,128]{1,0:T(8,128)}, f32[1920,128]{1,0:T(8,128)S(1)}, u32[]{:S(2)}, u32[]{:S(2)}) collective-permute-start(f32[1920,128]{1,0:T(8,128)} %get-tuple-element.113), channel_id=1, source_target_pairs={{0,2},{1,3},{2,0},{3,1},{4,6},{5,7},{6,4},{7,5},{8,10},{9,11},{10,... | collective-permute-start | bytes 2949128 | tf_op jit(solution)/shard_map/ppermute | solution.py:953
  193.6 5.4 %copy-start.9 = (f32[1920,128]{1,0:T(8,128)S(1)}, f32[1920,128]{1,0:T(8,128)}, u32[]{:S(2)}) copy-start(f32[1920,128]{1,0:T(8,128)} %get-tuple-element.112.refs_0_) | copy-start | bytes 2949124
  193.6 5.4 %copy-start.18 = (s32[5]{0:T(128)S(1)}, s32[5]{0:T(128)}, u32[]{:S(2)}) copy-start(s32[5]{0:T(128)} %compare_select_fusion.side.token.sides) | copy-start | bytes 64
  199.8 16.9 %collective-permute-start.6 = (f32[960,128]{1,0:T(8,128)S(1)}, f32[960,128]{1,0:T(8,128)S(1)}, u32[]{:S(2)}, u32[]{:S(2)}) collective-permute-start(f32[960,128]{1,0:T(8,128)S(1)} %fold.15), channel_id=1, source_target_pairs={{0,4},{1,5},{2,3},{3,2},{4,0},{5,1},{6,7},{7,6},{8,12},{9,13},{10,... | collective-permute-start | bytes 1474568 | tf_op jit(solution)/shard_map/ppermute | solution.py:953
  217.4 6.3 %collective-permute-start.7 = (f32[480,128]{1,0:T(8,128)S(1)}, f32[480,128]{1,0:T(8,128)S(1)}, u32[]{:S(2)}, u32[]{:S(2)}) collective-permute-start(f32[480,128]{1,0:T(8,128)S(1)} %fold.16), channel_id=1, source_target_pairs={{0,1},{1,0},{2,10},{3,11},{4,5},{5,4},{6,14},{7,15},{8,9},{9,8},{1... | collective-permute-start | bytes 737288 | tf_op jit(solution)/shard_map/ppermute | solution.py:953
  224.3 11.4 %copy-start.22 = (f32[16,128]{1,0:T(8,128)S(1)}, f32[16,128]{1,0:T(8,128)}, u32[]{:S(2)}) copy-start(f32[16,128]{1,0:T(8,128)} %get-tuple-element.123) | copy-start | bytes 24580
  224.4 4.9 %collective-permute-start.8 = (f32[240,128]{1,0:T(8,128)S(1)}, f32[240,128]{1,0:T(8,128)S(1)}, u32[]{:S(2)}, u32[]{:S(2)}) collective-permute-start(f32[240,128]{1,0:T(8,128)S(1)} %fold.17), channel_id=1, source_target_pairs={{0,8},{1,9},{2,6},{3,7},{4,12},{5,13},{6,2},{7,3},{8,0},{9,1},{10,... | collective-permute-start | bytes 368648 | tf_op jit(solution)/shard_map/ppermute | solution.py:953
  229.9 5.3 %collective-permute-start.9 = (f32[120,128]{1,0:T(8,128)S(1)}, f32[120,128]{1,0:T(8,128)S(1)}, u32[]{:S(2)}, u32[]{:S(2)}) collective-permute-start(f32[120,128]{1,0:T(8,128)S(1)} %fold.18), channel_id=1, source_target_pairs={{0,16},{1,17},{2,18},{3,19},{4,20},{5,21},{6,22},{7,23},{8,24},{9,... | collective-permute-start | bytes 184328 | tf_op jit(solution)/shard_map/ppermute | solution.py:953
  235.8 5.4 %collective-permute-start.10 = (f32[136,128]{1,0:T(8,128)S(1)}, f32[136,128]{1,0:T(8,128)S(1)}, u32[]{:S(2)}, u32[]{:S(2)}) collective-permute-start(f32[136,128]{1,0:T(8,128)S(1)} %pad_maximum_fusion.mine), channel_id=1, source_target_pairs={{0,16},{1,17},{2,18},{3,19},{4,20},{5,21},{6,22},{7,23},{8,24},{9,... | collective-permute-start | bytes 208904 | tf_op jit(solution)/shard_map/ppermute | solution.py:953
  241.9 6.5 %collective-permute-start.11 = (f32[272,128]{1,0:T(8,128)S(1)}, f32[272,128]{1,0:T(8,128)S(1)}, u32[]{:S(2)}, u32[]{:S(2)}) collective-permute-start(f32[272,128]{1,0:T(8,128)S(1)} %join.4.mine), channel_id=1, source_target_pairs={{0,8},{1,9},{2,6},{3,7},{4,12},{5,13},{6,2},{7,3},{8,0},{9,1},{10,... | collective-permute-start | bytes 417800 | tf_op jit(solution)/shard_map/ppermute | solution.py:953
  249.4 9.6 %collective-permute-start.12 = (f32[544,128]{1,0:T(8,128)S(1)}, f32[544,128]{1,0:T(8,128)S(1)}, u32[]{:S(2)}, u32[]{:S(2)}) collective-permute-start(f32[544,128]{1,0:T(8,128)S(1)} %join.5.mine), channel_id=1, source_target_pairs={{0,1},{1,0},{2,10},{3,11},{4,5},{5,4},{6,14},{7,15},{8,9},{9,8},{1... | collective-permute-start | bytes 835592 | tf_op jit(solution)/shard_map/ppermute | solution.py:953
  259.7 10.5 %collective-permute-start.13 = (f32[1088,128]{1,0:T(8,128)S(1)}, f32[1088,128]{1,0:T(8,128)S(1)}, u32[]{:S(2)}, u32[]{:S(2)}) collective-permute-start(f32[1088,128]{1,0:T(8,128)S(1)} %join.6.mine), channel_id=1, source_target_pairs={{0,4},{1,5},{2,3},{3,2},{4,0},{5,1},{6,7},{7,6},{8,12},{9,13},{10,... | collective-permute-start | bytes 1671176 | tf_op jit(solution)/shard_map/ppermute | solution.py:953
  270.9 9.7 %collective-permute-start.14 = (f32[2176,128]{1,0:T(8,128)S(1)}, f32[2176,128]{1,0:T(8,128)S(1)}, u32[]{:S(2)}, u32[]{:S(2)}) collective-permute-start(f32[2176,128]{1,0:T(8,128)S(1)} %join.7.mine), channel_id=1, source_target_pairs={{0,2},{1,3},{2,0},{3,1},{4,6},{5,7},{6,4},{7,5},{8,10},{9,11},{10,... | collective-permute-start | bytes 3342344 | tf_op jit(solution)/shard_map/ppermute | solution.py:953
Sparse Core Ops, SparseCore 0:
  11.5 56.6 all-gather.4
  160.4 67.9 all-gather.6
